TPU v7x, 32 devices: a whole 2x2x4 slice. The times are simulated.
32 devices in a mesh: dp: 4 (over y, core), head: 2 (over x), blk: 4 (over z).
Axes of the slice: x: 2, y: 2, z: 4, core: 2. Of those that a mesh axis runs over, the one named last changes fastest.
Arguments:
- block_input: bfloat16 [2, 4, 1024, 2048], P(None, 'dp', ('head', 'blk')), may hold values from -6 to 6
- attention_gain: bfloat16 [2048], P(('dp', 'blk')), may hold values from 0.099609375 to 1.8984375
- query_weight: bfloat16 [2048, 2048], P(('dp', 'blk'), 'head'), may hold values from -0.125 to 0.125
- key_weight: bfloat16 [2048, 2048], P(('dp', 'blk'), 'head'), may hold values from -0.125 to 0.125
- value_weight: bfloat16 [2048, 2048], P(('dp', 'blk'), 'head'), may hold values from -0.125 to 0.125
- output_weight: bfloat16 [2048, 2048], P('head', ('dp', 'blk')), may hold values from -0.5 to 0.5
- mlp_gain: bfloat16 [2048], P(('dp', 'blk')), may hold values from 0.099609375 to 1.8984375
- gate_weight: bfloat16 [2048, 8192], P(('dp', 'blk'), 'head'), may hold values from -0.125 to 0.125
- up_weight: bfloat16 [2048, 8192], P(('dp', 'blk'), 'head'), may hold values from -0.125 to 0.125
- down_weight: bfloat16 [8192, 2048], P('head', ('dp', 'blk')), may hold values from -0.09375 to 0.09375
- grad_output: bfloat16 [2, 4, 1024, 2048], P(None, 'dp', ('head', 'blk')), may hold values from -6 to 6
Outputs:
- block_output: bfloat16 [2, 4, 1024, 2048], P(None, 'dp', ('head', 'blk'))
- input_grad: bfloat16 [2, 4, 1024, 2048], P(None, 'dp', ('head', 'blk'))
- attention_gain_grad: float32 [2048], P(('dp', 'blk'))
- query_weight_grad: float32 [2048, 2048], P(('dp', 'blk'), 'head')
- key_weight_grad: float32 [2048, 2048], P(('dp', 'blk'), 'head')
- value_weight_grad: float32 [2048, 2048], P(('dp', 'blk'), 'head')
- output_weight_grad: float32 [2048, 2048], P('head', ('dp', 'blk'))
- mlp_gain_grad: float32 [2048], P(('dp', 'blk'))
- gate_weight_grad: float32 [2048, 8192], P(('dp', 'blk'), 'head')
- up_weight_grad: float32 [2048, 8192], P(('dp', 'blk'), 'head')
- down_weight_grad: float32 [8192, 2048], P('head', ('dp', 'blk'))
All inputs are finite; a program needn't handle non-finite values.
Results may differ from a plain program's by a relative error of at most 0.023.
Values may be sent and summed in bfloat16 or wider, within the bound.
A program may use at most 384 MiB of HBM per device.

v0:
```python
import jax
import jax.numpy as jnp
from jax import lax
from jax.sharding import PartitionSpec as P

HD = 64


EPSILON = 1e-05
ROPE_BASE = 130000.0
MASKED_SCORE = -1e30


def passed_along(value, axis, steps):
    count = lax.axis_size(axis)
    pairs = [(source, (source + steps) % count) for source in range(count)]
    return lax.ppermute(value, axis, pairs)


def for_sending(array):

    def short(part):
        return part.astype(jnp.bfloat16) if part.dtype == jnp.float32 else part

    return jax.tree.map(short, array)


def share_rows(local_rows):
    return lax.all_gather(local_rows, "head", axis=0, tiled=True)


def head_split(partial_total):
    return lax.psum_scatter(
        partial_total.astype(jnp.bfloat16), "head", scatter_dimension=0, tiled=True
    ).astype(jnp.float32)


def to_heads(stacked):
    return lax.all_to_all(stacked, "head", split_axis=3, concat_axis=1, tiled=True)


def from_heads(stacked):
    return lax.all_to_all(stacked, "head", split_axis=1, concat_axis=3, tiled=True)


def pass_keys(key_value):
    return passed_along(key_value, "blk", 1)


def pass_grads(key_grads):
    return passed_along(key_grads.astype(jnp.bfloat16), "blk", 1).astype(key_grads.dtype)


def fetch_weights(row_shards, column_shards):
    gathered_rows = jax.tree.map(
        lambda part, own: part.astype(own.dtype),
        lax.all_gather(for_sending(row_shards), ("dp", "blk"), axis=0, tiled=True),
        row_shards,
    )
    gathered_columns = jax.tree.map(
        lambda part, own: part.astype(own.dtype),
        lax.all_gather(for_sending(column_shards), ("dp", "blk"), axis=1, tiled=True),
        column_shards,
    )
    widened = (
        lax.all_gather(gathered_rows[0], "head", axis=1, tiled=True),
        lax.all_gather(gathered_rows[1], "head", axis=1, tiled=True),
        lax.all_gather(gathered_rows[2], "head", axis=1, tiled=True),
        lax.all_gather(gathered_columns[0], "head", axis=0, tiled=True),
    )
    gathered_rows = (widened[0], widened[1], widened[2]) + tuple(gathered_rows[3:])
    gathered_columns = (widened[3], gathered_columns[1])
    return (gathered_rows, gathered_columns)


def settle_grads(row_grads, column_grads):
    row_part = lax.psum_scatter(row_grads, ("dp", "blk"), scatter_dimension=0, tiled=True)
    column_part = lax.psum_scatter(column_grads, ("dp", "blk"), scatter_dimension=1, tiled=True)
    gain_pair = jnp.stack([row_part[5], row_part[6]])
    repeated = jnp.broadcast_to(gain_pair[None], (lax.axis_size("head"),) + gain_pair.shape)
    narrowed = (
        lax.psum_scatter(
            row_part[0].astype(jnp.bfloat16), "head", scatter_dimension=1, tiled=True
        ).astype(jnp.float32),
        lax.psum_scatter(
            row_part[1].astype(jnp.bfloat16), "head", scatter_dimension=1, tiled=True
        ).astype(jnp.float32),
        lax.psum_scatter(
            row_part[2].astype(jnp.bfloat16), "head", scatter_dimension=1, tiled=True
        ).astype(jnp.float32),
        lax.psum_scatter(
            column_part[0].astype(jnp.bfloat16), "head", scatter_dimension=0, tiled=True
        ).astype(jnp.float32),
        lax.psum_scatter(
            repeated.astype(jnp.bfloat16), "head", scatter_dimension=0, tiled=True
        ).astype(jnp.float32),
    )
    gain_sums = narrowed[4][0]
    row_part = (
        narrowed[0],
        narrowed[1],
        narrowed[2],
        row_part[3],
        row_part[4],
        gain_sums[0],
        gain_sums[1],
    )
    column_part = (narrowed[3], column_part[1])
    return (row_part, column_part)


def zero_grads(weights_kept):
    return (
        tuple((jnp.zeros(member.shape, jnp.float32) for member in weights_kept[0])),
        tuple((jnp.zeros(member.shape, jnp.float32) for member in weights_kept[1])),
    )


def matmul(left_side, right_side):
    return jnp.dot(left_side, right_side, preferred_element_type=jnp.float32)


def matmul_nt(left_side, right_side):
    return lax.dot_general(
        left_side, right_side, (((1,), (1,)), ((), ())), preferred_element_type=jnp.float32
    )


def matmul_tn(left_side, right_side):
    return lax.dot_general(
        left_side, right_side, (((0,), (0,)), ((), ())), preferred_element_type=jnp.float32
    )


def rope_tables(positions):
    half_width = HD // 2
    frequency = ROPE_BASE ** (-jnp.arange(half_width, dtype=jnp.float32) * 2.0 / HD)
    angles = positions[:, None] * frequency[None, :]
    return (jnp.cos(angles)[:, None, :], jnp.sin(angles)[:, None, :])


def rotate(flat_rows, cosine_table, sine_table, direction):
    row_count = flat_rows.shape[0]
    half_width = HD // 2
    heads_view = flat_rows.reshape(row_count, -1, HD)
    first_half = heads_view[..., :half_width]
    second_half = heads_view[..., half_width:]
    turned = jnp.concatenate(
        [
            first_half * cosine_table - direction * second_half * sine_table,
            second_half * cosine_table + direction * first_half * sine_table,
        ],
        -1,
    )
    return turned.reshape(row_count, -1)


def rms_forward(values, gain_row):
    inverse_rms = lax.rsqrt(jnp.mean(values * values, -1, keepdims=True) + EPSILON)
    return (inverse_rms, (values * inverse_rms * gain_row).astype(jnp.bfloat16))


def rms_backward(grad_normed, values, inverse_rms, gain_row):
    weighted = grad_normed * gain_row
    cubed = inverse_rms * inverse_rms * inverse_rms
    grad_values = inverse_rms * weighted - values * cubed * jnp.mean(
        weighted * values, -1, keepdims=True
    )
    grad_gain = jnp.sum(grad_normed * values * inverse_rms, 0)
    return (grad_values, grad_gain)


def absorb(running, query_portion, key_portion, value_portion, mask_table):
    row_top, row_total, accumulated = running
    scores = jnp.einsum(
        "zwpi,zfpi->zpwf", query_portion, key_portion, preferred_element_type=jnp.float32
    ) * HD ** (-0.5)
    if mask_table is not None:
        scores = jnp.where(mask_table, scores, MASKED_SCORE)
    new_top = jnp.maximum(row_top, jnp.max(scores, -1))
    weights = jnp.exp(scores - new_top[..., None])
    factor = jnp.exp(row_top - new_top)
    row_total = row_total * factor + jnp.sum(weights, -1)
    accumulated = accumulated * jnp.swapaxes(factor, 1, 2)[..., None] + jnp.einsum(
        "iugr,iruf->iguf",
        weights.astype(jnp.bfloat16),
        value_portion,
        preferred_element_type=jnp.float32,
    )
    return (new_top, row_total, accumulated)


def half_update(running, queries, key_portion, value_portion):
    upper = tuple((member[1:] for member in running))
    upper = absorb(upper, queries[1:], key_portion[:1], value_portion[:1], None)
    return tuple((jnp.concatenate([member[:1], newer], 0) for member, newer in zip(running, upper)))


def cycle_forward(queries, key_value, causal):
    cycle_size = lax.axis_size("blk")
    cycle_place = lax.axis_index("blk")
    halves, tok_count, heads_here, width = queries.shape
    running = (
        jnp.full((halves, heads_here, tok_count), MASKED_SCORE, jnp.float32),
        jnp.zeros((halves, heads_here, tok_count), jnp.float32),
        jnp.zeros((halves, tok_count, heads_here, width), jnp.float32),
    )
    running = absorb(running, queries, key_value[0], key_value[1], causal)
    running = half_update(running, queries, key_value[0], key_value[1])

    def advance(cycle_carry, cycle_step):
        current_state, travelling = cycle_carry
        travelling = pass_keys(travelling)
        current_state = half_update(current_state, queries, travelling[0], travelling[1])
        current_state = lax.cond(
            cycle_step <= cycle_place,
            lambda current: absorb(current, queries, travelling[0], travelling[1], None),
            lambda current: current,
            current_state,
        )
        return ((current_state, travelling), None)

    (running, unused), trailing = lax.scan(advance, (running, key_value), jnp.arange(1, cycle_size))
    row_top, row_total, accumulated = running
    attended = accumulated / jnp.swapaxes(row_total, 1, 2)[..., None]
    return (attended, row_top + jnp.log(row_total))


def pair_grads(
    query_portion, key_portion, value_portion, output_gradient, logsum, row_delta, mask_table
):
    scores = jnp.einsum(
        "zwpi,zfpi->zpwf", query_portion, key_portion, preferred_element_type=jnp.float32
    ) * HD ** (-0.5)
    if mask_table is not None:
        scores = jnp.where(mask_table, scores, MASKED_SCORE)
    probabilities = jnp.exp(scores - logsum[..., None])
    grad_value = jnp.einsum(
        "cmou,comb->cumb",
        probabilities.astype(jnp.bfloat16),
        output_gradient,
        preferred_element_type=jnp.float32,
    )
    grad_prob = jnp.einsum(
        "zwpi,zfpi->zpwf", output_gradient, value_portion, preferred_element_type=jnp.float32
    )
    score_gradient = (probabilities * (grad_prob - row_delta[..., None]) * HD ** (-0.5)).astype(
        jnp.bfloat16
    )
    grad_query = jnp.einsum(
        "iugr,iruf->iguf", score_gradient, key_portion, preferred_element_type=jnp.float32
    )
    grad_key = jnp.einsum(
        "cmou,comb->cumb", score_gradient, query_portion, preferred_element_type=jnp.float32
    )
    return (grad_query, grad_key, grad_value)


def cycle_backward(queries, key_value, output_gradient, logsum, row_delta, causal):
    cycle_size = lax.axis_size("blk")
    cycle_place = lax.axis_index("blk")

    def cross_grads(grads_now, travelling):
        grad_query, key_grads = grads_now
        part_query, part_key, part_value = pair_grads(
            queries[1:],
            travelling[0][:1],
            travelling[1][:1],
            output_gradient[1:],
            logsum[1:],
            row_delta[1:],
            None,
        )
        grad_query = jnp.concatenate([grad_query[:1], grad_query[1:] + part_query], 0)
        padding = jnp.zeros_like(part_key)
        key_grads = key_grads + jnp.stack(
            [jnp.concatenate([part_key, padding], 0), jnp.concatenate([part_value, padding], 0)]
        )
        return (grad_query, key_grads)

    def same_grads(grads_now, travelling, mask_table):
        grad_query, key_grads = grads_now
        part_query, part_key, part_value = pair_grads(
            queries, travelling[0], travelling[1], output_gradient, logsum, row_delta, mask_table
        )
        return (grad_query + part_query, key_grads + jnp.stack([part_key, part_value]))

    grads_now = (jnp.zeros(queries.shape, jnp.float32), jnp.zeros(key_value.shape, jnp.float32))
    grads_now = same_grads(grads_now, key_value, causal)
    grads_now = cross_grads(grads_now, key_value)

    def advance(cycle_carry, cycle_step):
        current_grads, travelling = cycle_carry
        travelling = pass_keys(travelling)
        current_grads = (current_grads[0], pass_grads(current_grads[1]))
        current_grads = cross_grads(current_grads, travelling)
        current_grads = lax.cond(
            cycle_step <= cycle_place,
            lambda current: same_grads(current, travelling, None),
            lambda current: current,
            current_grads,
        )
        return ((current_grads, travelling), None)

    (grads_now, unused), trailing = lax.scan(
        advance, (grads_now, key_value), jnp.arange(1, cycle_size)
    )
    grad_query, key_grads = grads_now
    key_grads = pass_grads(key_grads)
    return (grad_query, key_grads[0], key_grads[1])


def group_tables(tok_count):
    cycle_size = lax.axis_size("blk")
    cycle_place = lax.axis_index("blk")
    half_index = jnp.arange(2, dtype=jnp.int32)
    positions = (
        (
            (half_index[:, None] * cycle_size + cycle_place) * tok_count
            + jnp.arange(tok_count, dtype=jnp.int32)[None, :]
        )
        .reshape(-1)
        .astype(jnp.float32)
    )
    return rope_tables(positions)


def one_micro_heads(local_input, local_grad, weights_kept):
    (query_full, key_full, value_full, gate_full, up_full, gain_attention, gain_mlp), (
        output_full,
        down_full,
    ) = weights_kept
    tok_count = local_input.shape[0]
    heads_here = query_full.shape[1] // HD // lax.axis_size("head")
    cycle_size = lax.axis_size("blk")
    cycle_place = lax.axis_index("blk")
    head_place = lax.axis_index("head")
    own_positions = (
        (head_place * cycle_size + cycle_place) * tok_count + jnp.arange(tok_count, dtype=jnp.int32)
    ).astype(jnp.float32)
    own_cosine, own_sine = rope_tables(own_positions)
    cosine_table, sine_table = group_tables(tok_count)
    causal = (jnp.arange(tok_count)[None, :] <= jnp.arange(tok_count)[:, None])[None, None]
    gain_one = gain_attention.astype(jnp.float32)
    gain_two = gain_mlp.astype(jnp.float32)
    inputs_own = local_input.astype(jnp.float32)
    scale_one, normed_one = rms_forward(inputs_own, gain_one)
    query_own = rotate(matmul(normed_one, query_full), own_cosine, own_sine, 1.0).astype(
        jnp.bfloat16
    )
    key_own = rotate(matmul(normed_one, key_full), own_cosine, own_sine, 1.0).astype(jnp.bfloat16)
    value_own = matmul(normed_one, value_full).astype(jnp.bfloat16)
    grouped = to_heads(jnp.stack([query_own, key_own, value_own])[:, None])
    grouped = grouped.reshape(3, 2, tok_count, heads_here, HD)
    queries = grouped[0]
    key_value = grouped[1:]
    attended_full, logsum = cycle_forward(queries, key_value, causal)
    attended_group = attended_full.reshape(1, 2, tok_count, -1).astype(jnp.bfloat16)
    attended_rows = from_heads(attended_group)[0, 0]
    mixed = inputs_own + matmul(attended_rows, output_full)
    scale_two, normed_two = rms_forward(mixed, gain_two)
    normed_all = share_rows(normed_two)
    gate_lin = matmul(normed_all, gate_full)
    up_lin = matmul(normed_all, up_full)
    sigmoid_gate = jax.nn.sigmoid(gate_lin)
    activated = gate_lin * sigmoid_gate
    hidden = (activated * up_lin).astype(jnp.bfloat16)
    output_rows = (mixed + head_split(matmul(hidden, down_full))).astype(jnp.bfloat16)
    grad_rows_all = share_rows(local_grad)
    grad_hidden = matmul_nt(grad_rows_all, down_full)
    grad_down = matmul_tn(hidden, grad_rows_all)
    grad_gate = (
        grad_hidden * up_lin * sigmoid_gate * (1.0 + gate_lin * (1.0 - sigmoid_gate))
    ).astype(jnp.bfloat16)
    grad_up = (grad_hidden * activated).astype(jnp.bfloat16)
    grad_gate_weight = matmul_tn(normed_all, grad_gate)
    grad_up_weight = matmul_tn(normed_all, grad_up)
    grad_normed_two = lax.psum_scatter(
        (matmul_nt(grad_gate, gate_full) + matmul_nt(grad_up, up_full)).astype(jnp.bfloat16),
        "head",
        scatter_dimension=0,
        tiled=True,
    ).astype(jnp.float32)
    grad_mixed_norm, grad_gain_two = rms_backward(grad_normed_two, mixed, scale_two, gain_two)
    grad_mixed = local_grad.astype(jnp.float32) + grad_mixed_norm
    grad_mixed_low = grad_mixed.astype(jnp.bfloat16)
    grad_output_weight = matmul_tn(attended_rows, grad_mixed_low)
    grad_attended = matmul_nt(grad_mixed_low, output_full).astype(jnp.bfloat16)
    grad_blocks = to_heads(grad_attended[None, None])[0].reshape(2, tok_count, heads_here, HD)
    row_delta = jnp.swapaxes(jnp.sum(grad_blocks.astype(jnp.float32) * attended_full, -1), 1, 2)
    grad_query, grad_key, grad_value = cycle_backward(
        queries, key_value, grad_blocks, logsum, row_delta, causal
    )
    grad_query_lin = rotate(
        grad_query.reshape(2 * tok_count, -1), cosine_table, sine_table, -1.0
    ).astype(jnp.bfloat16)
    grad_key_lin = rotate(
        grad_key.reshape(2 * tok_count, -1), cosine_table, sine_table, -1.0
    ).astype(jnp.bfloat16)
    grad_value_lin = grad_value.reshape(2 * tok_count, -1).astype(jnp.bfloat16)
    returned = from_heads(
        jnp.stack([grad_query_lin, grad_key_lin, grad_value_lin]).reshape(3, 2, tok_count, -1)
    )[:, 0]
    grad_query_weight = matmul_tn(normed_one, returned[0])
    grad_key_weight = matmul_tn(normed_one, returned[1])
    grad_value_weight = matmul_tn(normed_one, returned[2])
    grad_normed_one = (
        matmul_nt(returned[0], query_full)
        + matmul_nt(returned[1], key_full)
        + matmul_nt(returned[2], value_full)
    )
    grad_inputs_norm, grad_gain_one = rms_backward(grad_normed_one, inputs_own, scale_one, gain_one)
    grad_mine = (grad_mixed + grad_inputs_norm).astype(jnp.bfloat16)
    new_rows = (
        grad_query_weight,
        grad_key_weight,
        grad_value_weight,
        grad_gate_weight,
        grad_up_weight,
        grad_gain_one,
        grad_gain_two,
    )
    new_columns = (grad_output_weight, grad_down)
    return (output_rows, grad_mine, (new_rows, new_columns))


def on_device(
    block_input,
    attention_gain,
    query_weight,
    key_weight,
    value_weight,
    output_weight,
    mlp_gain,
    gate_weight,
    up_weight,
    down_weight,
    grad_output,
):
    row_shards = (
        query_weight,
        key_weight,
        value_weight,
        gate_weight,
        up_weight,
        attention_gain,
        mlp_gain,
    )
    column_shards = (output_weight, down_weight)
    micro_count = block_input.shape[0]
    grads_full = None
    settled = None
    output_list = []
    grad_list = []
    for micro_index in range(micro_count):
        weights_kept = fetch_weights(row_shards, column_shards)
        grads_full = zero_grads(weights_kept)
        output_rows, grad_mine, grads_full = one_micro_heads(
            block_input[micro_index, 0], grad_output[micro_index, 0], weights_kept
        )
        output_list.append(output_rows)
        grad_list.append(grad_mine)
        fresh = settle_grads(grads_full[0], grads_full[1])
        if settled is None:
            settled = fresh
        else:
            settled = (
                tuple((older + newer for older, newer in zip(settled[0], fresh[0]))),
                tuple((older + newer for older, newer in zip(settled[1], fresh[1]))),
            )
        grads_full = None
    row_part, column_part = settled
    block_output = jnp.stack(output_list)[:, None]
    input_grad = jnp.stack(grad_list)[:, None]
    return (
        block_output,
        input_grad,
        row_part[5],
        row_part[0],
        row_part[1],
        row_part[2],
        column_part[0],
        row_part[6],
        row_part[3],
        row_part[4],
        column_part[1],
    )


def solution(mesh):
    return jax.shard_map(
        on_device,
        mesh=mesh,
        in_specs=(
            P(None, "dp", ("head", "blk"), None),
            P(("dp", "blk")),
            P(("dp", "blk"), "head"),
            P(("dp", "blk"), "head"),
            P(("dp", "blk"), "head"),
            P("head", ("dp", "blk")),
            P(("dp", "blk")),
            P(("dp", "blk"), "head"),
            P(("dp", "blk"), "head"),
            P("head", ("dp", "blk")),
            P(None, "dp", ("head", "blk"), None),
        ),
        out_specs=(
            P(None, "dp", ("head", "blk"), None),
            P(None, "dp", ("head", "blk"), None),
            P(("dp", "blk")),
            P(("dp", "blk"), "head"),
            P(("dp", "blk"), "head"),
            P(("dp", "blk"), "head"),
            P("head", ("dp", "blk")),
            P(("dp", "blk")),
            P(("dp", "blk"), "head"),
            P(("dp", "blk"), "head"),
            P("head", ("dp", "blk")),
        ),
        check_vma=False,
    )
```

profile of v0, /device:TPU:0, one launch (start us, length us, event | category | flops | bytes accessed | tf_op | source)
XLA Modules:
  0.0 4308.0 jit_solution(11002866716401183872)
XLA Ops:
  9.4 54.2 %all-gather.20.cloned.1.call-done = bf16[2048,1024]{1,0:T(8,128)(2,1)} async-done(((bf16[128,1024]{1,0:T(8,128)(2,1)}), bf16[2048,1024]{1,0:T(8,128)(2,1)}) %all-gather.20.cloned.1.call-update) | async-done | bytes 4194320 | tf_op jit(solution)/shard_map/all_gather | solution.py:57
  63.7 51.4 %all-gather.24.cloned.1.call-done = bf16[2048,1024]{1,0:T(8,128)(2,1)} async-done(((bf16[128,1024]{1,0:T(8,128)(2,1)}), bf16[2048,1024]{1,0:T(8,128)(2,1)}) %all-gather.24.cloned.1.call-update) | async-done | bytes 4194320 | tf_op jit(solution)/shard_map/all_gather | solution.py:57
  115.2 51.4 %all-gather.28.cloned.1.call-done = bf16[2048,1024]{1,0:T(8,128)(2,1)} async-done(((bf16[128,1024]{1,0:T(8,128)(2,1)}), bf16[2048,1024]{1,0:T(8,128)(2,1)}) %all-gather.28.cloned.1.call-update) | async-done | bytes 4194320 | tf_op jit(solution)/shard_map/all_gather | solution.py:57
  198.3 72.2 %all-gather.22.cloned.1.call-done = bf16[2048,2048]{1,0:T(8,128)(2,1)} async-done(((bf16[2048,1024]{1,0:T(8,128)(2,1)}), bf16[2048,2048]{1,0:T(8,128)(2,1)}) %all-gather.22.cloned.1.call-update) | async-done | bytes 8388624 | tf_op jit(solution)/shard_map/all_gather | solution.py:66
  282.9 93.0 %all-gather.26.cloned.1.call-done = bf16[2048,2048]{1,0:T(8,128)(2,1)} async-done(((bf16[2048,1024]{1,0:T(8,128)(2,1)}), bf16[2048,2048]{1,0:T(8,128)(2,1)}) %all-gather.26.cloned.1.call-update) | async-done | bytes 8388624 | tf_op jit(solution)/shard_map/all_gather | solution.py:67
  409.3 72.1 %all-gather.30.cloned.1.call-done = bf16[2048,2048]{1,0:T(8,128)(2,1)} async-done(((bf16[2048,1024]{1,0:T(8,128)(2,1)}), bf16[2048,2048]{1,0:T(8,128)(2,1)}) %all-gather.30.cloned.1.call-update) | async-done | bytes 8388624 | tf_op jit(solution)/shard_map/all_gather | solution.py:68
  541.4 85.3 %while.60 = (s32[]{:T(128)}, f32[2,16,128]{2,1,0:T(8,128)S(1)}, f32[2,16,128]{2,1,0:T(8,128)S(1)}, f32[2,128,16,64]{1,3,2,0:T(8,128)S(1)}, bf16[2,2,128,16,64]{2...) while((s32[]{:T(128)}, f32[2,16,128]{2,1,0:T(8,128)S(1)}, ...), condition=%wide.region_12.13_spmd, body=%wide.region_5.12_spmd.sunk | while | flops 208168960 | bytes 24854792 | solution.py:223
  715.7 106.4 %all-gather.38.cloned.1.call-done = bf16[2048,4096]{1,0:T(8,128)(2,1)} async-done(((bf16[128,4096]{1,0:T(8,128)(2,1)}), bf16[2048,4096]{1,0:T(8,128)(2,1)}) %all-gather.38.cloned.1.call-update) | async-done | bytes 16777232 | tf_op jit(solution)/shard_map/all_gather | solution.py:57
  834.8 114.6 %all-gather.40.cloned.1.call-done = bf16[2048,4096]{1,0:T(8,128)(2,1)} async-done(((bf16[128,4096]{1,0:T(8,128)(2,1)}), bf16[2048,4096]{1,0:T(8,128)(2,1)}) %all-gather.40.cloned.1.call-update) | async-done | bytes 16777232 | tf_op jit(solution)/shard_map/all_gather | solution.py:57
  970.9 132.5 %all-gather.42.cloned.1.call-done = bf16[4096,2048]{1,0:T(8,128)(2,1)} async-done(((bf16[4096,128]{1,0:T(8,128)(2,1)}), bf16[4096,2048]{1,0:T(8,128)(2,1)}) %all-gather.42.cloned.1.call-update) | async-done | bytes 16777232 | tf_op jit(solution)/shard_map/all_gather | solution.py:62
  1141.7 85.3 %while.61 = (s32[]{:T(128)}, f32[2,16,128]{2,1,0:T(8,128)S(1)}, f32[2,16,128]{2,1,0:T(8,128)S(1)}, f32[2,128,16,64]{1,3,2,0:T(8,128)S(1)}, bf16[2,2,128,16,64]{2...) while((s32[]{:T(128)}, f32[2,16,128]{2,1,0:T(8,128)S(1)}, ...), condition=%wide.region_27.28_spmd, body=%wide.region_20.27_spmd.sunk | while | flops 208168960 | bytes 24854792 | solution.py:223
  1474.2 259.1 %while.62 = (s32[]{:T(128)}, f32[2,128,16,64]{1,3,2,0:T(8,128)}, f32[2,2,128,16,64]{2,4,3,1,0:T(8,128)S(1)}, bf16[2,2,128,16,64]{2,4,3,1,0:T(8,128)(2,1)}, s32[3...) while((s32[]{:T(128)}, f32[2,128,16,64]{1,3,2,0:T(8,128)}, ...), condition=%wide.region_36.37_spmd, body=%wide.region_33.0_spmd.sunk | while | flops 513671168 | bytes 70091152 | solution.py:305
  1480.8 44.1 %collective-permute-done.2 = bf16[2,2,128,16,64]{2,4,3,1,0:T(8,128)(2,1)} collective-permute-done((bf16[2,2,128,16,64]{2,4,3,1,0:T(8,128)(2,1)}, bf16[2,2,128,16,64]{2,4,3,1,0:T(8,128)(2,1)}, u32[]{:S(2)}, u32[]{:S(2)}) %collective-permute-start.2) | collective-permute-done | bytes 1048608 | tf_op jit(solution)/shard_map/while/body/eval_jaxpr/ppermute | solution.py:17
  1773.5 222.2 %while.63 = (s32[]{:T(128)}, f32[2,128,16,64]{1,3,2,0:T(8,128)}, f32[2,2,128,16,64]{2,4,3,1,0:T(8,128)S(1)}, bf16[2,2,128,16,64]{2,4,3,1,0:T(8,128)(2,1)}, s32[3...) while((s32[]{:T(128)}, f32[2,128,16,64]{1,3,2,0:T(8,128)}, ...), condition=%wide.region_44.45_spmd, body=%wide.region_41.0_spmd.sunk | while | flops 513671168 | bytes 70091152 | solution.py:305
  2147.3 101.0 %reduce-scatter.36.cloned.1.call-done = f32[128,2048]{1,0:T(8,128)} async-done(((f32[2048,2048]{1,0:T(8,128)}), f32[128,2048]{1,0:T(8,128)}) %reduce-scatter.36.cloned.1.call-update) | async-done | bytes 1048592 | tf_op jit(solution)/shard_map/reduce_scatter | solution.py:77
  2250.5 179.6 %reduce-scatter.32.cloned.1.call-done = f32[128,2048]{1,0:T(8,128)} async-done(((f32[2048,2048]{1,0:T(8,128)}), f32[128,2048]{1,0:T(8,128)}) %reduce-scatter.32.cloned.1.call-update) | async-done | bytes 1048592 | tf_op jit(solution)/shard_map/reduce_scatter | solution.py:77
  2432.2 179.4 %reduce-scatter.44.cloned.1.call-done = f32[128,2048]{1,0:T(8,128)} async-done(((f32[2048,2048]{1,0:T(8,128)}), f32[128,2048]{1,0:T(8,128)}) %reduce-scatter.44.cloned.1.call-update) | async-done | bytes 1048592 | tf_op jit(solution)/shard_map/reduce_scatter | solution.py:77
  2613.8 179.5 %reduce-scatter.40.cloned.1.call-done = f32[128,2048]{1,0:T(8,128)} async-done(((f32[2048,2048]{1,0:T(8,128)}), f32[128,2048]{1,0:T(8,128)}) %reduce-scatter.40.cloned.1.call-update) | async-done | bytes 1048592 | tf_op jit(solution)/shard_map/reduce_scatter | solution.py:77
  2795.5 179.4 %reduce-scatter.52.cloned.1.call-done = f32[128,2048]{1,0:T(8,128)} async-done(((f32[2048,2048]{1,0:T(8,128)}), f32[128,2048]{1,0:T(8,128)}) %reduce-scatter.52.cloned.1.call-update) | async-done | bytes 1048592 | tf_op jit(solution)/shard_map/reduce_scatter | solution.py:77
  2997.3 159.1 %reduce-scatter.48.cloned.1.call-done = f32[128,2048]{1,0:T(8,128)} async-done(((f32[2048,2048]{1,0:T(8,128)}), f32[128,2048]{1,0:T(8,128)}) %reduce-scatter.48.cloned.1.call-update) | async-done | bytes 1048592 | tf_op jit(solution)/shard_map/reduce_scatter | solution.py:77
  3301.3 60.4 %all-reduce.14 = (bf16[2048]{0:T(1024)(128)(2,1)S(1)}, bf16[2048]{0:T(1024)(128)(2,1)S(1)}, bf16[2048]{0:T(1024)(128)(2,1)S(1)}, bf16[2048]{0:T(1024)(128)(2,1)S(1)}) all-reduce(f32[2048]{0:T(1024)S(1)} %copy-done.107, f32[2048]{0:T(1024)S(1)} %get-tuple-element.374, ...), channel_id=15, replica_groups=mesh['dp'=4,'head'=2,'blk'=4] {'dp','blk'}, use_global_device_ids=true, to_apply=%region_54.55.clone | all-reduce | flops 8192 | bytes 49152
  3379.8 248.2 %reduce-scatter.64.cloned.1.call-done = f32[128,4096]{1,0:T(8,128)} async-done(((f32[2048,4096]{1,0:T(8,128)}), f32[128,4096]{1,0:T(8,128)}) %reduce-scatter.64.cloned.1.call-update) | async-done | bytes 2097168 | tf_op jit(solution)/shard_map/reduce_scatter | solution.py:77
  3628.0 336.4 %reduce-scatter.66.cloned.1.call-done = f32[128,4096]{1,0:T(8,128)} async-done(((f32[2048,4096]{1,0:T(8,128)}), f32[128,4096]{1,0:T(8,128)}) %reduce-scatter.66.cloned.1.call-update) | async-done | bytes 2097168 | tf_op jit(solution)/shard_map/reduce_scatter | solution.py:77
  3964.4 336.6 %reduce-scatter.68.cloned.1.call-done = f32[4096,128]{1,0:T(8,128)} async-done(((f32[4096,2048]{1,0:T(8,128)}), f32[4096,128]{1,0:T(8,128)}) %reduce-scatter.68.cloned.1.call-update) | async-done | bytes 2097168 | tf_op jit(solution)/shard_map/reduce_scatter | solution.py:78
  (787 shorter events, 1530.2 us)
Async XLA Ops:
  63.7 312.2 %all-gather.26.cloned.1.call-start = ((), (), s32[]{:S(2)}) async-start(), calls=%async_computation.34 | async-start | bytes 12582912 | tf_op jit(solution)/shard_map/all_gather | solution.py:67
  115.1 366.2 %all-gather.30.cloned.1.call-start = ((), (), s32[]{:S(2)}) async-start(), calls=%async_computation.36 | async-start | bytes 12582912 | tf_op jit(solution)/shard_map/all_gather | solution.py:68
  166.6 369.9 %all-gather.32.cloned.1.call-start = ((), (), s32[]{:S(2)}) async-start(), calls=%async_computation.37 | async-start | bytes 4456448 | tf_op jit(solution)/shard_map/all_gather | solution.py:62
  669.0 434.3 %all-gather.42.cloned.1.call-start = ((), (), s32[]{:S(2)}) async-start(), calls=%async_computation.42 | async-start | bytes 17825792 | tf_op jit(solution)/shard_map/all_gather | solution.py:62
  683.7 558.7 %reduce-scatter.28.cloned.1.call-start = ((), (), s32[]{:S(2)}) async-start(), calls=%async_computation.46 | async-start | bytes 1572864 | tf_op jit(solution)/shard_map/reduce_scatter | solution.py:378
  1346.1 796.8 %reduce-scatter.60.cloned.1.call-start = ((), (), s32[]{:S(2)}) async-start(), calls=%async_computation.62 | async-start | bytes 17825792 | tf_op jit(solution)/shard_map/reduce_scatter | solution.py:78
  1402.6 742.5 %reduce-scatter.56.cloned.1.call-start = ((), (), s32[]{:S(2)}) async-start(), calls=%async_computation.60 | async-start | bytes 17825792 | tf_op jit(solution)/shard_map/reduce_scatter | solution.py:78
  1463.8 784.6 %reduce-scatter.36.cloned.1.call-start = ((), (), s32[]{:S(2)}) async-start(), calls=%async_computation.50 | async-start | bytes 17825792 | tf_op jit(solution)/shard_map/reduce_scatter | solution.py:77
  2071.7 358.4 %reduce-scatter.32.cloned.1.call-start = ((), (), s32[]{:S(2)}) async-start(), calls=%async_computation.48 | async-start | bytes 17825792 | tf_op jit(solution)/shard_map/reduce_scatter | solution.py:77
  2108.1 503.5 %reduce-scatter.44.cloned.1.call-start = ((), (), s32[]{:S(2)}) async-start(), calls=%async_computation.54 | async-start | bytes 17825792 | tf_op jit(solution)/shard_map/reduce_scatter | solution.py:77
  2116.5 676.8 %reduce-scatter.40.cloned.1.call-start = ((), (), s32[]{:S(2)}) async-start(), calls=%async_computation.52 | async-start | bytes 17825792 | tf_op jit(solution)/shard_map/reduce_scatter | solution.py:77
  2125.9 849.0 %reduce-scatter.52.cloned.1.call-start = ((), (), s32[]{:S(2)}) async-start(), calls=%async_computation.58 | async-start | bytes 17825792 | tf_op jit(solution)/shard_map/reduce_scatter | solution.py:77
  2134.4 1022.0 %reduce-scatter.48.cloned.1.call-start = ((), (), s32[]{:S(2)}) async-start(), calls=%async_computation.56 | async-start | bytes 17825792 | tf_op jit(solution)/shard_map/reduce_scatter | solution.py:77
  2142.9 1229.3 %reduce-scatter.62.cloned.1.call-start = ((), (), s32[]{:S(2)}) async-start(), calls=%async_computation.63 | async-start | bytes 786432 | tf_op jit(solution)/shard_map/reduce_scatter | solution.py:91
  2145.1 1227.1 %reduce-scatter.58.cloned.1.call-start = ((), (), s32[]{:S(2)}) async-start(), calls=%async_computation.61 | async-start | bytes 786432 | tf_op jit(solution)/shard_map/reduce_scatter | solution.py:91
  2147.3 1226.8 %reduce-scatter.38.cloned.1.call-start = ((), (), s32[]{:S(2)}) async-start(), calls=%async_computation.51 | async-start | bytes 786432 | tf_op jit(solution)/shard_map/reduce_scatter | solution.py:82
  2250.5 1123.6 %reduce-scatter.34.cloned.1.call-start = ((), (), s32[]{:S(2)}) async-start(), calls=%async_computation.49 | async-start | bytes 786432 | tf_op jit(solution)/shard_map/reduce_scatter | solution.py:82
  2432.2 943.8 %reduce-scatter.46.cloned.1.call-start = ((), (), s32[]{:S(2)}) async-start(), calls=%async_computation.55 | async-start | bytes 786432 | tf_op jit(solution)/shard_map/reduce_scatter | solution.py:85
  2613.8 762.2 %reduce-scatter.42.cloned.1.call-start = ((), (), s32[]{:S(2)}) async-start(), calls=%async_computation.53 | async-start | bytes 786432 | tf_op jit(solution)/shard_map/reduce_scatter | solution.py:85
  2795.5 582.4 %reduce-scatter.54.cloned.1.call-start = ((), (), s32[]{:S(2)}) async-start(), calls=%async_computation.59 | async-start | bytes 786432 | tf_op jit(solution)/shard_map/reduce_scatter | solution.py:88
  2977.0 400.9 %reduce-scatter.50.cloned.1.call-start = ((), (), s32[]{:S(2)}) async-start(), calls=%async_computation.57 | async-start | bytes 786432 | tf_op jit(solution)/shard_map/reduce_scatter | solution.py:88
  3158.5 469.4 %reduce-scatter.64.cloned.1.call-start = ((), (), s32[]{:S(2)}) async-start(), calls=%async_computation.66 | async-start | bytes 35651584 | tf_op jit(solution)/shard_map/reduce_scatter | solution.py:77
  3184.4 780.0 %reduce-scatter.66.cloned.1.call-start = ((), (), s32[]{:S(2)}) async-start(), calls=%async_computation.67 | async-start | bytes 35651584 | tf_op jit(solution)/shard_map/reduce_scatter | solution.py:77
  3225.0 1076.0 %reduce-scatter.68.cloned.1.call-start = ((), (), s32[]{:S(2)}) async-start(), calls=%async_computation.68 | async-start | bytes 35651584 | tf_op jit(solution)/shard_map/reduce_scatter | solution.py:78
  (165 other events, 6510.0 us)
Sparse Core Ops, SparseCore 0:
  10.2 53.3 all-gather.19
  65.9 49.1 all-gather.23
  117.3 49.1 all-gather.27
  168.0 102.4 all-gather.21
  271.9 103.9 all-gather.25
  377.3 103.9 all-gather.29
  483.4 52.9 all-gather.31
  538.0 107.7 all-gather.33
  666.7 24.5 all-gather.35
  693.3 128.7 all-gather.37
  824.4 124.9 all-gather.39
  973.0 130.3 all-gather.41
  1267.1 21.2 all-gather.47
  1402.8 241.3 reduce-scatter.59
  1648.3 229.5 reduce-scatter.55
  2071.8 176.5 reduce-scatter.35
  2252.5 177.5 reduce-scatter.31
  2434.1 177.5 reduce-scatter.43
  2615.7 177.5 reduce-scatter.39
  2797.3 177.5 reduce-scatter.51
  2978.8 177.5 reduce-scatter.47
  3294.8 333.0 reduce-scatter.63
  3632.6 331.7 reduce-scatter.65
  3969.2 331.7 reduce-scatter.67
  (14 shorter events, 232.7 us)
where the time goes:
time: 4320 us; the launch traced here: 4310 us
  waiting for transfers between devices  3310 us (77%)
  matrix products  468 us (11%)
  blocking collectives  168 us (4%)
  other arithmetic  116 us (3%)
  local copies, waits for them, and re-layouts  109 us (3%)
  starting transfers between devices  108 us (2%)
    reduce_scatter x8, waiting for transfers between devices, settle_grads(): lax.psum_scatter(row_grads, ('dp', 'blk'), scatter_dimension=0, tiled=True)  1560 us
    ppermute x20, waiting for transfers between devices, passed_along(): return lax.ppermute(value, axis, pairs)  517 us
    all_gather x5, waiting for transfers between devices, fetch_weights(): lax.all_gather(for_sending(row_shards), ('dp', 'blk'), axis=0, tiled=True)  378 us
    reduce_scatter x3, waiting for transfers between devices, settle_grads(): lax.psum_scatter(column_grads, ('dp', 'blk'), scatter_dimension=1, tiled=...  337 us
    dot_general x14, matrix products, matmul_tn(): lax.dot_general(left_side, right_side, (((0,), (0,)), ((), ())), preferre...  198 us
    all_gather x2, waiting for transfers between devices, fetch_weights(): lax.all_gather(for_sending(column_shards), ('dp', 'blk'), axis=1, tiled=T...  176 us
    dot_general x14, matrix products, matmul_nt(): lax.dot_general(left_side, right_side, (((1,), (1,)), ((), ())), preferre...  118 us
    dot_general x14, matrix products, matmul(): return jnp.dot(left_side, right_side, preferred_element_type=jnp.float32)  106 us
  transfers between devices with their start and end apart: 63, of which 44 were waited for; matrix products, arithmetic and copies ran while one was open for 14% of the time, Pallas kernels for 0%

commit v1 on v0

v1 whole, which is shorter than its diff:
```python
import functools

import jax
import jax.numpy as jnp
import numpy as np
from jax import lax
from jax.experimental import pallas as pl
from jax.experimental.pallas import tpu as pltpu
from jax.sharding import PartitionSpec as P

HD = 64
EPSILON = 1e-05
ROPE_BASE = 130000.0
MASKED_SCORE = -1e30
F32 = jnp.float32
BF16 = jnp.bfloat16
LANES = 128


def swap(value, axis, bit):
    count = lax.axis_size(axis)
    return lax.ppermute(value, axis, [(i, i ^ bit) for i in range(count)])


def bits_of(count):
    return [1 << i for i in range(count.bit_length() - 1)]


def replica_stages():
    upper = [("blk", bit) for bit in bits_of(lax.axis_size("blk"))[1:]]
    return upper + [("dp", bit) for bit in reversed(bits_of(lax.axis_size("dp")))]


def matmul(left_side, right_side):
    return jnp.dot(left_side, right_side, preferred_element_type=F32)


def matmul_nt(left_side, right_side):
    return lax.dot_general(left_side, right_side, (((1,), (1,)), ((), ())), preferred_element_type=F32)


def matmul_tn(left_side, right_side):
    return lax.dot_general(left_side, right_side, (((0,), (0,)), ((), ())), preferred_element_type=F32)


def feature_order():
    n_blk, n_dp = lax.axis_size("blk"), lax.axis_size("dp")
    order = np.zeros((1,), np.int32)
    for axis, bit in replica_stages():
        order = np.concatenate([order, order ^ (bit if axis == "blk" else bit * n_blk)])
    order = np.concatenate([order, order ^ 1])
    assert order.size == n_blk * n_dp
    mine = lax.axis_index("dp") * n_blk + lax.axis_index("blk")
    back = np.argsort(order).astype(np.int32)
    absolute = jnp.arange(order.size, dtype=jnp.int32) ^ mine
    return jnp.asarray(order) ^ mine, jnp.asarray(back)[absolute]


def reorder_kernel(order_ref, source_ref, target_ref):
    target_ref[...] = source_ref[...]


def reorder(rows, order):
    count, width = rows.shape
    blocks = order.shape[0]
    piece = width // blocks
    if piece % LANES:
        return jnp.take(rows.reshape(count, blocks, piece), order, axis=1).reshape(count, width)
    return pl.pallas_call(
        reorder_kernel,
        grid_spec=pltpu.PrefetchScalarGridSpec(
            num_scalar_prefetch=1,
            grid=(blocks,),
            in_specs=[pl.BlockSpec((count, piece), lambda j, order_ref: (0, order_ref[j]))],
            out_specs=pl.BlockSpec((count, piece), lambda j, order_ref: (0, j)),
        ),
        out_shape=jax.ShapeDtypeStruct(rows.shape, rows.dtype),
    )(order, rows)


def turn_features(rows):
    half = rows.shape[1] // 2
    return jnp.concatenate([rows[:, half:], rows[:, :half]], 1)


def gather_tokens(rows, head_first):
    count = rows.shape[0]
    if head_first:
        other = swap(rows, "head", 1)
        far = swap(turn_features(jnp.concatenate([rows, other], 0)), "blk", 1)
        return jnp.concatenate([rows, far[:count], other, far[count:]], 0)
    both = jnp.concatenate([rows, swap(turn_features(rows), "blk", 1)], 0)
    return jnp.concatenate([both, swap(both, "head", 1)], 0)


def scatter_tokens(partial, head_first):
    partial = partial.astype(BF16)
    count = partial.shape[0] // 4
    if head_first:
        came = swap(partial[2 * count :], "head", 1)
        mine = partial[:count].astype(F32) + came[:count].astype(F32)
        theirs = (partial[count : 2 * count].astype(F32) + came[count:].astype(F32)).astype(BF16)
        return mine + swap(turn_features(theirs), "blk", 1).astype(F32)
    leaving = jnp.concatenate([partial[count : 2 * count], partial[3 * count :]], 0)
    came = swap(turn_features(leaving), "blk", 1)
    mine = partial[:count].astype(F32) + came[:count].astype(F32)
    theirs = (partial[2 * count : 3 * count].astype(F32) + came[count:].astype(F32)).astype(BF16)
    return mine + swap(theirs, "head", 1).astype(F32)


def own_and_other(columns):
    width = columns.shape[1] // 2
    place = lax.axis_index("blk") % 2
    return (
        lax.dynamic_slice_in_dim(columns, place * width, width, 1),
        lax.dynamic_slice_in_dim(columns, (1 - place) * width, width, 1),
    )


def gather_weight(own, other):
    streams = [own, swap(other, "blk", 1)]
    stages = replica_stages()
    for axis, bit in stages[:-1]:
        streams = [jnp.concatenate([held, swap(held, axis, bit)], 0) for held in streams]
    pieces = []
    for held in streams:
        pieces += [held, swap(held, *stages[-1])]
    return jnp.concatenate(pieces, 0)


def scatter_weight_grad(acts, grads):
    quarter = acts.shape[1] // 4
    stages = replica_stages()[::-1]

    def piece(place):
        return matmul_tn(acts[:, place * quarter : (place + 1) * quarter], grads).astype(BF16)

    streams = []
    for first in (2, 0):
        came = swap(piece(first + 1), *stages[0])
        held = piece(first).astype(F32) + came.astype(F32)
        for axis, bit in stages[1:]:
            half = held.shape[0] // 2
            held = held.astype(BF16)
            came = swap(held[half:], axis, bit)
            held = held[:half].astype(F32) + came.astype(F32)
        streams.append(held)
    return streams[1], swap(streams[0].astype(BF16), "blk", 1)


def side_by_side(own, other):
    other = other.astype(F32)
    low = lax.axis_index("blk") % 2 == 0
    return jnp.concatenate([jnp.where(low, own, other), jnp.where(low, other, own)], 1)


def head_groups():
    return lax.axis_size("blk") // 2


def to_sequences(parts):
    groups = head_groups()
    upper = lax.axis_index("blk") // 2
    width = parts[0].shape[1] // groups
    arrived = []
    for r in range(groups):
        chosen = jnp.stack([lax.dynamic_slice_in_dim(part, (upper ^ r) * width, width, 1) for part in parts])
        if r:
            chosen = lax.ppermute(chosen, "blk", [(i, i ^ (2 * r)) for i in range(2 * groups)])
        arrived.append(chosen.reshape(len(parts), 4, -1, width))
    return jnp.concatenate(arrived, 1)


def from_sequences(blocks):
    groups = head_groups()
    upper = lax.axis_index("blk") // 2
    count, _, tokens, width = blocks.shape
    arrived = []
    for r in range(groups):
        chosen = blocks[:, 4 * r : 4 * r + 4]
        if r:
            chosen = lax.ppermute(chosen, "blk", [(i, i ^ (2 * r)) for i in range(2 * groups)])
        arrived.append(chosen.reshape(count, 4 * tokens, width))
    stacked = jnp.stack(arrived)
    ordered = [lax.dynamic_index_in_dim(stacked, h ^ upper, 0, keepdims=False) for h in range(groups)]
    return jnp.concatenate(ordered, 2)


def block_order():
    n_blk, n_head = lax.axis_size("blk"), lax.axis_size("head")
    block = np.arange(n_blk * n_head, dtype=np.int32)
    r_head = (block // n_blk) ^ lax.axis_index("head")
    r_blk = (block % n_blk) ^ lax.axis_index("blk")
    return ((r_blk // 2) * 2 + r_head) * 2 + r_blk % 2


def rope_tables(length, lanes):
    half = HD // 2
    frequency = ROPE_BASE ** (-jnp.arange(half, dtype=F32) * 2.0 / HD)
    angles = jnp.arange(length, dtype=F32)[:, None] * frequency[None, :]
    cosine, sine = jnp.cos(angles), jnp.sin(angles)
    return (
        jnp.tile(cosine, (1, lanes // half)),
        jnp.tile(jnp.concatenate([-sine, sine], 1), (1, lanes // HD)),
    )


def turned(rows, cosine, sine):
    half = HD // 2
    parts = []
    for start in range(0, rows.shape[1], HD):
        parts += [rows[:, start + half : start + HD], rows[:, start : start + half]]
    return rows * cosine + jnp.concatenate(parts, 1) * sine


def load_sequence(order_ref, qkv_ref, cosine_ref, sine_ref, held, tokens, blocks):
    def one(block, carry):
        place = order_ref[block]
        rows = pl.ds(pl.multiple_of(block * tokens, tokens), tokens)
        for part in range(3):
            value = qkv_ref[part, place]
            if part < 2:
                value = turned(value.astype(F32), cosine_ref[rows, :], sine_ref[rows, :]).astype(BF16)
            held[part][rows, :] = value
        return carry

    lax.fori_loop(0, blocks, one, 0)


def softmax_rows(query, keys, first_row):
    scores = matmul_nt(query, keys) * HD ** (-0.5)
    row = first_row + lax.broadcasted_iota(jnp.int32, scores.shape, 0)
    scores = jnp.where(lax.broadcasted_iota(jnp.int32, scores.shape, 1) <= row, scores, MASKED_SCORE)
    weights = jnp.exp(scores - jnp.max(scores, 1, keepdims=True))
    return weights, 1.0 / jnp.sum(weights, 1, keepdims=True)


def attend_kernel(tokens, blocks, rows_at_once, order_ref, qkv_ref, cosine_ref, sine_ref, out_ref, q_s, k_s, v_s):
    lanes = qkv_ref.shape[-1]
    load_sequence(order_ref, qkv_ref, cosine_ref, sine_ref, (q_s, k_s, v_s), tokens, blocks)
    for first in range(0, tokens * blocks, rows_at_once):
        last = first + rows_at_once
        results = []
        for lane in range(0, lanes, HD):
            head = slice(lane, lane + HD)
            weights, inverse = softmax_rows(q_s[first:last, head], k_s[:last, head], first)
            results.append(matmul(weights.astype(BF16), v_s[:last, head]) * inverse)
        result = jnp.concatenate(results, 1).astype(BF16)
        for offset in range(0, rows_at_once, tokens):
            out_ref[order_ref[(first + offset) // tokens]] = result[offset : offset + tokens]


def attend_back_kernel(
    tokens, blocks, rows_at_once, order_ref, qkv_ref, grad_ref, cosine_ref, sine_ref, out_ref,
    q_s, k_s, v_s, dk_s, dv_s,
):
    lanes = qkv_ref.shape[-1]
    load_sequence(order_ref, qkv_ref, cosine_ref, sine_ref, (q_s, k_s, v_s), tokens, blocks)
    dk_s[...] = jnp.zeros_like(dk_s)
    dv_s[...] = jnp.zeros_like(dv_s)
    for first in range(0, tokens * blocks, rows_at_once):
        last = first + rows_at_once
        arrived = [grad_ref[order_ref[row // tokens]] for row in range(first, last, tokens)]
        grad_rows = jnp.concatenate(arrived, 0)
        query_parts, key_parts, value_parts = [], [], []
        for lane in range(0, lanes, HD):
            head = slice(lane, lane + HD)
            query, keys, grad = q_s[first:last, head], k_s[:last, head], grad_rows[:, head]
            weights, inverse = softmax_rows(query, keys, first)
            probabilities = weights * inverse
            grad_prob = matmul_nt(grad, v_s[:last, head])
            row_delta = jnp.sum(probabilities * grad_prob, 1, keepdims=True)
            grad_scores = (probabilities * (grad_prob - row_delta) * HD ** (-0.5)).astype(BF16)
            query_parts.append(matmul(grad_scores, keys))
            key_parts.append(matmul_tn(grad_scores, query))
            value_parts.append(matmul_tn(probabilities.astype(BF16), grad))
        grad_query = jnp.concatenate(query_parts, 1)
        grad_query = turned(grad_query, cosine_ref[first:last, :], -sine_ref[first:last, :]).astype(BF16)
        for offset in range(0, rows_at_once, tokens):
            out_ref[0, order_ref[(first + offset) // tokens]] = grad_query[offset : offset + tokens]
        dk_s[:last, :] += jnp.concatenate(key_parts, 1)
        dv_s[:last, :] += jnp.concatenate(value_parts, 1)

    def one(block, carry):
        place = order_ref[block]
        rows = pl.ds(pl.multiple_of(block * tokens, tokens), tokens)
        out_ref[1, place] = turned(dk_s[rows, :], cosine_ref[rows, :], -sine_ref[rows, :]).astype(BF16)
        out_ref[2, place] = dv_s[rows, :].astype(BF16)
        return carry

    lax.fori_loop(0, blocks, one, 0)


def attention_call(order, qkv, tables, grad=None):
    _, blocks, tokens, width = qkv.shape
    length = blocks * tokens
    lanes = min(LANES, width)
    rows_at_once = min(256, length)
    back = grad is not None

    def fixed(j, order_ref):
        return (0, 0)

    part = pl.BlockSpec((blocks, tokens, lanes), lambda j, order_ref: (0, 0, j))
    three = pl.BlockSpec((3, blocks, tokens, lanes), lambda j, order_ref: (0, 0, 0, j))
    table = pl.BlockSpec((length, lanes), fixed)
    kernel = attend_back_kernel if back else attend_kernel
    scratch = [pltpu.VMEM((length, lanes), BF16)] * 3
    if back:
        scratch += [pltpu.VMEM((length, lanes), F32)] * 2
    products = 5 if back else 2
    return pl.pallas_call(
        functools.partial(kernel, tokens, blocks, rows_at_once),
        grid_spec=pltpu.PrefetchScalarGridSpec(
            num_scalar_prefetch=1,
            grid=(width // lanes,),
            in_specs=[three] + ([part] if back else []) + [table, table],
            out_specs=three if back else part,
            scratch_shapes=scratch,
        ),
        out_shape=jax.ShapeDtypeStruct(qkv.shape if back else qkv.shape[1:], BF16),
        compiler_params=pltpu.CompilerParams(vmem_limit_bytes=48 * 1024 * 1024),
        cost_estimate=pl.CostEstimate(
            flops=products * 4 * length * length * width,
            bytes_accessed=(7 if back else 4) * length * width * 2,
            transcendentals=length * length * (width // HD),
        ),
    )(order, qkv, *([grad] if back else []), *tables)


def scale_of(values):
    return lax.rsqrt(jnp.mean(values * values, -1, keepdims=True) + EPSILON)


def norm_back(grad, values, scale):
    return scale * grad - values * (scale * scale * scale) * jnp.mean(grad * values, -1, keepdims=True)


def on_device(
    block_input,
    attention_gain,
    query_weight,
    key_weight,
    value_weight,
    output_weight,
    mlp_gain,
    gate_weight,
    up_weight,
    down_weight,
    grad_output,
):
    micros, _, tokens, width = block_input.shape
    heads_width = query_weight.shape[1] // 2
    length = tokens * lax.axis_size("blk") * lax.axis_size("head")
    to_own, to_absolute = feature_order()
    order = block_order()
    tables = rope_tables(length, min(LANES, heads_width // head_groups()))
    each = range(micros)
    head_first = [m % 2 == 1 for m in each]

    gain_one = attention_gain.astype(F32)[:, None]
    gain_two = mlp_gain.astype(F32)[:, None]

    def scaled(weight, gain):
        return (weight.astype(F32) * gain).astype(BF16)

    attention_parts = [own_and_other(scaled(w, gain_one)) for w in (query_weight, key_weight, value_weight)]
    qkv_full = gather_weight(*(jnp.concatenate(side, 1) for side in zip(*attention_parts)))
    output_full = gather_weight(*own_and_other(output_weight.T))
    gate_full = gather_weight(*own_and_other(scaled(gate_weight, gain_two)))
    up_full = gather_weight(*own_and_other(scaled(up_weight, gain_two)))
    down_full = gather_weight(*own_and_other(down_weight.T))

    inputs_low = reorder(block_input.reshape(micros * tokens, width), to_own).reshape(micros, tokens, width)
    grad_low = reorder(grad_output.reshape(micros * tokens, width), to_own).reshape(micros, tokens, width)
    inputs = [inputs_low[m].astype(F32) for m in each]
    scale_one = [scale_of(inputs[m]) for m in each]
    normed_one = [gather_tokens((inputs[m] * scale_one[m]).astype(BF16), head_first[m]) for m in each]

    sequences = []
    for m in each:
        qkv = matmul(normed_one[m], qkv_full).astype(BF16)
        parts = [qkv[:, i * heads_width : (i + 1) * heads_width] for i in range(3)]
        sequences.append(to_sequences(parts))
    attended = [from_sequences(attention_call(order, sequences[m], tables)[None])[0] for m in each]
    mixed = [
        inputs[m] + scatter_tokens(matmul_nt(attended[m], output_full), head_first[m]) for m in each
    ]
    scale_two = [scale_of(mixed[m]) for m in each]
    normed_two = [gather_tokens((mixed[m] * scale_two[m]).astype(BF16), head_first[m]) for m in each]
    grad_rows = [gather_tokens(grad_low[m], head_first[m]) for m in each]

    hidden, grad_gate, grad_up, grad_mixed, outputs = [], [], [], [], []
    for m in each:
        gate = matmul(normed_two[m], gate_full)
        up = matmul(normed_two[m], up_full)
        sigmoid = jax.nn.sigmoid(gate)
        activated = gate * sigmoid
        hidden.append((activated * up).astype(BF16))
        grad_hidden = matmul(grad_rows[m], down_full)
        grad_gate.append((grad_hidden * up * sigmoid * (1.0 + gate * (1.0 - sigmoid))).astype(BF16))
        grad_up.append((grad_hidden * activated).astype(BF16))
        grad_normed = matmul_nt(grad_gate[m], gate_full) + matmul_nt(grad_up[m], up_full)
        grad_normed = scatter_tokens(grad_normed, head_first[m])
        grad_mixed.append(grad_low[m].astype(F32) + norm_back(grad_normed, mixed[m], scale_two[m]))
    for m in each:
        outputs.append(
            (mixed[m] + scatter_tokens(matmul_nt(hidden[m], down_full), head_first[m])).astype(BF16)
        )

    def joined(parts):
        return jnp.concatenate(parts, 0)

    normed_two_all = joined(normed_two)
    gate_grad = scatter_weight_grad(normed_two_all, joined(grad_gate))
    up_grad = scatter_weight_grad(normed_two_all, joined(grad_up))
    down_grad = scatter_weight_grad(joined(grad_rows), joined(hidden))

    grad_mixed_rows = [gather_tokens(grad_mixed[m].astype(BF16), head_first[m]) for m in each]
    grad_qkv, input_grads = [], []
    for m in each:
        grad_attended = matmul(grad_mixed_rows[m], output_full).astype(BF16)
        grad_sequences = attention_call(order, sequences[m], tables, to_sequences([grad_attended])[0])
        returned = from_sequences(grad_sequences)
        grad_qkv.append(jnp.concatenate([returned[0], returned[1], returned[2]], 1))
        grad_normed = scatter_tokens(matmul_nt(grad_qkv[m], qkv_full), head_first[m])
        input_grads.append((grad_mixed[m] + norm_back(grad_normed, inputs[m], scale_one[m])).astype(BF16))
    output_grad = scatter_weight_grad(joined(grad_mixed_rows), joined(attended))
    qkv_grad = scatter_weight_grad(joined(normed_one), joined(grad_qkv))

    qkv_grads = [
        side_by_side(*(side[:, i * heads_width : (i + 1) * heads_width] for side in qkv_grad)) for i in range(3)
    ]
    mlp_grads = [side_by_side(*gate_grad), side_by_side(*up_grad)]

    def gain_grad(weights, grads):
        terms = [jnp.sum(w.astype(F32) * g, 1) for w, g in zip(weights, grads)]
        here = functools.reduce(jnp.add, terms)
        return here + swap(here, "head", 1)

    attention_gain_grad = gain_grad((query_weight, key_weight, value_weight), qkv_grads)
    mlp_gain_grad = gain_grad((gate_weight, up_weight), mlp_grads)

    def absolute(parts):
        rows = reorder(joined(parts), to_absolute)
        return rows.reshape(micros, 1, tokens, width)

    return (
        absolute(outputs),
        absolute(input_grads),
        attention_gain_grad,
        qkv_grads[0] * gain_one,
        qkv_grads[1] * gain_one,
        qkv_grads[2] * gain_one,
        side_by_side(*output_grad).T,
        mlp_gain_grad,
        mlp_grads[0] * gain_two,
        mlp_grads[1] * gain_two,
        side_by_side(*down_grad).T,
    )


def solution(mesh):
    rows, row_split = P(None, "dp", ("head", "blk"), None), P(("dp", "blk"), "head")
    column_split, gain = P("head", ("dp", "blk")), P(("dp", "blk"))
    return jax.shard_map(
        on_device,
        mesh=mesh,
        in_specs=(
            rows, gain, row_split, row_split, row_split, column_split, gain, row_split, row_split, column_split, rows,
        ),
        out_specs=(
            rows, rows, gain, row_split, row_split, row_split, column_split, gain, row_split, row_split, column_split,
        ),
        check_vma=False,
    )
```

time: 4320 us -> 1380 us (0.32)
  waiting for transfers between devices: 3310 us -> 732 us
  matrix products: 468 us -> 212 us
  blocking collectives: 168 us -> 0 us
  Pallas kernels: 0 us -> 101 us
    reduce_scatter x23 -> x0, waiting for transfers between devices: 1940 us -> none  [the longest x8 1560 us: settle_grads(): lax.psum_scatter(row_grads, ('dp', 'blk'), scatter_dimension=0, tiled=True)]
    all_gather x15 -> x0, waiting for transfers between devices: 822 us -> none  [the longest x5 378 us: fetch_weights(): lax.all_gather(for_sending(row_shards), ('dp', 'blk'), axis=0, tiled=True)]
    ppermute x20 -> x112, waiting for transfers between devices: 517 us -> 732 us  [the longest x104 616 us: swap(): return lax.ppermute(value, axis, [(i, i ^ bit) for i in range(count)])]
    dot_general x14 -> x20, matrix products: 198 us -> 65.6 us  [matmul_tn(): lax.dot_general(left_side, right_side, (((0,), (0,)), ((), ())), preferre...]
    pallas_call x0 -> x8, Pallas kernels: none -> 101 us  [the longest x4 62.5 us: attention_call(): pl.pallas_call(functools.partial(kernel, tokens, blocks, rows_at_once), g...]
    dot_general x80 -> x10, matrix products: 152 us -> 75.7 us  [matmul(): return jnp.dot(left_side, right_side, preferred_element_type=F32)]
    unnamed x2 -> x0, blocking collectives: 65.3 us -> none
    all_gather x2 -> x0, blocking collectives: 58.1 us -> none  [fetch_weights(): lax.all_gather(for_sending(row_shards), ('dp', 'blk'), axis=0, tiled=True)]
  transfers between devices with their start and end apart: 63 -> 112, of which waited for: 44 -> 52; matrix products, arithmetic and copies ran while one was open for 14% -> 23% of each run, Pallas kernels for 0% -> 7%
where the time goes in v1:
time: 1380 us; the launch traced here: 1370 us
  waiting for transfers between devices  732 us (53%)
  matrix products  212 us (15%)
  starting transfers between devices  124 us (9%)
  other arithmetic  102 us (7%)
  Pallas kernels  101 us (7%)
  local copies, waits for them, and re-layouts  92.7 us (7%)
    ppermute x104, waiting for transfers between devices, swap(): return lax.ppermute(value, axis, [(i, i ^ bit) for i in range(count)])  616 us
    ppermute x104, starting transfers between devices, swap(): return lax.ppermute(value, axis, [(i, i ^ bit) for i in range(count)])  117 us
    ppermute x4, waiting for transfers between devices, to_sequences(): lax.ppermute(chosen, 'blk', [(i, i ^ 2 * r) for i in range(2 * groups)])  88.5 us
    dot_general x10, matrix products, matmul(): return jnp.dot(left_side, right_side, preferred_element_type=F32)  75.7 us
    dot_general x10, matrix products, matmul_nt(): lax.dot_general(left_side, right_side, (((1,), (1,)), ((), ())), preferre...  70.5 us
    dot_general x20, matrix products, matmul_tn(): lax.dot_general(left_side, right_side, (((0,), (0,)), ((), ())), preferre...  65.6 us
    pallas_call x4, Pallas kernels, attention_call(): pl.pallas_call(functools.partial(kernel, tokens, blocks, rows_at_once), g...  62.5 us
    unnamed x291, local copies, waits for them, and re-layouts  59.3 us
  transfers between devices with their start and end apart: 112, of which 52 were waited for; matrix products, arithmetic and copies ran while one was open for 23% of the time, Pallas kernels for 7%

profile of v1, /device:TPU:0, one launch (start us, length us, event | category | flops | bytes accessed | tf_op | source)
XLA Modules:
  0.0 1368.1 jit_solution(14134024486519536127)
XLA Ops:
  80.6 28.7 %collective-permute-done.29 = bf16[128,2048]{1,0:T(8,128)(2,1)S(1)} collective-permute-done((bf16[128,2048]{1,0:T(8,128)(2,1)S(1)}, bf16[128,2048]{1,0:T(8,128)(2,1)S(1)}, u32[]{:S(2)}, u32[]{:S(2)}) %collective-permute-start.29) | collective-permute-done | bytes 524320 | tf_op jit(solution)/shard_map/ppermute | solution.py:22
  181.0 17.7 %collective-permute-done.33 = bf16[128,2048]{1,0:T(8,128)(2,1)S(1)} collective-permute-done((bf16[128,2048]{1,0:T(8,128)(2,1)S(1)}, bf16[128,2048]{1,0:T(8,128)(2,1)S(1)}, u32[]{:S(2)}, u32[]{:S(2)}) %collective-permute-start.33) | collective-permute-done | bytes 524320 | tf_op jit(solution)/shard_map/ppermute | solution.py:22
  240.5 20.2 %collective-permute-done.37 = bf16[256,2048]{0,1:T(8,128)(2,1)S(1)} collective-permute-done((bf16[256,2048]{0,1:T(8,128)(2,1)S(1)}, bf16[256,2048]{0,1:T(8,128)(2,1)S(1)}, u32[]{:S(2)}, u32[]{:S(2)}) %collective-permute-start.37) | collective-permute-done | bytes 1048608 | tf_op jit(solution)/shard_map/ppermute | solution.py:22
  279.5 20.7 %collective-permute-done.34 = bf16[256,2048]{1,0:T(8,128)(2,1)S(1)} collective-permute-done((bf16[256,2048]{1,0:T(8,128)(2,1)S(1)}, bf16[256,2048]{1,0:T(8,128)(2,1)S(1)}, u32[]{:S(2)}, u32[]{:S(2)}) %collective-permute-start.34) | collective-permute-done | bytes 1048608 | tf_op jit(solution)/shard_map/ppermute | solution.py:22
  300.4 22.2 %collective-permute-done.27 = bf16[256,2048]{1,0:T(8,128)(2,1)S(1)} collective-permute-done((bf16[256,2048]{1,0:T(8,128)(2,1)S(1)}, bf16[256,2048]{1,0:T(8,128)(2,1)S(1)}, u32[]{:S(2)}, u32[]{:S(2)}) %collective-permute-start.27) | collective-permute-done | bytes 1048608 | tf_op jit(solution)/shard_map/ppermute | solution.py:22
  324.1 18.7 %collective-permute-done.41 = bf16[256,2048]{0,1:T(8,128)(2,1)S(1)} collective-permute-done((bf16[256,2048]{0,1:T(8,128)(2,1)S(1)}, bf16[256,2048]{0,1:T(8,128)(2,1)S(1)}, u32[]{:S(2)}, u32[]{:S(2)}) %collective-permute-start.41) | collective-permute-done | bytes 1048608 | tf_op jit(solution)/shard_map/ppermute | solution.py:22
  342.8 16.6 %collective-permute-start.46 = (bf16[256,2048]{1,0:T(8,128)(2,1)S(1)}, bf16[256,2048]{1,0:T(8,128)(2,1)S(1)}, u32[]{:S(2)}, u32[]{:S(2)}) collective-permute-start(bf16[256,2048]{1,0:T(8,128)(2,1)S(1)} %fusion.101), channel_id=1, source_target_pairs={{0,1},{1,0},{2,3},{3,2},{4,5},{5,4},{6,7},{7,6},{8,9},{9,8},{10,11... | collective-permute-start | bytes 3145736 | tf_op jit(solution)/shard_map/ppermute | solution.py:22
  405.3 48.2 %collective-permute-done.47 = bf16[3,512,256]{2,1,0:T(8,128)(2,1)S(1)} collective-permute-done((bf16[3,512,256]{2,1,0:T(8,128)(2,1)S(1)}, bf16[3,512,256]{2,1,0:T(8,128)(2,1)S(1)}, u32[]{:S(2)}, u32[]{:S(2)}) %collective-permute-start.47) | collective-permute-done | bytes 786464 | tf_op jit(solution)/shard_map/ppermute | solution.py:169
  635.8 21.7 %collective-permute-done.57 = bf16[256,2048]{1,0:T(8,128)(2,1)S(1)} collective-permute-done((bf16[256,2048]{1,0:T(8,128)(2,1)S(1)}, bf16[256,2048]{1,0:T(8,128)(2,1)S(1)}, u32[]{:S(2)}, u32[]{:S(2)}) %collective-permute-start.57) | collective-permute-done | bytes 1048608 | tf_op jit(solution)/shard_map/ppermute | solution.py:22
  667.6 32.2 %collective-permute-done.52 = bf16[256,2048]{1,0:T(8,128)(2,1)S(1)} collective-permute-done((bf16[256,2048]{1,0:T(8,128)(2,1)S(1)}, bf16[256,2048]{1,0:T(8,128)(2,1)S(1)}, u32[]{:S(2)}, u32[]{:S(2)}) %collective-permute-start.52) | collective-permute-done | bytes 1048608 | tf_op jit(solution)/shard_map/ppermute | solution.py:22
  814.8 20.4 %collective-permute-done.67 = bf16[256,2048]{1,0:T(8,128)(2,1)S(1)} collective-permute-done((bf16[256,2048]{1,0:T(8,128)(2,1)S(1)}, bf16[256,2048]{1,0:T(8,128)(2,1)S(1)}, u32[]{:S(2)}, u32[]{:S(2)}) %collective-permute-start.67) | collective-permute-done | bytes 1048608 | tf_op jit(solution)/shard_map/ppermute | solution.py:22
  872.7 21.1 %shard_map.235 = bf16[3,8,128,256]{3,2,1,0:T(8,128)(2,1)S(1)} custom-call(s32[8]{0:T(128)S(1)} %copy-done.9, bf16[3,8,128,256]{3,2,1,0:T(8,128)(2,1)S(1)} %copy-done.3, bf16[8,128,256]{2,1,0:T(8,128)(2,1)S(1)} %maximum_bitcast_fusion.3.grad_ref, f32[1024,128]{1,0:T(8,128)S(1)} %copy-done.7, f32[1024,128]{1,0:T(8,128)S(1)} %copy-done.5), custom_call_target="tpu_custom_call" | custom-call | flops 5368709120 | bytes 3670016 | tf_op jit(solution)/shard_map/pallas_call | solution.py:312
  920.0 19.4 %collective-permute-done.62 = bf16[3,4,128,256]{3,2,1,0:T(8,128)(2,1)S(1)} collective-permute-done((bf16[3,4,128,256]{3,2,1,0:T(8,128)(2,1)S(1)}, bf16[3,4,128,256]{3,2,1,0:T(8,128)(2,1)S(1)}, u32[]{:S(2)}, u32[]{:S(2)}) %collective-permute-start.62) | collective-permute-done | bytes 786464 | tf_op jit(solution)/shard_map/ppermute | solution.py:182
  958.0 19.7 %collective-permute-done.91 = bf16[256,2048]{1,0:T(8,128)(2,1)} collective-permute-done((bf16[256,2048]{1,0:T(8,128)(2,1)}, bf16[256,2048]{1,0:T(8,128)(2,1)}, u32[]{:S(2)}, u32[]{:S(2)}) %collective-permute-start.91) | collective-permute-done | bytes 1048608 | tf_op jit(solution)/shard_map/ppermute | solution.py:22
  981.8 18.2 %collective-permute-done.94 = bf16[256,2048]{1,0:T(8,128)(2,1)S(1)} collective-permute-done((bf16[256,2048]{1,0:T(8,128)(2,1)}, bf16[256,2048]{1,0:T(8,128)(2,1)S(1)}, u32[]{:S(2)}, u32[]{:S(2)}) %collective-permute-start.94) | collective-permute-done | bytes 1048608 | tf_op jit(solution)/shard_map/ppermute | solution.py:22
  1003.5 19.0 %collective-permute-done.98 = bf16[256,2048]{1,0:T(8,128)(2,1)S(1)} collective-permute-done((bf16[256,2048]{1,0:T(8,128)(2,1)}, bf16[256,2048]{1,0:T(8,128)(2,1)S(1)}, u32[]{:S(2)}, u32[]{:S(2)}) %collective-permute-start.98) | collective-permute-done | bytes 1048608 | tf_op jit(solution)/shard_map/ppermute | solution.py:22
  1025.9 18.3 %collective-permute-done.101 = bf16[256,2048]{1,0:T(8,128)(2,1)S(1)} collective-permute-done((bf16[256,2048]{1,0:T(8,128)(2,1)}, bf16[256,2048]{1,0:T(8,128)(2,1)S(1)}, u32[]{:S(2)}, u32[]{:S(2)}) %collective-permute-start.101) | collective-permute-done | bytes 1048608 | tf_op jit(solution)/shard_map/ppermute | solution.py:22
  1053.1 28.1 %collective-permute-done.71 = bf16[1,512,256]{2,1,0:T(8,128)(2,1)S(1)} collective-permute-done((bf16[1,512,256]{2,1,0:T(8,128)(2,1)S(1)}, bf16[1,512,256]{2,1,0:T(8,128)(2,1)S(1)}, u32[]{:S(2)}, u32[]{:S(2)}) %collective-permute-start.71) | collective-permute-done | bytes 262176 | tf_op jit(solution)/shard_map/ppermute | solution.py:169
  1081.2 21.1 %shard_map.236 = bf16[3,8,128,256]{3,2,1,0:T(8,128)(2,1)S(1)} custom-call(s32[8]{0:T(128)S(1)} %copy-done.9, bf16[3,8,128,256]{3,2,1,0:T(8,128)(2,1)S(1)} %copy-done.1, bf16[8,128,256]{2,1,0:T(8,128)(2,1)S(1)} %maximum_bitcast_fusion.4.grad_ref, f32[1024,128]{1,0:T(8,128)S(1)} %copy-done.7, f32[1024,128]{1,0:T(8,128)S(1)} %copy-done.5), custom_call_target="tpu_custom_call" | custom-call | flops 5368709120 | bytes 3670016 | tf_op jit(solution)/shard_map/pallas_call | solution.py:312
  1111.5 29.3 %collective-permute-done.95 = bf16[128,2048]{1,0:T(8,128)(2,1)S(1)} collective-permute-done((bf16[128,2048]{1,0:T(8,128)(2,1)S(1)}, bf16[128,2048]{1,0:T(8,128)(2,1)S(1)}, u32[]{:S(2)}, u32[]{:S(2)}) %collective-permute-start.95) | collective-permute-done | bytes 524320 | tf_op jit(solution)/shard_map/ppermute | solution.py:22
  1141.0 28.0 %collective-permute-done.102 = bf16[128,2048]{1,0:T(8,128)(2,1)S(1)} collective-permute-done((bf16[128,2048]{1,0:T(8,128)(2,1)S(1)}, bf16[128,2048]{1,0:T(8,128)(2,1)S(1)}, u32[]{:S(2)}, u32[]{:S(2)}) %collective-permute-start.102) | collective-permute-done | bytes 524320 | tf_op jit(solution)/shard_map/ppermute | solution.py:22
  1185.9 27.9 %collective-permute-done.88 = bf16[128,512]{1,0:T(8,128)(2,1)S(1)} collective-permute-done((bf16[128,512]{1,0:T(8,128)(2,1)S(1)}, bf16[128,512]{1,0:T(8,128)(2,1)S(1)}, u32[]{:S(2)}, u32[]{:S(2)}) %collective-permute-start.88) | collective-permute-done | bytes 131104 | tf_op jit(solution)/shard_map/ppermute | solution.py:22
  1223.6 18.6 %maximum_maximum_fusion = bf16[1024,1536]{1,0:T(8,128)(2,1)S(1)} fusion(bf16[512,512]{1,0:T(8,128)(2,1)S(1)} %get-tuple-element.95, bf16[512,512]{1,0:T(8,128)(2,1)S(1)} %get-tuple-element.96, bf16[512,512]{1,0:T(8,128)(2,1)S(1)} %get-tuple-element.94, bf16[512,512]{1,0:T(8,128)(2,1)S(1)} %copy-done.45, bf16[512,512]{1,0:T(8,128)(2,1)S(1)} %copy-done.47, ...), kind=kLoop, calls=%fused_computation.22 | loop fusion | flops 18874368 | bytes 6291456 | tf_op jit(solution)/shard_map/concatenate | solution.py:412
  1337.2 16.5 %collective-permute-done.77 = bf16[128,1536]{1,0:T(8,128)(2,1)S(1)} collective-permute-done((bf16[128,1536]{1,0:T(8,128)(2,1)S(1)}, bf16[128,1536]{1,0:T(8,128)(2,1)S(1)}, u32[]{:S(2)}, u32[]{:S(2)}) %collective-permute-start.77) | collective-permute-done | bytes 393248 | tf_op jit(solution)/shard_map/ppermute | solution.py:22
  (752 shorter events, 812.1 us)
Async XLA Ops:
  24.4 112.0 %collective-permute-start.5 = (bf16[128,1536]{1,0:T(8,128)(2,1)}, bf16[128,1536]{1,0:T(8,128)(2,1)S(1)}, u32[]{:S(2)}, u32[]{:S(2)}) collective-permute-start(bf16[128,1536]{1,0:T(8,128)(2,1)} %pad_maximum_fusion.59), channel_id=1, source_target_pairs={{0,1},{1,0},{2,3},{3,2},{4,5},{5,4},{6,7},{7,6},{8,9},{9,8},{10,11... | collective-permute-start | bytes 1179656 | tf_op jit(solution)/shard_map/ppermute | solution.py:22
  65.8 79.6 %collective-permute-start.32 = (bf16[128,2048]{1,0:T(8,128)(2,1)}, bf16[128,2048]{1,0:T(8,128)(2,1)S(1)}, u32[]{:S(2)}, u32[]{:S(2)}) collective-permute-start(bf16[128,2048]{1,0:T(8,128)(2,1)} %get-tuple-element.140), channel_id=1, source_target_pairs={{0,1},{1,0},{2,3},{3,2},{4,5},{5,4},{6,7},{7,6},{8,9},{9,8},{10,11... | collective-permute-start | bytes 1572872 | tf_op jit(solution)/shard_map/ppermute | solution.py:22
  145.4 81.9 %collective-permute-start.3 = (bf16[256,1536]{1,0:T(8,128)(2,1)S(1)}, bf16[256,1536]{1,0:T(8,128)(2,1)S(1)}, u32[]{:S(2)}, u32[]{:S(2)}) collective-permute-start(bf16[256,1536]{1,0:T(8,128)(2,1)S(1)} %pad_maximum_fusion.40), channel_id=1, source_target_pairs={{0,16},{8,24},{16,0},{24,8},{1,17},{9,25},{17,1},{25,9},{2,18},{10... | collective-permute-start | bytes 2359304 | tf_op jit(solution)/shard_map/ppermute | solution.py:22
  230.4 69.7 %collective-permute-start.34 = (bf16[256,2048]{1,0:T(8,128)(2,1)S(1)}, bf16[256,2048]{1,0:T(8,128)(2,1)S(1)}, u32[]{:S(2)}, u32[]{:S(2)}) collective-permute-start(bf16[256,2048]{1,0:T(8,128)(2,1)S(1)} %pad_maximum_fusion.30), channel_id=1, source_target_pairs={{0,16},{8,24},{16,0},{24,8},{1,17},{9,25},{17,1},{25,9},{2,18},{10... | collective-permute-start | bytes 3145736 | tf_op jit(solution)/shard_map/ppermute | solution.py:22
  231.7 90.9 %collective-permute-start.27 = (bf16[256,2048]{1,0:T(8,128)(2,1)S(1)}, bf16[256,2048]{1,0:T(8,128)(2,1)S(1)}, u32[]{:S(2)}, u32[]{:S(2)}) collective-permute-start(bf16[256,2048]{1,0:T(8,128)(2,1)S(1)} %pad_maximum_fusion.28), channel_id=1, source_target_pairs={{0,16},{8,24},{16,0},{24,8},{1,17},{9,25},{17,1},{25,9},{2,18},{10... | collective-permute-start | bytes 3145736 | tf_op jit(solution)/shard_map/ppermute | solution.py:22
  238.3 122.6 %collective-permute-start.4 = (bf16[512,1536]{1,0:T(8,128)(2,1)S(1)}, bf16[512,1536]{1,0:T(8,128)(2,1)S(1)}, u32[]{:S(2)}, u32[]{:S(2)}) collective-permute-start(bf16[512,1536]{1,0:T(8,128)(2,1)S(1)} %pad_maximum_fusion.13), channel_id=1, source_target_pairs={{0,8},{8,0},{16,24},{24,16},{1,9},{9,1},{17,25},{25,17},{2,10},{10... | collective-permute-start | bytes 4718600 | tf_op jit(solution)/shard_map/ppermute | solution.py:22
  277.6 65.2 %collective-permute-start.41 = (bf16[256,2048]{0,1:T(8,128)(2,1)S(1)}, bf16[256,2048]{0,1:T(8,128)(2,1)S(1)}, u32[]{:S(2)}, u32[]{:S(2)}) collective-permute-start(bf16[256,2048]{0,1:T(8,128)(2,1)S(1)} %pad_maximum_fusion.32), channel_id=1, source_target_pairs={{0,16},{8,24},{16,0},{24,8},{1,17},{9,25},{17,1},{25,9},{2,18},{10... | collective-permute-start | bytes 3145736 | tf_op jit(solution)/shard_map/ppermute | solution.py:22
  277.8 279.3 %collective-permute-start.56 = (bf16[256,2048]{1,0:T(8,128)(2,1)}, bf16[256,2048]{1,0:T(8,128)(2,1)}, u32[]{:S(2)}, u32[]{:S(2)}) collective-permute-start(bf16[256,2048]{1,0:T(8,128)(2,1)} %pad_maximum_fusion.34), channel_id=1, source_target_pairs={{0,4},{4,0},{1,5},{5,1},{2,6},{6,2},{3,7},{7,3},{8,12},{12,8},{9,1... | collective-permute-start | bytes 3145736 | tf_op jit(solution)/shard_map/ppermute | solution.py:22
  300.1 94.1 %collective-permute-start.31 = (bf16[512,2048]{1,0:T(8,128)(2,1)S(1)}, bf16[512,2048]{1,0:T(8,128)(2,1)S(1)}, u32[]{:S(2)}, u32[]{:S(2)}) collective-permute-start(bf16[512,2048]{1,0:T(8,128)(2,1)S(1)} %pad_maximum_fusion.6), channel_id=1, source_target_pairs={{0,8},{8,0},{16,24},{24,16},{1,9},{9,1},{17,25},{25,17},{2,10},{10... | collective-permute-start | bytes 6291464 | tf_op jit(solution)/shard_map/ppermute | solution.py:22
  322.6 75.9 %collective-permute-start.24 = (bf16[512,2048]{1,0:T(8,128)(2,1)S(1)}, bf16[512,2048]{1,0:T(8,128)(2,1)S(1)}, u32[]{:S(2)}, u32[]{:S(2)}) collective-permute-start(bf16[512,2048]{1,0:T(8,128)(2,1)S(1)} %pad_maximum_fusion.4), channel_id=1, source_target_pairs={{0,8},{8,0},{16,24},{24,16},{1,9},{9,1},{17,25},{25,17},{2,10},{10... | collective-permute-start | bytes 6291464 | tf_op jit(solution)/shard_map/ppermute | solution.py:22
  378.0 189.3 %collective-permute-start.35 = (bf16[512,2048]{1,0:T(8,128)(2,1)S(1)}, bf16[512,2048]{1,0:T(8,128)(2,1)}, u32[]{:S(2)}, u32[]{:S(2)}) collective-permute-start(bf16[512,2048]{1,0:T(8,128)(2,1)S(1)} %pad_maximum_fusion.7), channel_id=1, source_target_pairs={{0,8},{8,0},{16,24},{24,16},{1,9},{9,1},{17,25},{25,17},{2,10},{10... | collective-permute-start | bytes 6291464 | tf_op jit(solution)/shard_map/ppermute | solution.py:22
  394.2 150.6 %collective-permute-start.42 = (bf16[512,2048]{0,1:T(8,128)(2,1)}, bf16[512,2048]{0,1:T(8,128)(2,1)S(1)}, u32[]{:S(2)}, u32[]{:S(2)}) collective-permute-start(bf16[512,2048]{0,1:T(8,128)(2,1)} %pad_maximum_fusion.9), channel_id=1, source_target_pairs={{0,8},{8,0},{16,24},{24,16},{1,9},{9,1},{17,25},{25,17},{2,10},{10... | collective-permute-start | bytes 6291464 | tf_op jit(solution)/shard_map/ppermute | solution.py:22
  400.5 75.5 %collective-permute-start.9 = (bf16[3,512,256]{2,1,0:T(8,128)(2,1)}, bf16[3,512,256]{2,1,0:T(8,128)(2,1)}, u32[]{:S(2)}, u32[]{:S(2)}) collective-permute-start(bf16[3,512,256]{2,1,0:T(8,128)(2,1)} %pad_maximum_fusion.42), channel_id=1, source_target_pairs={{0,2},{1,3},{2,0},{3,1},{4,6},{5,7},{6,4},{7,5},{8,10},{9,11},{10,... | collective-permute-start | bytes 2359304 | tf_op jit(solution)/shard_map/ppermute | solution.py:169
  632.6 71.5 %collective-permute-start.66 = (bf16[256,2048]{1,0:T(8,128)(2,1)S(1)}, bf16[256,2048]{1,0:T(8,128)(2,1)S(1)}, u32[]{:S(2)}, u32[]{:S(2)}) collective-permute-start(bf16[256,2048]{1,0:T(8,128)(2,1)S(1)} %fusion.97), channel_id=1, source_target_pairs={{0,1},{1,0},{2,3},{3,2},{4,5},{5,4},{6,7},{7,6},{8,9},{9,8},{10,11... | collective-permute-start | bytes 3145736 | tf_op jit(solution)/shard_map/ppermute | solution.py:22
  919.2 80.8 %collective-permute-start.94 = (bf16[256,2048]{1,0:T(8,128)(2,1)}, bf16[256,2048]{1,0:T(8,128)(2,1)S(1)}, u32[]{:S(2)}, u32[]{:S(2)}) collective-permute-start(bf16[256,2048]{1,0:T(8,128)(2,1)} %slice.843), channel_id=1, source_target_pairs={{0,16},{8,24},{16,0},{24,8},{1,17},{9,25},{17,1},{25,9},{2,18},{10... | collective-permute-start | bytes 3145736 | tf_op jit(solution)/shard_map/ppermute | solution.py:22
  939.4 83.0 %collective-permute-start.98 = (bf16[256,2048]{1,0:T(8,128)(2,1)}, bf16[256,2048]{1,0:T(8,128)(2,1)S(1)}, u32[]{:S(2)}, u32[]{:S(2)}) collective-permute-start(bf16[256,2048]{1,0:T(8,128)(2,1)} %slice.847), channel_id=1, source_target_pairs={{0,16},{8,24},{16,0},{24,8},{1,17},{9,25},{17,1},{25,9},{2,18},{10... | collective-permute-start | bytes 3145736 | tf_op jit(solution)/shard_map/ppermute | solution.py:22
  950.4 93.8 %collective-permute-start.101 = (bf16[256,2048]{1,0:T(8,128)(2,1)}, bf16[256,2048]{1,0:T(8,128)(2,1)S(1)}, u32[]{:S(2)}, u32[]{:S(2)}) collective-permute-start(bf16[256,2048]{1,0:T(8,128)(2,1)} %slice.851), channel_id=1, source_target_pairs={{0,16},{8,24},{16,0},{24,8},{1,17},{9,25},{17,1},{25,9},{2,18},{10... | collective-permute-start | bytes 3145736 | tf_op jit(solution)/shard_map/ppermute | solution.py:22
  955.0 92.3 %collective-permute-start.70 = (bf16[256,2048]{1,0:T(8,128)(2,1)S(1)}, bf16[256,2048]{1,0:T(8,128)(2,1)S(1)}, u32[]{:S(2)}, u32[]{:S(2)}) collective-permute-start(bf16[256,2048]{1,0:T(8,128)(2,1)S(1)} %fusion.96), channel_id=1, source_target_pairs={{0,1},{1,0},{2,3},{3,2},{4,5},{5,4},{6,7},{7,6},{8,9},{9,8},{10,11... | collective-permute-start | bytes 3145736 | tf_op jit(solution)/shard_map/ppermute | solution.py:22
  977.6 192.9 %collective-permute-start.63 = (bf16[256,2048]{1,0:T(8,128)(2,1)}, bf16[256,2048]{1,0:T(8,128)(2,1)S(1)}, u32[]{:S(2)}, u32[]{:S(2)}) collective-permute-start(bf16[256,2048]{1,0:T(8,128)(2,1)} %fusion.98), channel_id=1, source_target_pairs={{0,1},{1,0},{2,3},{3,2},{4,5},{5,4},{6,7},{7,6},{8,9},{9,8},{10,11... | collective-permute-start | bytes 3145736 | tf_op jit(solution)/shard_map/ppermute | solution.py:22
  1000.0 245.3 %collective-permute-start.107 = (bf16[128,2048]{1,0:T(8,128)(2,1)}, bf16[128,2048]{1,0:T(8,128)(2,1)}, u32[]{:S(2)}, u32[]{:S(2)}) collective-permute-start(bf16[128,2048]{1,0:T(8,128)(2,1)} %slice.859), channel_id=1, source_target_pairs={{0,2},{1,3},{2,0},{3,1},{4,6},{5,7},{6,4},{7,5},{8,10},{9,11},{10,... | collective-permute-start | bytes 1572872 | tf_op jit(solution)/shard_map/ppermute | solution.py:22
  1022.5 80.1 %collective-permute-start.110 = (bf16[128,2048]{1,0:T(8,128)(2,1)}, bf16[128,2048]{1,0:T(8,128)(2,1)}, u32[]{:S(2)}, u32[]{:S(2)}) collective-permute-start(bf16[128,2048]{1,0:T(8,128)(2,1)} %slice.865), channel_id=1, source_target_pairs={{0,2},{1,3},{2,0},{3,1},{4,6},{5,7},{6,4},{7,5},{8,10},{9,11},{10,... | collective-permute-start | bytes 1572872 | tf_op jit(solution)/shard_map/ppermute | solution.py:22
  1044.2 207.2 %collective-permute-start.92 = (bf16[128,2048]{1,0:T(8,128)(2,1)}, bf16[128,2048]{1,0:T(8,128)(2,1)}, u32[]{:S(2)}, u32[]{:S(2)}) collective-permute-start(bf16[128,2048]{1,0:T(8,128)(2,1)} %slice.839), channel_id=1, source_target_pairs={{0,2},{1,3},{2,0},{3,1},{4,6},{5,7},{6,4},{7,5},{8,10},{9,11},{10,... | collective-permute-start | bytes 1572872 | tf_op jit(solution)/shard_map/ppermute | solution.py:22
  1140.8 73.0 %collective-permute-start.72 = (bf16[3,4,128,256]{3,2,1,0:T(8,128)(2,1)S(1)}, bf16[3,4,128,256]{3,2,1,0:T(8,128)(2,1)S(1)}, u32[]{:S(2)}, u32[]{:S(2)}) collective-permute-start(bf16[3,4,128,256]{3,2,1,0:T(8,128)(2,1)S(1)} %get-tuple-element.99), channel_id=1, source_target_pairs={{0,2},{1,3},{2,0},{3,1},{4,6},{5,7},{6,4},{7,5},{8,10},{9,11},{10,... | collective-permute-start | bytes 2359304 | tf_op jit(solution)/shard_map/ppermute | solution.py:182
  1182.7 72.7 %collective-permute-start.99 = (bf16[128,2048]{1,0:T(8,128)(2,1)S(1)}, bf16[128,2048]{1,0:T(8,128)(2,1)S(1)}, u32[]{:S(2)}, u32[]{:S(2)}) collective-permute-start(bf16[128,2048]{1,0:T(8,128)(2,1)S(1)} %copy-done.65), channel_id=1, source_target_pairs={{0,2},{1,3},{2,0},{3,1},{4,6},{5,7},{6,4},{7,5},{8,10},{9,11},{10,... | collective-permute-start | bytes 1572872 | tf_op jit(solution)/shard_map/ppermute | solution.py:22
  (207 other events, 5766.6 us)

commit v2 on v1

--- a/solution.py
+++ b/solution.py
@@ -15,6 +15,7 @@
 F32 = jnp.float32
 BF16 = jnp.bfloat16
 LANES = 128
+MESH = pl.DeviceIdType.MESH
 
 
 def swap(value, axis, bit):
@@ -295,7 +296,7 @@
     _, blocks, tokens, width = qkv.shape
     length = blocks * tokens
     lanes = min(LANES, width)
-    rows_at_once = min(256, length)
+    rows_at_once = min(256, length) if length <= 2048 else LANES
     back = grad is not None
 
     def fixed(j, order_ref):
@@ -328,6 +329,420 @@
     )(order, qkv, *([grad] if back else []), *tables)
 
 
+def greet():
+    masks = [("head", 1)] + [("dp", bit) for bit in bits_of(lax.axis_size("dp"))]
+    masks += [("blk", 1)] + [("blk", 2 * r) for r in range(1, head_groups())]
+    barrier = pltpu.get_barrier_semaphore()
+    for axis, mask in masks:
+        pl.semaphore_signal(barrier, inc=1, device_id={axis: flipped(axis, mask)}, device_id_type=MESH)
+    pl.semaphore_wait(barrier, len(masks))
+
+
+def flipped(axis, mask):
+    place, other = lax.axis_index(axis), 0
+    for bit in bits_of(lax.axis_size(axis)):
+        digit = (place // bit) % 2
+        other = other + bit * ((1 - digit) if mask & bit else digit)
+    return other
+
+
+class Copies:
+    def __init__(self, send, recv, local):
+        self.send, self.recv, self.local = send, recv, local
+        self.remote_count = self.local_count = 0
+        self.sent = []
+
+    def remote(self, source, target, axis, mask):
+        k = self.remote_count
+        self.remote_count += 1
+        copy = pltpu.make_async_remote_copy(
+            src_ref=source, dst_ref=target, send_sem=self.send.at[k], recv_sem=self.recv.at[k],
+            device_id={axis: flipped(axis, mask)}, device_id_type=MESH,
+        )
+        copy.start()
+        self.sent.append(copy)
+        return copy
+
+    def inside(self, source, target):
+        copy = pltpu.make_async_copy(source, target, self.local.at[self.local_count])
+        self.local_count += 1
+        copy.start()
+        return copy
+
+    def finish(self):
+        for copy in self.sent:
+            copy.wait_send()
+
+
+def halves_turned(rows):
+    half = rows.shape[-1] // 2
+    return jnp.concatenate([rows[:, half:], rows[:, :half]], 1)
+
+
+class WeightGather:
+    def __init__(self, copies, own, other, full):
+        self.copies, self.full, self.stage = copies, full, 0
+        self.mine = copies.inside(own, full.at[0, 0])
+        self.copy = copies.remote(other, full.at[1, 0], "blk", 1)
+
+    def advance(self):
+        if self.mine is not None:
+            self.mine.wait()
+            self.mine = None
+        self.copy.wait_recv()
+        stages = replica_stages()
+        if self.stage < len(stages):
+            held = 1 << self.stage
+            self.copy = self.copies.remote(
+                self.full.at[:, 0:held], self.full.at[:, held : 2 * held], *stages[self.stage]
+            )
+        self.stage += 1
+
+
+class TokenGather:
+    def __init__(self, copies, rows, turned_rows, m):
+        self.copies, self.rows, self.turned_rows, self.m = copies, rows, turned_rows, m
+        self.head_first = m % 2 == 1
+        if self.head_first:
+            self.copy = copies.remote(rows.at[m, 0, 0], rows.at[m, 1, 0], "head", 1)
+        else:
+            turned_rows[m, 0] = halves_turned(rows[m, 0, 0])
+            self.copy = copies.remote(turned_rows.at[m, 0], rows.at[m, 0, 1], "blk", 1)
+
+    def second(self):
+        m, rows, turned_rows = self.m, self.rows, self.turned_rows
+        self.copy.wait_recv()
+        if self.head_first:
+            turned_rows[m, 0] = halves_turned(rows[m, 0, 0])
+            turned_rows[m, 1] = halves_turned(rows[m, 1, 0])
+            self.copy = self.copies.remote(turned_rows.at[m], rows.at[m, :, 1], "blk", 1)
+        else:
+            self.copy = self.copies.remote(rows.at[m, 0], rows.at[m, 1], "head", 1)
+
+    def end(self):
+        self.copy.wait_recv()
+
+
+class TokenScatter:
+    def __init__(self, copies, partial, leaving, came, passing, last, total, m):
+        self.copies, self.partial, self.came, self.passing = copies, partial, came, passing
+        self.last, self.total, self.m = last, total, m
+        self.head_first = m % 2 == 0
+        if self.head_first:
+            self.copy = copies.remote(partial.at[m, 1], came.at[m], "head", 1)
+        else:
+            leaving[m, 0] = halves_turned(partial[m, 0, 1])
+            leaving[m, 1] = halves_turned(partial[m, 1, 1])
+            self.copy = copies.remote(leaving.at[m], came.at[m], "blk", 1)
+
+    def second(self):
+        m, partial = self.m, self.partial
+        self.copy.wait_recv()
+        kept = partial[m, 0, 1] if self.head_first else partial[m, 1, 0]
+        theirs = (kept.astype(F32) + self.came[m, 1].astype(F32)).astype(BF16)
+        if self.head_first:
+            self.passing[m] = halves_turned(theirs)
+            self.copy = self.copies.remote(self.passing.at[m], self.last.at[m], "blk", 1)
+        else:
+            self.passing[m] = theirs
+            self.copy = self.copies.remote(self.passing.at[m], self.last.at[m], "head", 1)
+        self.total[m] += partial[m, 0, 0].astype(F32) + self.came[m, 0].astype(F32)
+
+    def end(self):
+        self.copy.wait_recv()
+        self.total[self.m] += self.last[self.m].astype(F32)
+
+
+def place_of(block):
+    n_blk = lax.axis_size("blk")
+    head, blk = block // n_blk, block % n_blk
+    near = (blk + lax.axis_index("blk")) % 2
+    return blk // 2, ((head + lax.axis_index("head")) % 2) * 2 + near
+
+
+def load_heads(seq, m, lane, cosine_ref, sine_ref, held):
+    tokens = seq.shape[-2]
+    lanes = held[0].shape[1]
+    blocks = held[0].shape[0] // tokens
+
+    def one(block, carry):
+        upper, group = place_of(block)
+        rows = pl.ds(pl.multiple_of(block * tokens, tokens), tokens)
+        for part in range(3):
+            value = seq[m, upper, part, group, :, pl.ds(lane, lanes)]
+            if part < 2:
+                value = turned(value.astype(F32), cosine_ref[rows, :], sine_ref[rows, :]).astype(BF16)
+            held[part][rows, :] = value
+        return carry
+
+    lax.fori_loop(0, blocks, one, 0)
+
+
+def attend(seq, out, m, cosine_ref, sine_ref, held):
+    tokens, width = seq.shape[-2:]
+    q_s, k_s, v_s = held
+    length, lanes = q_s.shape
+    rows_at_once = min(256, length) if length <= 2048 else LANES
+
+    def rows_of(first, last, lane):
+        results = []
+        for start in range(0, lanes, HD):
+            head = slice(start, start + HD)
+            weights, inverse = softmax_rows(q_s[pl.ds(first, rows_at_once), head], k_s[:last, head], first)
+            results.append(matmul(weights.astype(BF16), v_s[:last, head]) * inverse)
+        result = jnp.concatenate(results, 1).astype(BF16)
+        for offset in range(0, rows_at_once, tokens):
+            upper, group = place_of((first + offset) // tokens)
+            out[m, upper, group, :, pl.ds(lane, lanes)] = result[offset : offset + tokens]
+
+    def heads(lane):
+        load_heads(seq, m, lane, cosine_ref, sine_ref, held)
+        over_rows(length, rows_at_once, lambda first, last: rows_of(first, last, lane))
+
+    over_lanes(width, lanes, heads)
+
+
+def over_rows(length, rows_at_once, body):
+    if length // rows_at_once <= 8:
+        for first in range(0, length, rows_at_once):
+            body(first, first + rows_at_once)
+        return
+
+    def one(j, carry):
+        body(pl.multiple_of(j * rows_at_once, rows_at_once), length)
+        return carry
+
+    lax.fori_loop(0, length // rows_at_once, one, 0)
+
+
+def over_lanes(width, lanes, body):
+    if width == lanes:
+        body(0)
+        return
+
+    def one(j, carry):
+        body(pl.multiple_of(j * lanes, lanes))
+        return carry
+
+    lax.fori_loop(0, width // lanes, one, 0)
+
+
+def store_normed(values, target, at):
+    scale = lax.rsqrt(jnp.mean(values * values, -1, keepdims=True) + EPSILON)
+    target[at] = (values * scale).astype(BF16)
+
+
+def front_kernel(sizes, *refs):
+    micros, groups, n_att, n_mlp = sizes
+    x_ref, att_in, mlp_in, cosine_ref, sine_ref = refs[:5]
+    refs = refs[5:]
+    w_att, refs = refs[:n_att], refs[n_att:]
+    w_mlp, refs = refs[:n_mlp], refs[n_mlp:]
+    xg_out, seq_out, attended_out, mixed_out, x2_out = refs[:5]
+    (xg, x2, turned_rows, turned_more, w_in, w_out, made, seq, heads_out, attended, partial,
+     leaving, came, passing, last, mixed, q_s, k_s, v_s, send, recv, local) = refs[5:]
+    held = (q_s, k_s, v_s)
+    each = range(micros)
+    near = lax.axis_index("blk") % 2
+    upper = lax.axis_index("blk") // 2
+    width = x_ref.shape[-1]
+    tokens = x_ref.shape[-2]
+    heads_width = w_in.shape[-1]
+    here = heads_width // groups
+    copies = Copies(send, recv, local)
+
+    greet()
+    att = [WeightGather(copies, att_in.at[i, near], att_in.at[i, 1 - near], w_att[i]) for i in range(n_att)]
+    gathers = []
+    for m in each:
+        store_normed(x_ref[m].astype(F32), xg, (m, 0, 0))
+        gathers.append(TokenGather(copies, xg, turned_rows, m))
+    for chunk in att:
+        chunk.advance()
+    per_weight = n_mlp // 3
+    order = [(w, j) for j in range(per_weight) for w in range(2)] + [(2, j) for j in range(per_weight)]
+    mlp = [
+        WeightGather(
+            copies, mlp_in.at[w, near * per_weight + j], mlp_in.at[w, (1 - near) * per_weight + j], full
+        )
+        for (w, j), full in zip(order, w_mlp)
+    ]
+    for gather in gathers:
+        gather.second()
+    stages = len(replica_stages())
+    steps = [[] for _ in range(stages + n_att)]
+    for s in range(stages):
+        for i in range(n_att):
+            steps[s + i].append(att[i])
+    for step in steps:
+        for chunk in step:
+            if chunk.stage <= stages:
+                chunk.advance()
+
+    background = [[] for _ in range(stages + n_mlp + 1)]
+    for i, chunk in enumerate(mlp):
+        for s in range(stages + 1):
+            background[i + s].append(chunk)
+    done = [0]
+
+    def pump(count):
+        for step in background[done[0] : done[0] + count]:
+            for chunk in reversed(step):
+                chunk.advance()
+        done[0] += count
+
+    for gather in gathers:
+        gather.end()
+    writes = [copies.inside(xg, xg_out)]
+    loads = [copies.inside(w_att[i], w_in.at[i]) for i in range(3)] + [copies.inside(w_att[3], w_out)]
+    crossing = [[] for _ in each]
+    mine = [[] for _ in each]
+    tile = min(256, heads_width)
+    for i in range(3):
+        loads[i].wait()
+        for m in each:
+            rows = xg[m].reshape(4 * tokens, width)
+            for start in range(0, heads_width, tile):
+                columns = w_in[i, :, :, :, start : start + tile].reshape(width, tile)
+                product = matmul(rows, columns).astype(BF16)
+                for lane in range(0, tile, min(here, tile)):
+                    place = (start + lane) // here
+                    inner = (start + lane) % here
+                    for group in range(4):
+                        made[m, place, i, group, :, inner : inner + min(here, tile)] = product[
+                            group * tokens : (group + 1) * tokens, lane : lane + min(here, tile)
+                        ]
+            mine[m].append(copies.inside(made.at[m, upper, i], seq.at[m, upper, i]))
+            for r in range(1, groups):
+                crossing[m].append(
+                    copies.remote(made.at[m, flipped("blk", 2 * r) // 2, i], seq.at[m, upper, i], "blk", 2 * r)
+                )
+    returning = []
+    for m in each:
+        pump(1)
+        for copy in mine[m]:
+            copy.wait()
+        for copy in crossing[m]:
+            copy.wait_recv()
+        attend(seq, heads_out, m, cosine_ref, sine_ref, held)
+        back = [copies.inside(heads_out.at[m, upper], attended.at[m, upper])]
+        for r in range(1, groups):
+            back.append(
+                copies.remote(heads_out.at[m, flipped("blk", 2 * r) // 2], attended.at[m, upper], "blk", 2 * r)
+            )
+        returning.append(back)
+    writes.append(copies.inside(seq, seq_out))
+    pump(1)
+    loads[3].wait()
+    scatters = []
+    rows_tile = min(256, width)
+    for m in each:
+        returning[m][0].wait()
+        for copy in returning[m][1:]:
+            copy.wait_recv()
+        rows = jnp.concatenate([attended[m, g].reshape(4 * tokens, here) for g in range(groups)], 1)
+        _, replicas, piece, _ = w_out.shape
+        for start in range(0, width, rows_tile):
+            half, first = start // (replicas * piece), start // piece % replicas
+            part = w_out[half, first : first + rows_tile // piece].reshape(rows_tile, heads_width)
+            product = matmul_nt(rows, part).astype(BF16)
+            for group in range(4):
+                partial[m, group // 2, group % 2, :, start : start + rows_tile] = product[
+                    group * tokens : (group + 1) * tokens
+                ]
+        mixed[m] = x_ref[m].astype(F32)
+        scatters.append(TokenScatter(copies, partial, leaving, came, passing, last, mixed, m))
+    writes.append(copies.inside(attended, attended_out))
+    pump(1)
+    for scatter in scatters:
+        scatter.second()
+    pump(1)
+    gathers = []
+    for m in each:
+        scatters[m].end()
+        store_normed(mixed[m], x2, (m, 0, 0))
+        gathers.append(TokenGather(copies, x2, turned_more, m))
+    writes.append(copies.inside(mixed, mixed_out))
+    pump(1)
+    for gather in gathers:
+        gather.second()
+    pump(1)
+    for gather in gathers:
+        gather.end()
+    writes.append(copies.inside(x2, x2_out))
+    pump(len(background) - done[0])
+    for copy in writes:
+        copy.wait()
+    copies.finish()
+
+
+def front(x_rows, att_in, mlp_in, tables):
+    micros, tokens, width = x_rows.shape
+    n_att, _, piece, heads_width = att_in.shape
+    n_weights, parts, _, columns = mlp_in.shape
+    n_mlp = n_weights * parts // 2
+    groups = head_groups()
+    here = heads_width // groups
+    replicas = width // piece // 2
+    length, lanes = tables[0].shape
+    any_space = pl.BlockSpec(memory_space=pl.ANY)
+    in_vmem = pl.BlockSpec(memory_space=pltpu.VMEM)
+
+    def bf16(*shape):
+        return jax.ShapeDtypeStruct(shape, BF16)
+
+    token_rows = (micros, 2, 2, tokens, width)
+    outs = [bf16(2, replicas, piece, heads_width)] * n_att + [bf16(2, replicas, piece, columns)] * n_mlp
+    outs += [
+        bf16(*token_rows),
+        bf16(micros, groups, 3, 4, tokens, here),
+        bf16(micros, groups, 4, tokens, here),
+        jax.ShapeDtypeStruct((micros, tokens, width), F32),
+        bf16(*token_rows),
+    ]
+
+    def room(*shape):
+        return pltpu.VMEM(shape, BF16)
+
+    scratch = [
+        room(*token_rows),
+        room(*token_rows),
+        room(micros, 2, tokens, width),
+        room(micros, 2, tokens, width),
+        room(3, 2, replicas, piece, heads_width),
+        room(2, replicas, piece, heads_width),
+        room(micros, groups, 3, 4, tokens, here),
+        room(micros, groups, 3, 4, tokens, here),
+        room(micros, groups, 4, tokens, here),
+        room(micros, groups, 4, tokens, here),
+        room(*token_rows),
+        room(micros, 2, tokens, width),
+        room(micros, 2, tokens, width),
+        room(micros, tokens, width),
+        room(micros, tokens, width),
+        pltpu.VMEM((micros, tokens, width), F32),
+        room(length, lanes),
+        room(length, lanes),
+        room(length, lanes),
+        pltpu.SemaphoreType.DMA((192,)),
+        pltpu.SemaphoreType.DMA((192,)),
+        pltpu.SemaphoreType.DMA((64,)),
+    ]
+    results = pl.pallas_call(
+        functools.partial(front_kernel, (micros, groups, n_att, n_mlp)),
+        out_shape=outs,
+        in_specs=[in_vmem, any_space, any_space, in_vmem, in_vmem],
+        out_specs=[any_space] * len(outs),
+        scratch_shapes=scratch,
+        compiler_params=pltpu.CompilerParams(
+            collective_id=0, has_side_effects=True, vmem_limit_bytes=60 * 1024 * 1024
+        ),
+    )(x_rows, att_in, mlp_in, *tables)
+    w_att, results = results[:n_att], results[n_att:]
+    w_mlp, results = results[:n_mlp], results[n_mlp:]
+    return [w.reshape(width, -1) for w in w_att], [w.reshape(width, -1) for w in w_mlp], results
+
+
 def scale_of(values):
     return lax.rsqrt(jnp.mean(values * values, -1, keepdims=True) + EPSILON)
 
@@ -364,69 +779,79 @@
     def scaled(weight, gain):
         return (weight.astype(F32) * gain).astype(BF16)
 
-    attention_parts = [own_and_other(scaled(w, gain_one)) for w in (query_weight, key_weight, value_weight)]
-    qkv_full = gather_weight(*(jnp.concatenate(side, 1) for side in zip(*attention_parts)))
-    output_full = gather_weight(*own_and_other(output_weight.T))
-    gate_full = gather_weight(*own_and_other(scaled(gate_weight, gain_two)))
-    up_full = gather_weight(*own_and_other(scaled(up_weight, gain_two)))
-    down_full = gather_weight(*own_and_other(down_weight.T))
-
+    def joined(parts):
+        return jnp.concatenate(parts, 0)
+
+    def columns_of(weight, parts):
+        rows, columns = weight.shape
+        return weight.reshape(rows, parts, columns // parts).swapaxes(0, 1)
+
+    att_in = jnp.stack(
+        [columns_of(scaled(w, gain_one), 2) for w in (query_weight, key_weight, value_weight)]
+        + [columns_of(output_weight.T, 2)]
+    )
+    mlp_in = jnp.stack(
+        [columns_of(scaled(w, gain_two), 4) for w in (gate_weight, up_weight)] + [columns_of(down_weight.T, 4)]
+    )
     inputs_low = reorder(block_input.reshape(micros * tokens, width), to_own).reshape(micros, tokens, width)
+    w_att, w_mlp, held = front(inputs_low, att_in, mlp_in, tables)
+    normed_one_all, sequences, attended, mixed, normed_two_all = held
+    upper = lax.axis_index("blk") // 2
+    sequences = [lax.dynamic_index_in_dim(sequences, upper ^ r, 1, keepdims=False) for r in range(head_groups())]
+    sequences = jnp.concatenate(sequences, 2)
+    attended = jnp.concatenate([attended[:, g] for g in range(head_groups())], -1)
+    attended_all = attended.reshape(micros * 4 * tokens, -1)
+    normed_one_all = normed_one_all.reshape(-1, width)
+    normed_two_all = normed_two_all.reshape(-1, width)
+    gate_parts, up_parts, down_parts = w_mlp[0:4:2], w_mlp[1:4:2], w_mlp[4:]
+
     grad_low = reorder(grad_output.reshape(micros * tokens, width), to_own).reshape(micros, tokens, width)
     inputs = [inputs_low[m].astype(F32) for m in each]
     scale_one = [scale_of(inputs[m]) for m in each]
-    normed_one = [gather_tokens((inputs[m] * scale_one[m]).astype(BF16), head_first[m]) for m in each]
-
-    sequences = []
-    for m in each:
-        qkv = matmul(normed_one[m], qkv_full).astype(BF16)
-        parts = [qkv[:, i * heads_width : (i + 1) * heads_width] for i in range(3)]
-        sequences.append(to_sequences(parts))
-    attended = [from_sequences(attention_call(order, sequences[m], tables)[None])[0] for m in each]
-    mixed = [
-        inputs[m] + scatter_tokens(matmul_nt(attended[m], output_full), head_first[m]) for m in each
-    ]
     scale_two = [scale_of(mixed[m]) for m in each]
-    normed_two = [gather_tokens((mixed[m] * scale_two[m]).astype(BF16), head_first[m]) for m in each]
-    grad_rows = [gather_tokens(grad_low[m], head_first[m]) for m in each]
-
-    hidden, grad_gate, grad_up, grad_mixed, outputs = [], [], [], [], []
-    for m in each:
-        gate = matmul(normed_two[m], gate_full)
-        up = matmul(normed_two[m], up_full)
+    grad_rows_all = joined([gather_tokens(grad_low[m], head_first[m]) for m in each])
+
+    hidden, grad_gate, grad_up = [], [], []
+    grad_normed = produced = 0.0
+    for gate_full, up_full, down_full in zip(gate_parts, up_parts, down_parts):
+        gate = matmul(normed_two_all, gate_full)
+        up = matmul(normed_two_all, up_full)
         sigmoid = jax.nn.sigmoid(gate)
         activated = gate * sigmoid
         hidden.append((activated * up).astype(BF16))
-        grad_hidden = matmul(grad_rows[m], down_full)
+        grad_hidden = matmul(grad_rows_all, down_full)
         grad_gate.append((grad_hidden * up * sigmoid * (1.0 + gate * (1.0 - sigmoid))).astype(BF16))
         grad_up.append((grad_hidden * activated).astype(BF16))
-        grad_normed = matmul_nt(grad_gate[m], gate_full) + matmul_nt(grad_up[m], up_full)
-        grad_normed = scatter_tokens(grad_normed, head_first[m])
-        grad_mixed.append(grad_low[m].astype(F32) + norm_back(grad_normed, mixed[m], scale_two[m]))
+        grad_normed += matmul_nt(grad_gate[-1], gate_full) + matmul_nt(grad_up[-1], up_full)
+        produced += matmul_nt(hidden[-1], down_full)
+
+    def split(rows):
+        size = rows.shape[0] // micros
+        return [rows[m * size : (m + 1) * size] for m in each]
+
+    grad_normed = split(grad_normed)
+    grad_mixed = []
     for m in each:
-        outputs.append(
-            (mixed[m] + scatter_tokens(matmul_nt(hidden[m], down_full), head_first[m])).astype(BF16)
-        )
-
-    def joined(parts):
-        return jnp.concatenate(parts, 0)
-
-    normed_two_all = joined(normed_two)
-    gate_grad = scatter_weight_grad(normed_two_all, joined(grad_gate))
-    up_grad = scatter_weight_grad(normed_two_all, joined(grad_up))
-    down_grad = scatter_weight_grad(joined(grad_rows), joined(hidden))
+        back = norm_back(scatter_tokens(grad_normed[m], head_first[m]), mixed[m], scale_two[m])
+        grad_mixed.append(grad_low[m].astype(F32) + back)
+    produced = split(produced)
+    outputs = [(mixed[m] + scatter_tokens(produced[m], head_first[m])).astype(BF16) for m in each]
+
+    gate_grad = scatter_weight_grad(normed_two_all, jnp.concatenate(grad_gate, 1))
+    up_grad = scatter_weight_grad(normed_two_all, jnp.concatenate(grad_up, 1))
+    down_grad = scatter_weight_grad(grad_rows_all, jnp.concatenate(hidden, 1))
 
     grad_mixed_rows = [gather_tokens(grad_mixed[m].astype(BF16), head_first[m]) for m in each]
     grad_qkv, input_grads = [], []
     for m in each:
-        grad_attended = matmul(grad_mixed_rows[m], output_full).astype(BF16)
+        grad_attended = matmul(grad_mixed_rows[m], w_att[3]).astype(BF16)
         grad_sequences = attention_call(order, sequences[m], tables, to_sequences([grad_attended])[0])
         returned = from_sequences(grad_sequences)
         grad_qkv.append(jnp.concatenate([returned[0], returned[1], returned[2]], 1))
-        grad_normed = scatter_tokens(matmul_nt(grad_qkv[m], qkv_full), head_first[m])
+        grad_normed = scatter_tokens(functools.reduce(jnp.add, [matmul_nt(returned[i], w_att[i]) for i in range(3)]), head_first[m])
         input_grads.append((grad_mixed[m] + norm_back(grad_normed, inputs[m], scale_one[m])).astype(BF16))
-    output_grad = scatter_weight_grad(joined(grad_mixed_rows), joined(attended))
-    qkv_grad = scatter_weight_grad(joined(normed_one), joined(grad_qkv))
+    output_grad = scatter_weight_grad(joined(grad_mixed_rows), attended_all)
+    qkv_grad = scatter_weight_grad(normed_one_all, joined(grad_qkv))
 
     qkv_grads = [
         side_by_side(*(side[:, i * heads_width : (i + 1) * heads_width] for side in qkv_grad)) for i in range(3)

time: 1380 us -> 1220 us (0.88)
  waiting for transfers between devices: 732 us -> 329 us
  Pallas kernels: 101 us -> 453 us
  starting transfers between devices: 124 us -> 63.5 us
  other arithmetic: 102 us -> 62.4 us
  local copies, waits for them, and re-layouts: 92.7 us -> 57.1 us
  matrix products: 212 us -> 238 us
    pallas_call x0 -> x1, Pallas kernels: none -> 373 us  [front(): pl.pallas_call(functools.partial(front_kernel, (micros, groups, n_att, n_...]
    ppermute x104 -> x57, waiting for transfers between devices: 616 us -> 284 us  [swap(): return lax.ppermute(value, axis, [(i, i ^ bit) for i in range(count)])]
    ppermute x104 -> x57, starting transfers between devices: 117 us -> 59.4 us  [swap(): return lax.ppermute(value, axis, [(i, i ^ bit) for i in range(count)])]
    dot_general x20, matrix products: 65.6 us -> 121 us  [matmul_tn(): lax.dot_general(left_side, right_side, (((0,), (0,)), ((), ())), preferre...]
    ppermute x4 -> x2, waiting for transfers between devices: 88.5 us -> 45.8 us  [to_sequences(): lax.ppermute(chosen, 'blk', [(i, i ^ 2 * r) for i in range(2 * groups)])]
    unnamed x291 -> x213, local copies, waits for them, and re-layouts: 59.3 us -> 22.7 us
    ppermute x4 -> x2, waiting for transfers between devices: 27.9 us -> 0.01 us  [from_sequences(): lax.ppermute(chosen, 'blk', [(i, i ^ 2 * r) for i in range(2 * groups)])]
    pallas_call x4 -> x2, Pallas kernels: 62.5 us -> 42.1 us  [attention_call(): pl.pallas_call(functools.partial(kernel, tokens, blocks, rows_at_once), g...]
  transfers between devices with their start and end apart: 112 -> 61, of which waited for: 52 -> 27; matrix products, arithmetic and copies ran while one was open for 23% -> 23% of each run, Pallas kernels for 7% -> 37%
where the time goes in v2:
time: 1220 us; the launch traced here: 1210 us
  Pallas kernels  453 us (37%)
  waiting for transfers between devices  329 us (27%)
  matrix products  238 us (20%)
  starting transfers between devices  63.5 us (5%)
  other arithmetic  62.4 us (5%)
  local copies, waits for them, and re-layouts  57.1 us (5%)
    pallas_call x1, Pallas kernels, front(): pl.pallas_call(functools.partial(front_kernel, (micros, groups, n_att, n_...  373 us
    ppermute x57, waiting for transfers between devices, swap(): return lax.ppermute(value, axis, [(i, i ^ bit) for i in range(count)])  284 us
    dot_general x20, matrix products, matmul_tn(): lax.dot_general(left_side, right_side, (((0,), (0,)), ((), ())), preferre...  121 us
    dot_general x12, matrix products, matmul_nt(): lax.dot_general(left_side, right_side, (((1,), (1,)), ((), ())), preferre...  59.8 us
    ppermute x57, starting transfers between devices, swap(): return lax.ppermute(value, axis, [(i, i ^ bit) for i in range(count)])  59.4 us
    dot_general x8, matrix products, matmul(): return jnp.dot(left_side, right_side, preferred_element_type=F32)  57.3 us
    ppermute x2, waiting for transfers between devices, to_sequences(): lax.ppermute(chosen, 'blk', [(i, i ^ 2 * r) for i in range(2 * groups)])  45.8 us
    pallas_call x2, Pallas kernels, attention_call(): pl.pallas_call(functools.partial(kernel, tokens, blocks, rows_at_once), g...  42.1 us
  transfers between devices with their start and end apart: 61, of which 27 were waited for; matrix products, arithmetic and copies ran while one was open for 23% of the time, Pallas kernels for 37%

profile of v2, /device:TPU:0, one launch (start us, length us, event | category | flops | bytes accessed | tf_op | source)
XLA Modules:
  0.0 1206.6 jit_solution(12089880243123122466)
XLA Ops:
  50.6 373.1 %shard_map.231 = (bf16[2,8,128,512]{3,2,1,0:T(8,128)(2,1)}, bf16[2,8,128,512]{3,2,1,0:T(8,128)(2,1)}, bf16[2,8,128,512]{3,2,1,0:T(8,128)(2,1)}, bf16[2,8,128,512...) custom-call(bf16[2,128,2048]{2,1,0:T(8,128)(2,1)} %bitcast.181, ...), custom_call_target="tpu_custom_call" | custom-call | tf_op jit(solution)/shard_map/pallas_call | solution.py:731
  423.6 10.2 fusion.140
  472.4 12.4 %collective-permute-done.5 = bf16[256,2048]{1,0:T(8,128)(2,1)} collective-permute-done((bf16[256,2048]{1,0:T(8,128)(2,1)}, bf16[256,2048]{1,0:T(8,128)(2,1)}, u32[]{:S(2)}, u32[]{:S(2)}) %collective-permute-start.5) | collective-permute-done | bytes 1048608 | tf_op jit(solution)/shard_map/ppermute | solution.py:23
  498.9 14.9 %multiply_convert_fusion.2 = (bf16[1024,1024]{0,1:T(8,128)(2,1)}, bf16[1024,1024]{0,1:T(8,128)(2,1)}, bf16[1024,1024]{0,1:T(8,128)(2,1)}) fusion(f32[1024,1024]{0,1:T(8,128)} %fusion.139, f32[1024,1024]{0,1:T(8,128)} %fusion.140, bf16[1024,2048]{1,0:T(8,128)(2,1)} %slice_dynamic-update-slice_fusion, bf16[2048,1024]{1,0:T(8,128)(2,1)} %bitcast.249), kind=kOutput, calls=%fused_computation.16 | convolution fusion | flops 4310695936 | bytes 23068672 | tf_op jit(solution)/shard_map/dot_general | solution.py:36
  513.8 10.5 multiply_convert_fusion
  582.4 16.9 %add_convert_fusion = bf16[1024,2048]{1,0:T(8,128)(2,1)} fusion(f32[1024,2048]{1,0:T(8,128)} %fusion.146, f32[1024,2048]{1,0:T(8,128)} %fusion.144, f32[1024,2048]{1,0:T(8,128)} %fusion.145, bf16[1024,1024]{0,1:T(8,128)(2,1)} %get-tuple-element.77, bf16[2048,1024]{1,0:T(8,128)(2,1)} %bitcast.239), kind=kOutput, calls=%fused_computation.1 | convolution fusion | flops 4303355904 | bytes 35651584 | tf_op jit(solution)/shard_map/dot_general | solution.py:40
  617.6 10.6 collective-permute-done.8
  703.4 19.1 %collective-permute-done.58 = bf16[256,2048]{1,0:T(8,128)(2,1)S(1)} collective-permute-done((bf16[256,2048]{1,0:T(8,128)(2,1)S(1)}, bf16[256,2048]{1,0:T(8,128)(2,1)S(1)}, u32[]{:S(2)}, u32[]{:S(2)}) %collective-permute-start.58) | collective-permute-done | bytes 1048608 | tf_op jit(solution)/shard_map/ppermute | solution.py:23
  724.8 20.1 %collective-permute-done.40 = bf16[256,2048]{1,0:T(8,128)(2,1)S(1)} collective-permute-done((bf16[256,2048]{1,0:T(8,128)(2,1)S(1)}, bf16[256,2048]{1,0:T(8,128)(2,1)S(1)}, u32[]{:S(2)}, u32[]{:S(2)}) %collective-permute-start.40) | collective-permute-done | bytes 1048608 | tf_op jit(solution)/shard_map/ppermute | solution.py:23
  745.9 21.5 %collective-permute-done.43 = bf16[256,2048]{1,0:T(8,128)(2,1)S(1)} collective-permute-done((bf16[256,2048]{1,0:T(8,128)(2,1)S(1)}, bf16[256,2048]{1,0:T(8,128)(2,1)S(1)}, u32[]{:S(2)}, u32[]{:S(2)}) %collective-permute-start.43) | collective-permute-done | bytes 1048608 | tf_op jit(solution)/shard_map/ppermute | solution.py:23
  774.8 15.0 %collective-permute-done.47 = bf16[256,2048]{1,0:T(8,128)(2,1)S(1)} collective-permute-done((bf16[256,2048]{1,0:T(8,128)(2,1)S(1)}, bf16[256,2048]{1,0:T(8,128)(2,1)S(1)}, u32[]{:S(2)}, u32[]{:S(2)}) %collective-permute-start.47) | collective-permute-done | bytes 1048608 | tf_op jit(solution)/shard_map/ppermute | solution.py:23
  794.3 16.9 %collective-permute-done.50 = bf16[256,2048]{1,0:T(8,128)(2,1)S(1)} collective-permute-done((bf16[256,2048]{1,0:T(8,128)(2,1)S(1)}, bf16[256,2048]{1,0:T(8,128)(2,1)S(1)}, u32[]{:S(2)}, u32[]{:S(2)}) %collective-permute-start.50) | collective-permute-done | bytes 1048608 | tf_op jit(solution)/shard_map/ppermute | solution.py:23
  813.0 34.6 %collective-permute-done.12 = bf16[1,512,256]{2,1,0:T(8,128)(2,1)S(1)} collective-permute-done((bf16[1,512,256]{2,1,0:T(8,128)(2,1)S(1)}, bf16[1,512,256]{2,1,0:T(8,128)(2,1)S(1)}, u32[]{:S(2)}, u32[]{:S(2)}) %collective-permute-start.12) | collective-permute-done | bytes 262176 | tf_op jit(solution)/shard_map/ppermute | solution.py:170
  847.8 20.9 %shard_map.234 = bf16[3,8,128,256]{3,2,1,0:T(8,128)(2,1)S(1)} custom-call(s32[8]{0:T(128)S(1)} %fusion.121.order_ref, bf16[3,8,128,256]{3,2,1,0:T(8,128)(2,1)S(1)} %copy-done.2, bf16[8,128,256]{2,1,0:T(8,128)(2,1)S(1)} %maximum_bitcast_fusion.1.grad_ref, f32[1024,128]{1,0:T(8,128)S(1)} %copy-done.1, f32[1024,128]{1,0:T(8,128)S(1)} %copy-done), custom_call_target="tpu_custom_call" | custom-call | flops 5368709120 | bytes 3670016 | tf_op jit(solution)/shard_map/pallas_call | solution.py:313
  915.4 20.0 %collective-permute-done.45 = bf16[128,2048]{1,0:T(8,128)(2,1)} collective-permute-done((bf16[128,2048]{1,0:T(8,128)(2,1)}, bf16[128,2048]{1,0:T(8,128)(2,1)}, u32[]{:S(2)}, u32[]{:S(2)}) %collective-permute-start.45) | collective-permute-done | bytes 524320 | tf_op jit(solution)/shard_map/ppermute | solution.py:23
  974.0 11.2 collective-permute-done.20
  985.2 21.2 %shard_map.235 = bf16[3,8,128,256]{3,2,1,0:T(8,128)(2,1)S(1)} custom-call(s32[8]{0:T(128)S(1)} %fusion.121.order_ref, bf16[3,8,128,256]{3,2,1,0:T(8,128)(2,1)S(1)} %get-tuple-element.94.qkv_ref, bf16[8,128,256]{2,1,0:T(8,128)(2,1)S(1)} %maximum_bitcast_fusion.2.grad_ref, f32[1024,128]{1,0:T(8,128)S(1)} %copy-done.1, f32[1024,128]{1,0:T(8,128)S(1)} %copy-done), custom_call_target="tpu_custom_call" | custom-call | flops 5368709120 | bytes 3670016 | tf_op jit(solution)/shard_map/pallas_call | solution.py:313
  1026.8 23.8 %collective-permute-done.37 = bf16[128,512]{1,0:T(8,128)(2,1)S(1)} collective-permute-done((bf16[128,512]{1,0:T(8,128)(2,1)S(1)}, bf16[128,512]{1,0:T(8,128)(2,1)S(1)}, u32[]{:S(2)}, u32[]{:S(2)}) %collective-permute-start.37) | collective-permute-done | bytes 131104 | tf_op jit(solution)/shard_map/ppermute | solution.py:23
  1054.6 20.4 %convolution_convert_fusion.12 = bf16[512,1536]{1,0:T(8,128)(2,1)} fusion(bf16[1024,2048]{1,0:T(8,128)(2,1)} %bitcast.223, bf16[512,512]{1,0:T(8,128)(2,1)S(1)} %get-tuple-element.118, bf16[512,512]{1,0:T(8,128)(2,1)S(1)} %get-tuple-element.120, bf16[512,512]{1,0:T(8,128)(2,1)S(1)} %get-tuple-element.119, bf16[512,512]{1,0:T(8,128)(2,1)S(1)} %copy-done.45, ...), kind=kOutput, calls=%fused_computation.42 | convolution fusion | flops 1630273536 | bytes 5767168 | tf_op jit(solution)/shard_map/dot_general | solution.py:44
  1088.1 15.8 %collective-permute-done.22 = bf16[256,2048]{1,0:T(8,128)(2,1)S(1)} collective-permute-done((bf16[256,2048]{1,0:T(8,128)(2,1)}, bf16[256,2048]{1,0:T(8,128)(2,1)S(1)}, u32[]{:S(2)}, u32[]{:S(2)}) %collective-permute-start.22) | collective-permute-done | bytes 1048608 | tf_op jit(solution)/shard_map/ppermute | solution.py:23
  1105.9 17.8 %add_convert_fusion.10 = bf16[512,1536]{1,0:T(8,128)(2,1)S(1)} fusion(bf16[512,1536]{1,0:T(8,128)(2,1)S(1)} %collective-permute-done.27, bf16[1024,2048]{1,0:T(8,128)(2,1)S(1)} %bitcast.225, bf16[512,512]{1,0:T(8,128)(2,1)S(1)} %copy-done.49, bf16[512,512]{1,0:T(8,128)(2,1)S(1)} %get-tuple-element.120, bf16[512,512]{1,0:T(8,128)(2,1)S(1)} %get-tuple-element.119, ...), kind=kOutput, calls=%fused_computation.28 | convolution fusion | flops 1633419264 | bytes 7340032 | tf_op jit(solution)/shard_map/dot_general | solution.py:44
  1125.1 18.2 %add_convert_fusion.11 = bf16[512,1536]{1,0:T(8,128)(2,1)S(1)} fusion(bf16[512,1536]{1,0:T(8,128)(2,1)S(1)} %collective-permute-done.24, bf16[1024,2048]{1,0:T(8,128)(2,1)S(1)} %bitcast.226, bf16[512,512]{1,0:T(8,128)(2,1)S(1)} %copy-done.49, bf16[512,512]{1,0:T(8,128)(2,1)S(1)} %get-tuple-element.120, bf16[512,512]{1,0:T(8,128)(2,1)S(1)} %get-tuple-element.119, ...), kind=kOutput, calls=%fused_computation.29 | convolution fusion | flops 1633419264 | bytes 7340032 | tf_op jit(solution)/shard_map/dot_general | solution.py:44
  1148.8 11.3 collective-permute-done.25
  1160.4 14.7 %collective-permute-done.29 = bf16[128,1536]{1,0:T(8,128)(2,1)S(1)} collective-permute-done((bf16[128,1536]{1,0:T(8,128)(2,1)S(1)}, bf16[128,1536]{1,0:T(8,128)(2,1)S(1)}, u32[]{:S(2)}, u32[]{:S(2)}) %collective-permute-start.29) | collective-permute-done | bytes 393248 | tf_op jit(solution)/shard_map/ppermute | solution.py:23
  (500 shorter events, 432.4 us)
Async XLA Ops:
  13.4 443.3 %collective-permute-start.4 = (bf16[128,2048]{1,0:T(8,128)(2,1)}, bf16[128,2048]{1,0:T(8,128)(2,1)}, u32[]{:S(2)}, u32[]{:S(2)}) collective-permute-start(bf16[128,2048]{1,0:T(8,128)(2,1)} %pad_maximum_fusion.21), channel_id=1, source_target_pairs={{0,1},{1,0},{2,3},{3,2},{4,5},{5,4},{6,7},{7,6},{8,9},{9,8},{10,11... | collective-permute-start | bytes 1572872 | tf_op jit(solution)/shard_map/ppermute | solution.py:23
  18.8 442.6 %collective-permute-start.6 = (bf16[128,2048]{1,0:T(8,128)(2,1)S(1)}, bf16[128,2048]{1,0:T(8,128)(2,1)}, u32[]{:S(2)}, u32[]{:S(2)}) collective-permute-start(bf16[128,2048]{1,0:T(8,128)(2,1)S(1)} %get-tuple-element.138), channel_id=1, source_target_pairs={{0,4},{4,0},{1,5},{5,1},{2,6},{6,2},{3,7},{7,3},{8,12},{12,8},{9,1... | collective-permute-start | bytes 1572872 | tf_op jit(solution)/shard_map/ppermute | solution.py:23
  559.1 54.7 %collective-permute-start = (bf16[256,2048]{1,0:T(8,128)(2,1)}, bf16[256,2048]{1,0:T(8,128)(2,1)}, u32[]{:S(2)}, u32[]{:S(2)}) collective-permute-start(bf16[256,2048]{1,0:T(8,128)(2,1)} %fusion.65), channel_id=1, source_target_pairs={{0,1},{1,0},{2,3},{3,2},{4,5},{5,4},{6,7},{7,6},{8,9},{9,8},{10,11... | collective-permute-start | bytes 3145736 | tf_op jit(solution)/shard_map/ppermute | solution.py:23
  560.8 53.0 %collective-permute-start.2 = (bf16[256,2048]{1,0:T(8,128)(2,1)}, bf16[256,2048]{1,0:T(8,128)(2,1)}, u32[]{:S(2)}, u32[]{:S(2)}) collective-permute-start(bf16[256,2048]{1,0:T(8,128)(2,1)} %slice.611), channel_id=1, source_target_pairs={{0,4},{4,0},{1,5},{5,1},{2,6},{6,2},{3,7},{7,3},{8,12},{12,8},{9,1... | collective-permute-start | bytes 3145736 | tf_op jit(solution)/shard_map/ppermute | solution.py:23
  681.7 40.7 %collective-permute-start.58 = (bf16[256,2048]{1,0:T(8,128)(2,1)S(1)}, bf16[256,2048]{1,0:T(8,128)(2,1)S(1)}, u32[]{:S(2)}, u32[]{:S(2)}) collective-permute-start(bf16[256,2048]{1,0:T(8,128)(2,1)S(1)} %slice.736), channel_id=1, source_target_pairs={{0,16},{8,24},{16,0},{24,8},{1,17},{9,25},{17,1},{25,9},{2,18},{10... | collective-permute-start | bytes 3145736 | tf_op jit(solution)/shard_map/ppermute | solution.py:23
  687.4 57.5 %collective-permute-start.40 = (bf16[256,2048]{1,0:T(8,128)(2,1)S(1)}, bf16[256,2048]{1,0:T(8,128)(2,1)S(1)}, u32[]{:S(2)}, u32[]{:S(2)}) collective-permute-start(bf16[256,2048]{1,0:T(8,128)(2,1)S(1)} %slice.710), channel_id=1, source_target_pairs={{0,16},{8,24},{16,0},{24,8},{1,17},{9,25},{17,1},{25,9},{2,18},{10... | collective-permute-start | bytes 3145736 | tf_op jit(solution)/shard_map/ppermute | solution.py:23
  693.7 73.7 %collective-permute-start.43 = (bf16[256,2048]{1,0:T(8,128)(2,1)S(1)}, bf16[256,2048]{1,0:T(8,128)(2,1)S(1)}, u32[]{:S(2)}, u32[]{:S(2)}) collective-permute-start(bf16[256,2048]{1,0:T(8,128)(2,1)S(1)} %slice.716), channel_id=1, source_target_pairs={{0,16},{8,24},{16,0},{24,8},{1,17},{9,25},{17,1},{25,9},{2,18},{10... | collective-permute-start | bytes 3145736 | tf_op jit(solution)/shard_map/ppermute | solution.py:23
  699.1 90.8 %collective-permute-start.47 = (bf16[256,2048]{1,0:T(8,128)(2,1)S(1)}, bf16[256,2048]{1,0:T(8,128)(2,1)S(1)}, u32[]{:S(2)}, u32[]{:S(2)}) collective-permute-start(bf16[256,2048]{1,0:T(8,128)(2,1)S(1)} %slice.720), channel_id=1, source_target_pairs={{0,16},{8,24},{16,0},{24,8},{1,17},{9,25},{17,1},{25,9},{2,18},{10... | collective-permute-start | bytes 3145736 | tf_op jit(solution)/shard_map/ppermute | solution.py:23
  701.3 109.9 %collective-permute-start.50 = (bf16[256,2048]{1,0:T(8,128)(2,1)S(1)}, bf16[256,2048]{1,0:T(8,128)(2,1)S(1)}, u32[]{:S(2)}, u32[]{:S(2)}) collective-permute-start(bf16[256,2048]{1,0:T(8,128)(2,1)S(1)} %slice.724), channel_id=1, source_target_pairs={{0,16},{8,24},{16,0},{24,8},{1,17},{9,25},{17,1},{25,9},{2,18},{10... | collective-permute-start | bytes 3145736 | tf_op jit(solution)/shard_map/ppermute | solution.py:23
  722.4 47.6 %collective-permute-start.11 = (bf16[256,2048]{1,0:T(8,128)(2,1)S(1)}, bf16[256,2048]{1,0:T(8,128)(2,1)S(1)}, u32[]{:S(2)}, u32[]{:S(2)}) collective-permute-start(bf16[256,2048]{1,0:T(8,128)(2,1)S(1)} %pad_maximum_fusion.15), channel_id=1, source_target_pairs={{0,4},{4,0},{1,5},{5,1},{2,6},{6,2},{3,7},{7,3},{8,12},{12,8},{9,1... | collective-permute-start | bytes 3145736 | tf_op jit(solution)/shard_map/ppermute | solution.py:23
  744.9 151.9 %collective-permute-start.56 = (bf16[128,2048]{1,0:T(8,128)(2,1)}, bf16[128,2048]{1,0:T(8,128)(2,1)}, u32[]{:S(2)}, u32[]{:S(2)}) collective-permute-start(bf16[128,2048]{1,0:T(8,128)(2,1)} %slice.732), channel_id=1, source_target_pairs={{0,2},{1,3},{2,0},{3,1},{4,6},{5,7},{6,4},{7,5},{8,10},{9,11},{10,... | collective-permute-start | bytes 1572872 | tf_op jit(solution)/shard_map/ppermute | solution.py:23
  767.4 102.6 %collective-permute-start.59 = (bf16[128,2048]{1,0:T(8,128)(2,1)}, bf16[128,2048]{1,0:T(8,128)(2,1)S(1)}, u32[]{:S(2)}, u32[]{:S(2)}) collective-permute-start(bf16[128,2048]{1,0:T(8,128)(2,1)} %slice.738), channel_id=1, source_target_pairs={{0,2},{1,3},{2,0},{3,1},{4,6},{5,7},{6,4},{7,5},{8,10},{9,11},{10,... | collective-permute-start | bytes 1572872 | tf_op jit(solution)/shard_map/ppermute | solution.py:23
  770.0 143.3 %collective-permute-start.41 = (bf16[128,2048]{1,0:T(8,128)(2,1)}, bf16[128,2048]{1,0:T(8,128)(2,1)}, u32[]{:S(2)}, u32[]{:S(2)}) collective-permute-start(bf16[128,2048]{1,0:T(8,128)(2,1)} %slice.712), channel_id=1, source_target_pairs={{0,2},{1,3},{2,0},{3,1},{4,6},{5,7},{6,4},{7,5},{8,10},{9,11},{10,... | collective-permute-start | bytes 1572872 | tf_op jit(solution)/shard_map/ppermute | solution.py:23
  789.9 80.9 %collective-permute-start.44 = (bf16[128,2048]{1,0:T(8,128)(2,1)}, bf16[128,2048]{1,0:T(8,128)(2,1)S(1)}, u32[]{:S(2)}, u32[]{:S(2)}) collective-permute-start(bf16[128,2048]{1,0:T(8,128)(2,1)} %slice.718), channel_id=1, source_target_pairs={{0,2},{1,3},{2,0},{3,1},{4,6},{5,7},{6,4},{7,5},{8,10},{9,11},{10,... | collective-permute-start | bytes 1572872 | tf_op jit(solution)/shard_map/ppermute | solution.py:23
  847.7 89.4 %collective-permute-start.48 = (bf16[128,2048]{1,0:T(8,128)(2,1)}, bf16[128,2048]{1,0:T(8,128)(2,1)}, u32[]{:S(2)}, u32[]{:S(2)}) collective-permute-start(bf16[128,2048]{1,0:T(8,128)(2,1)} %slice.722), channel_id=1, source_target_pairs={{0,2},{1,3},{2,0},{3,1},{4,6},{5,7},{6,4},{7,5},{8,10},{9,11},{10,... | collective-permute-start | bytes 1572872 | tf_op jit(solution)/shard_map/ppermute | solution.py:23
  895.9 56.4 %collective-permute-start.13 = (bf16[3,4,128,256]{3,2,1,0:T(8,128)(2,1)}, bf16[3,4,128,256]{3,2,1,0:T(8,128)(2,1)}, u32[]{:S(2)}, u32[]{:S(2)}) collective-permute-start(bf16[3,4,128,256]{3,2,1,0:T(8,128)(2,1)} %get-tuple-element.116), channel_id=1, source_target_pairs={{0,2},{1,3},{2,0},{3,1},{4,6},{5,7},{6,4},{7,5},{8,10},{9,11},{10,... | collective-permute-start | bytes 2359304 | tf_op jit(solution)/shard_map/ppermute | solution.py:183
  913.3 55.7 %collective-permute-start.19 = (bf16[256,2048]{1,0:T(8,128)(2,1)}, bf16[256,2048]{1,0:T(8,128)(2,1)S(1)}, u32[]{:S(2)}, u32[]{:S(2)}) collective-permute-start(bf16[256,2048]{1,0:T(8,128)(2,1)} %fusion.61), channel_id=1, source_target_pairs={{0,1},{1,0},{2,3},{3,2},{4,5},{5,4},{6,7},{7,6},{8,9},{9,8},{10,11... | collective-permute-start | bytes 3145736 | tf_op jit(solution)/shard_map/ppermute | solution.py:23
  959.5 56.6 %collective-permute-start.14 = (bf16[256,2048]{1,0:T(8,128)(2,1)S(1)}, bf16[256,2048]{1,0:T(8,128)(2,1)S(1)}, u32[]{:S(2)}, u32[]{:S(2)}) collective-permute-start(bf16[256,2048]{1,0:T(8,128)(2,1)S(1)} %fusion.62), channel_id=1, source_target_pairs={{0,1},{1,0},{2,3},{3,2},{4,5},{5,4},{6,7},{7,6},{8,9},{9,8},{10,11... | collective-permute-start | bytes 3145736 | tf_op jit(solution)/shard_map/ppermute | solution.py:23
  970.1 39.9 %collective-permute-start.32 = (bf16[512,512]{1,0:T(8,128)(2,1)S(1)}, bf16[512,512]{1,0:T(8,128)(2,1)S(1)}, u32[]{:S(2)}, u32[]{:S(2)}) collective-permute-start(bf16[512,512]{1,0:T(8,128)(2,1)S(1)} %convolution_convert_fusion.18), channel_id=1, source_target_pairs={{0,8},{8,0},{16,24},{24,16},{1,9},{9,1},{17,25},{25,17},{2,10},{10... | collective-permute-start | bytes 1572872 | tf_op jit(solution)/shard_map/ppermute | solution.py:23
  973.9 40.1 %collective-permute-start.35 = (bf16[512,512]{1,0:T(8,128)(2,1)S(1)}, bf16[512,512]{1,0:T(8,128)(2,1)S(1)}, u32[]{:S(2)}, u32[]{:S(2)}) collective-permute-start(bf16[512,512]{1,0:T(8,128)(2,1)S(1)} %convolution_convert_fusion.16), channel_id=1, source_target_pairs={{0,8},{8,0},{16,24},{24,16},{1,9},{9,1},{17,25},{25,17},{2,10},{10... | collective-permute-start | bytes 1572872 | tf_op jit(solution)/shard_map/ppermute | solution.py:23
  1006.5 44.2 %collective-permute-start.21 = (bf16[3,4,128,256]{3,2,1,0:T(8,128)(2,1)S(1)}, bf16[3,4,128,256]{3,2,1,0:T(8,128)(2,1)S(1)}, u32[]{:S(2)}, u32[]{:S(2)}) collective-permute-start(bf16[3,4,128,256]{3,2,1,0:T(8,128)(2,1)S(1)} %get-tuple-element.123), channel_id=1, source_target_pairs={{0,2},{1,3},{2,0},{3,1},{4,6},{5,7},{6,4},{7,5},{8,10},{9,11},{10,... | collective-permute-start | bytes 2359304 | tf_op jit(solution)/shard_map/ppermute | solution.py:183
  1017.2 127.2 %collective-permute-start.15 = (bf16[128,2048]{1,0:T(8,128)(2,1)}, bf16[128,2048]{1,0:T(8,128)(2,1)}, u32[]{:S(2)}, u32[]{:S(2)}) collective-permute-start(bf16[128,2048]{1,0:T(8,128)(2,1)} %add_convert_fusion.25), channel_id=1, source_target_pairs={{0,4},{4,0},{1,5},{5,1},{2,6},{6,2},{3,7},{7,3},{8,12},{12,8},{9,1... | collective-permute-start | bytes 1572872 | tf_op jit(solution)/shard_map/ppermute | solution.py:23
  1024.1 56.5 %collective-permute-start.34 = (bf16[128,512]{1,0:T(8,128)(2,1)S(1)}, bf16[128,512]{1,0:T(8,128)(2,1)S(1)}, u32[]{:S(2)}, u32[]{:S(2)}) collective-permute-start(bf16[128,512]{1,0:T(8,128)(2,1)S(1)} %slice.700), channel_id=1, source_target_pairs={{0,2},{1,3},{2,0},{3,1},{4,6},{5,7},{6,4},{7,5},{8,10},{9,11},{10,... | collective-permute-start | bytes 393224 | tf_op jit(solution)/shard_map/ppermute | solution.py:23
  1104.1 40.2 %collective-permute-start.23 = (bf16[128,2048]{1,0:T(8,128)(2,1)S(1)}, bf16[128,2048]{1,0:T(8,128)(2,1)S(1)}, u32[]{:S(2)}, u32[]{:S(2)}) collective-permute-start(bf16[128,2048]{1,0:T(8,128)(2,1)S(1)} %pad_maximum_fusion.24), channel_id=1, source_target_pairs={{0,1},{1,0},{2,3},{3,2},{4,5},{5,4},{6,7},{7,6},{8,9},{9,8},{10,11... | collective-permute-start | bytes 1572872 | tf_op jit(solution)/shard_map/ppermute | solution.py:23
  (138 other events, 2512.1 us)

commit v3 on v2

--- a/solution.py
+++ b/solution.py
@@ -57,26 +57,28 @@
     return jnp.asarray(order) ^ mine, jnp.asarray(back)[absolute]
 
 
-def reorder_kernel(order_ref, source_ref, target_ref):
-    target_ref[...] = source_ref[...]
-
-
-def reorder(rows, order):
-    count, width = rows.shape
+def reorder_kernel(count, order_ref, *refs):
+    for source, target in zip(refs[:count], refs[count:]):
+        blocks = order_ref.shape[0]
+        piece = source.shape[1] // blocks
+        for j in range(blocks):
+            start = pl.multiple_of(order_ref[j] * piece, piece)
+            target[:, j * piece : (j + 1) * piece] = source[:, pl.ds(start, piece)]
+
+
+def reorder(order, *arrays):
+    count, width = arrays[0].shape
     blocks = order.shape[0]
     piece = width // blocks
     if piece % LANES:
-        return jnp.take(rows.reshape(count, blocks, piece), order, axis=1).reshape(count, width)
+        return [jnp.take(rows.reshape(count, blocks, piece), order, axis=1).reshape(count, width) for rows in arrays]
+    in_vmem = pl.BlockSpec(memory_space=pltpu.VMEM)
     return pl.pallas_call(
-        reorder_kernel,
-        grid_spec=pltpu.PrefetchScalarGridSpec(
-            num_scalar_prefetch=1,
-            grid=(blocks,),
-            in_specs=[pl.BlockSpec((count, piece), lambda j, order_ref: (0, order_ref[j]))],
-            out_specs=pl.BlockSpec((count, piece), lambda j, order_ref: (0, j)),
-        ),
-        out_shape=jax.ShapeDtypeStruct(rows.shape, rows.dtype),
-    )(order, rows)
+        functools.partial(reorder_kernel, len(arrays)),
+        in_specs=[pl.BlockSpec(memory_space=pltpu.SMEM)] + [in_vmem] * len(arrays),
+        out_specs=[in_vmem] * len(arrays),
+        out_shape=[jax.ShapeDtypeStruct(rows.shape, rows.dtype) for rows in arrays],
+    )(order, *arrays)
 
 
 def turn_features(rows):
@@ -197,12 +199,12 @@
 
 def rope_tables(length, lanes):
     half = HD // 2
-    frequency = ROPE_BASE ** (-jnp.arange(half, dtype=F32) * 2.0 / HD)
-    angles = jnp.arange(length, dtype=F32)[:, None] * frequency[None, :]
-    cosine, sine = jnp.cos(angles), jnp.sin(angles)
+    frequency = ROPE_BASE ** (-np.arange(half, dtype=np.float32) * np.float32(2.0 / HD))
+    angles = np.arange(length, dtype=np.float32)[:, None] * frequency.astype(np.float32)[None, :]
+    cosine, sine = np.cos(angles), np.sin(angles)
     return (
-        jnp.tile(cosine, (1, lanes // half)),
-        jnp.tile(jnp.concatenate([-sine, sine], 1), (1, lanes // HD)),
+        jnp.asarray(np.tile(cosine, (1, lanes // half)), F32),
+        jnp.asarray(np.tile(np.concatenate([-sine, sine], 1), (1, lanes // HD)), F32),
     )
 
 
@@ -369,6 +371,13 @@
         copy.start()
         return copy
 
+    def is_unsent(self, copy):
+        return any(copy is other for other in self.sent)
+
+    def wait_sent(self, copy):
+        copy.wait_send()
+        self.sent = [other for other in self.sent if other is not copy]
+
     def finish(self):
         for copy in self.sent:
             copy.wait_send()
@@ -434,6 +443,7 @@
             leaving[m, 0] = halves_turned(partial[m, 0, 1])
             leaving[m, 1] = halves_turned(partial[m, 1, 1])
             self.copy = copies.remote(leaving.at[m], came.at[m], "blk", 1)
+        self.first = self.copy
 
     def second(self):
         m, partial = self.m, self.partial
@@ -452,6 +462,10 @@
         self.copy.wait_recv()
         self.total[self.m] += self.last[self.m].astype(F32)
 
+    def release(self):
+        self.copies.wait_sent(self.first)
+        self.copies.wait_sent(self.copy)
+
 
 def place_of(block):
     n_blk = lax.axis_size("blk")
@@ -534,13 +548,13 @@
 
 def front_kernel(sizes, *refs):
     micros, groups, n_att, n_mlp = sizes
-    x_ref, att_in, mlp_in, cosine_ref, sine_ref = refs[:5]
-    refs = refs[5:]
+    x_ref, g_in, g_turned, att_in, mlp_in, cosine_ref, sine_ref = refs[:7]
+    refs = refs[7:]
     w_att, refs = refs[:n_att], refs[n_att:]
     w_mlp, refs = refs[:n_mlp], refs[n_mlp:]
-    xg_out, seq_out, attended_out, mixed_out, x2_out = refs[:5]
+    xg_out, seq_out, attended_out, mixed_out, x2_out, gg_out = refs[:6]
     (xg, x2, turned_rows, turned_more, w_in, w_out, made, seq, heads_out, attended, partial,
-     leaving, came, passing, last, mixed, q_s, k_s, v_s, send, recv, local) = refs[5:]
+     leaving, came, passing, last, mixed, q_s, k_s, v_s, send, recv, local) = refs[6:]
     held = (q_s, k_s, v_s)
     each = range(micros)
     near = lax.axis_index("blk") % 2
@@ -569,6 +583,8 @@
     ]
     for gather in gathers:
         gather.second()
+    grad_own = [copies.inside(g_in.at[m], gg_out.at[m, 0, 0]) for m in each]
+    grad_rows = [copies.remote(g_turned.at[m], gg_out.at[m, 0, 1], "blk", 1) for m in each]
     stages = len(replica_stages())
     steps = [[] for _ in range(stages + n_att)]
     for s in range(stages):
@@ -617,6 +633,10 @@
                 crossing[m].append(
                     copies.remote(made.at[m, flipped("blk", 2 * r) // 2, i], seq.at[m, upper, i], "blk", 2 * r)
                 )
+    for m in each:
+        grad_own[m].wait()
+        grad_rows[m].wait_recv()
+        grad_rows[m] = copies.remote(gg_out.at[m, 0], gg_out.at[m, 1], "head", 1)
     returning = []
     for m in each:
         pump(1)
@@ -671,12 +691,14 @@
         gather.end()
     writes.append(copies.inside(x2, x2_out))
     pump(len(background) - done[0])
+    for copy in grad_rows:
+        copy.wait_recv()
     for copy in writes:
         copy.wait()
     copies.finish()
 
 
-def front(x_rows, att_in, mlp_in, tables):
+def front(x_rows, grad_rows, grad_turned, att_in, mlp_in, tables):
     micros, tokens, width = x_rows.shape
     n_att, _, piece, heads_width = att_in.shape
     n_weights, parts, _, columns = mlp_in.shape
@@ -698,6 +720,7 @@
         bf16(micros, groups, 3, 4, tokens, here),
         bf16(micros, groups, 4, tokens, here),
         jax.ShapeDtypeStruct((micros, tokens, width), F32),
+        bf16(*token_rows),
         bf16(*token_rows),
     ]
 
@@ -731,16 +754,403 @@
     results = pl.pallas_call(
         functools.partial(front_kernel, (micros, groups, n_att, n_mlp)),
         out_shape=outs,
-        in_specs=[in_vmem, any_space, any_space, in_vmem, in_vmem],
+        in_specs=[in_vmem] + [any_space] * 4 + [in_vmem, in_vmem],
         out_specs=[any_space] * len(outs),
         scratch_shapes=scratch,
         compiler_params=pltpu.CompilerParams(
             collective_id=0, has_side_effects=True, vmem_limit_bytes=60 * 1024 * 1024
         ),
-    )(x_rows, att_in, mlp_in, *tables)
+    )(x_rows, grad_rows, grad_turned, att_in, mlp_in, *tables)
     w_att, results = results[:n_att], results[n_att:]
     w_mlp, results = results[:n_mlp], results[n_mlp:]
-    return [w.reshape(width, -1) for w in w_att], [w.reshape(width, -1) for w in w_mlp], results
+    return w_att, [w.reshape(width, -1) for w in w_mlp], results
+
+
+class GradScatter:
+    def __init__(self, copies, kept, first_copy, landed, room, final, own, other):
+        self.copies, self.kept, self.copy, self.landed = copies, kept, first_copy, landed
+        self.room, self.final, self.own, self.other = room, final, own, other
+        self.stage = 0
+
+    def advance(self):
+        copies, kept, stage = self.copies, self.kept, self.stage
+        stages = replica_stages()[::-1]
+        self.copy.wait_recv()
+        self.stage += 1
+        if stage == len(stages):
+            return
+        count = kept.shape[1] >> stage
+        columns = kept.shape[-1]
+        mine, came = (part.at[:, 0:count, :, 0:columns] for part in self.room)
+        loads = [copies.inside(kept.at[:, 0:count], mine), copies.inside(self.landed[stage], came)]
+        for load in loads:
+            load.wait()
+        if stage == len(stages) - 1:
+            self.final[:, 0:columns] = mine[0, 0].astype(F32) + came[0, 0].astype(F32)
+            mine[1, 0] = (mine[1, 0].astype(F32) + came[1, 0].astype(F32)).astype(BF16)
+            stores = [
+                copies.inside(self.final.at[:, 0:columns], self.own),
+                copies.inside(mine.at[1, 0], kept.at[1, 0]),
+            ]
+            for store in stores:
+                store.wait()
+            self.copy = copies.remote(kept.at[1, 0], self.other, "blk", 1)
+            return
+
+        def one(i, carry):
+            half, row = i // count, i % count
+            mine[half, row] = (mine[half, row].astype(F32) + came[half, row].astype(F32)).astype(BF16)
+            return carry
+
+        lax.fori_loop(0, 2 * count, one, 0)
+        copies.inside(mine, kept.at[:, 0:count]).wait()
+        self.copy = copies.remote(
+            kept.at[:, count // 2 : count], self.landed[stage + 1], *stages[stage + 1]
+        )
+
+
+def attend_back(seq, seq_at, grad, out, m, cosine_ref, sine_ref, held, sums):
+    tokens, width = seq.shape[-2:]
+    q_s, k_s, v_s = held
+    dk_s, dv_s = sums
+    length, lanes = q_s.shape
+    rows_at_once = min(256, length)
+
+    def rows_of(first, last, lane):
+        places = [place_of((first + offset) // tokens) for offset in range(0, rows_at_once, tokens)]
+        grad_rows = jnp.concatenate([grad[m, u, g, :, pl.ds(lane, lanes)] for u, g in places], 0)
+        rows = pl.ds(first, rows_at_once)
+        query_parts, key_parts, value_parts = [], [], []
+        for start in range(0, lanes, HD):
+            head = slice(start, start + HD)
+            query, keys, grad_part = q_s[rows, head], k_s[:last, head], grad_rows[:, head]
+            weights, inverse = softmax_rows(query, keys, first)
+            probabilities = weights * inverse
+            grad_prob = matmul_nt(grad_part, v_s[:last, head])
+            row_delta = jnp.sum(probabilities * grad_prob, 1, keepdims=True)
+            grad_scores = (probabilities * (grad_prob - row_delta) * HD ** (-0.5)).astype(BF16)
+            query_parts.append(matmul(grad_scores, keys))
+            key_parts.append(matmul_tn(grad_scores, query))
+            value_parts.append(matmul_tn(probabilities.astype(BF16), grad_part))
+        grad_query = jnp.concatenate(query_parts, 1)
+        grad_query = turned(grad_query, cosine_ref[rows, :], -sine_ref[rows, :]).astype(BF16)
+        for i, (u, g) in enumerate(places):
+            out[m, u, 0, g, :, pl.ds(lane, lanes)] = grad_query[i * tokens : (i + 1) * tokens]
+        dk_s[:last, :] += jnp.concatenate(key_parts, 1)
+        dv_s[:last, :] += jnp.concatenate(value_parts, 1)
+
+    def heads(lane):
+        load_heads(seq, seq_at, lane, cosine_ref, sine_ref, held)
+        dk_s[...] = jnp.zeros_like(dk_s)
+        dv_s[...] = jnp.zeros_like(dv_s)
+        over_rows(length, rows_at_once, lambda first, last: rows_of(first, last, lane))
+
+        def one(block, carry):
+            u, g = place_of(block)
+            rows = pl.ds(pl.multiple_of(block * tokens, tokens), tokens)
+            grad_key = turned(dk_s[rows, :], cosine_ref[rows, :], -sine_ref[rows, :])
+            out[m, u, 1, g, :, pl.ds(lane, lanes)] = grad_key.astype(BF16)
+            out[m, u, 2, g, :, pl.ds(lane, lanes)] = dv_s[rows, :].astype(BF16)
+            return carry
+
+        lax.fori_loop(0, length // tokens, one, 0)
+
+    over_lanes(width, lanes, heads)
+
+
+def back_kernel(sizes, *refs):
+    micros, groups, n_mlp, n_att = sizes
+    stages = len(replica_stages())
+
+    def take(count):
+        nonlocal refs
+        taken, refs = refs[:count], refs[count:]
+        return taken
+
+    e_in, mixed_in, x2_in, gg_in, xg_in, attended_in, seq_in, g_ref, x_ref, cosine_ref, sine_ref = take(11)
+    grads_in, w_att = take(n_mlp), take(n_att)
+    own_mlp, other_mlp, own_att, other_att = take(n_mlp), take(n_mlp), take(n_att), take(n_att)
+    (input_out,) = take(1)
+    kept_mlp, kept_att = take(n_mlp), take(n_att)
+    landed_mlp = [take(stages) for _ in range(n_mlp)]
+    landed_att = [take(stages) for _ in range(n_att)]
+    (partial, leaving, came, passing, last, came_c, last_c, total, total_c, rows_g,
+     turned_g, leaves, room_a, room_b, final, made_o, arrived_o, made_b, rows_b, rows_o,
+     acts, weights, seq, q_s, k_s, v_s, dk_s, dv_s, send, recv, local) = refs
+    each = range(micros)
+    upper = lax.axis_index("blk") // 2
+    tokens, width = x_ref.shape[-2:]
+    here = made_o.shape[-1]
+    heads_width = here * groups
+    _, kept_pieces, piece, _ = kept_mlp[0].shape
+    copies = Copies(send, recv, local)
+    count = 4 * tokens
+    tile = 256
+
+    greet()
+    loads = [copies.inside(e_in, partial), copies.inside(mixed_in, total_c)]
+    for load in loads:
+        load.wait()
+    for m in each:
+        total[m] = jnp.zeros_like(total[m])
+    scatters = [TokenScatter(copies, partial, leaving, came, passing, last, total, m) for m in each]
+
+    busy = []
+
+    def weight_grad(acts, grads, kept, landed, own, other):
+        part_columns = grads[0].shape[-1]
+        columns = part_columns * len(grads)
+        for copy in busy:
+            copies.wait_sent(copy)
+        busy.clear()
+        per_half = kept_pieces * piece // tile
+        pieces = tile // piece
+        for side in (1, 0):
+            side_room = leaves if side else room_a
+
+            def one(i, carry, side=side, side_room=side_room):
+                low, part = i // per_half, i % per_half
+                start = low * (2 * kept_pieces * piece) + side * (kept_pieces * piece) + part * tile
+                lanes = pl.ds(pl.multiple_of(start, tile), tile)
+                left = acts[:, :, :, :, lanes].reshape(micros * count, tile)
+                for j, right in enumerate(grads):
+                    product = matmul_tn(left, right[...].reshape(micros * count, part_columns)).astype(BF16)
+                    columns_here = slice(j * part_columns, (j + 1) * part_columns)
+                    side_room[low, pl.ds(part * pieces, pieces), :, columns_here] = product.reshape(
+                        pieces, piece, part_columns
+                    )
+                return carry
+
+            lax.fori_loop(0, 2 * per_half, one, 0)
+            source = side_room.at[:, :, :, 0:columns]
+            if side:
+                first = copies.remote(source, landed[0], *replica_stages()[-1])
+                busy.append(first)
+            else:
+                copies.inside(source, kept).wait()
+        return GradScatter(copies, kept, first, landed, (room_a, room_b), final, own, other)
+
+    chunks = []
+
+    def pump():
+        for chunk in reversed(chunks):
+            if chunk.stage <= stages:
+                chunk.advance()
+
+    def load_grads(k):
+        loads = []
+        for half_of in range(2):
+            lanes = slice(half_of * heads_width, (half_of + 1) * heads_width)
+            for row in range(2 * kept_pieces):
+                source = grads_in[k].at[row * piece : (row + 1) * piece, lanes]
+                loads.append(copies.inside(source, weights.at[k % 2, half_of, row]))
+        return loads
+
+    acts_load = copies.inside(x2_in, acts)
+    slots = [load_grads(0)]
+
+    def mlp_chunk(k):
+        for load in slots[k]:
+            load.wait()
+        if k + 1 < n_mlp:
+            slots.append(load_grads(k + 1))
+        parts = [weights.at[k % 2, half] for half in range(2)]
+        return weight_grad(acts, parts, kept_mlp[k], landed_mlp[k], own_mlp[k], other_mlp[k])
+
+    acts_load.wait()
+    chunks.append(mlp_chunk(0))
+    chunks.append(mlp_chunk(1))
+    for scatter in scatters:
+        scatter.second()
+    pump()
+    chunks.append(mlp_chunk(2))
+    gathers = []
+    for m in each:
+        scatters[m].end()
+        mixed = total_c[m]
+        scale = lax.rsqrt(jnp.mean(mixed * mixed, -1, keepdims=True) + EPSILON)
+        total[m] = g_ref[m].astype(F32) + norm_back(total[m], mixed, scale)
+        rows_g[m, 0, 0] = total[m].astype(BF16)
+        gathers.append(TokenGather(copies, rows_g, turned_g, m))
+    pump()
+    chunks.append(mlp_chunk(3))
+    acts_load = copies.inside(gg_in, acts)
+    for gather in gathers:
+        gather.second()
+    acts_load.wait()
+    chunks.append(mlp_chunk(4))
+    pump()
+    chunks.append(mlp_chunk(5))
+    for gather in gathers:
+        gather.end()
+
+    for scatter in scatters:
+        scatter.release()
+    w_loads = [copies.inside(w_att[i], weights.at[slot]) for i, slot in ((3, 0), (0, 1), (1, 2))]
+    seq_load = copies.inside(seq_in.at[0], seq.at[0])
+    att_loads = [
+        copies.inside(attended_in.at[m, place], rows_o.at[4 * m : 4 * m + 4, :, place * here : (place + 1) * here])
+        for m in each
+        for place in range(groups)
+    ]
+    w_loads[0].wait()
+    crossing = []
+    for m in each:
+        rows = rows_g[m].reshape(count, width)
+        product = matmul(rows, weights[0].reshape(width, heads_width)).astype(BF16)
+        for place in range(groups):
+            for group in range(4):
+                made_o[m, place, group] = product[
+                    group * tokens : (group + 1) * tokens, place * here : (place + 1) * here
+                ]
+        moves = [copies.inside(made_o.at[m, upper], arrived_o.at[m, upper])]
+        for r in range(1, groups):
+            source = made_o.at[m, flipped("blk", 2 * r) // 2]
+            moves.append(copies.remote(source, arrived_o.at[m, upper], "blk", 2 * r))
+        crossing.append(moves)
+    w_loads.append(copies.inside(w_att[2], weights.at[0]))
+    for load in att_loads:
+        load.wait()
+    chunks.append(weight_grad(rows_g, [rows_o], kept_att[3], landed_att[3], own_att[3], other_att[3]))
+    returning = []
+    own_lanes = pl.ds(pl.multiple_of(upper * here, here), here)
+    for m in each:
+        seq_load.wait()
+        crossing[m][0].wait()
+        for copy in crossing[m][1:]:
+            copy.wait_recv()
+        attend_back(seq, 0, arrived_o, made_b, m, cosine_ref, sine_ref, (q_s, k_s, v_s), (dk_s, dv_s))
+        if m + 1 < micros:
+            seq_load = copies.inside(seq_in.at[m + 1], seq.at[0])
+        moves = ([], [])
+        for i in range(3):
+            target = rows_b.at[i, 4 * m : 4 * m + 4, :, own_lanes]
+            moves[0].append(copies.inside(made_b.at[m, upper, i], target))
+            for r in range(1, groups):
+                source = made_b.at[m, flipped("blk", 2 * r) // 2, i]
+                moves[1].append(copies.remote(source, target, "blk", 2 * r))
+        returning.append(moves)
+        pump()
+    for load in w_loads[1:]:
+        load.wait()
+    started = []
+    for m in each:
+        for copy in returning[m][0]:
+            copy.wait()
+        for copy in returning[m][1]:
+            copy.wait_recv()
+        pieces = tile // piece
+        for start in range(0, width, tile):
+            low, first = start // (2 * kept_pieces * piece), start // piece % (2 * kept_pieces)
+            product = functools.reduce(
+                jnp.add,
+                [
+                    matmul_nt(
+                        rows_b[i, 4 * m : 4 * m + 4].reshape(count, heads_width),
+                        weights[(i + 1) % 3, low, first : first + pieces].reshape(tile, heads_width),
+                    )
+                    for i in range(3)
+                ],
+            ).astype(BF16)
+            for group in range(4):
+                partial[m, group // 2, group % 2, :, start : start + tile] = product[
+                    group * tokens : (group + 1) * tokens
+                ]
+        total_c[m] = jnp.zeros_like(total_c[m])
+        started.append(TokenScatter(copies, partial, leaving, came_c, passing, last_c, total_c, m))
+
+    copies.inside(xg_in, acts).wait()
+    for i in range(3):
+        chunks.append(weight_grad(acts, [rows_b.at[i]], kept_att[i], landed_att[i], own_att[i], other_att[i]))
+    pump()
+    for scatter in started:
+        scatter.second()
+    pump()
+    for m in each:
+        started[m].end()
+        started[m].release()
+        values = x_ref[m].astype(F32)
+        scale = lax.rsqrt(jnp.mean(values * values, -1, keepdims=True) + EPSILON)
+        passing[m] = (total[m] + norm_back(total_c[m], values, scale)).astype(BF16)
+    copies.inside(passing, input_out).wait()
+    while any(chunk.stage <= stages for chunk in chunks):
+        pump()
+    copies.finish()
+
+
+def back(partial, mixed, x2, grad_rows, normed_one, attended, sequences, g_rows, x_rows, tables, grads, w_att):
+    micros, tokens, width = x_rows.shape
+    n_mlp, n_att = len(grads), len(w_att)
+    columns = grads[0].shape[1]
+    _, replicas, piece, heads_width = w_att[0].shape
+    groups = head_groups()
+    here = heads_width // groups
+    stages = len(replica_stages())
+    any_space = pl.BlockSpec(memory_space=pl.ANY)
+    in_vmem = pl.BlockSpec(memory_space=pltpu.VMEM)
+
+    def bf16(*shape):
+        return jax.ShapeDtypeStruct(shape, BF16)
+
+    def room(*shape):
+        return pltpu.VMEM(shape, BF16)
+
+    def f32_room(*shape):
+        return pltpu.VMEM(shape, F32)
+
+    widths = [columns] * n_mlp + [heads_width] * n_att
+    outs = [jax.ShapeDtypeStruct((piece, columns), F32)] * n_mlp + [bf16(piece, columns)] * n_mlp
+    outs += [jax.ShapeDtypeStruct((piece, heads_width), F32)] * n_att + [bf16(piece, heads_width)] * n_att
+    outs += [bf16(micros, tokens, width)]
+    outs += [bf16(2, replicas // 2, piece, w) for w in widths]
+    outs += [bf16(2, replicas >> (s + 1), piece, w) for w in widths for s in range(stages)]
+    token_rows = (micros, 2, 2, tokens, width)
+    half_room = (2, replicas // 2, piece, max(columns, heads_width))
+    scratch = [
+        room(*token_rows),
+        room(micros, 2, tokens, width),
+        room(micros, 2, tokens, width),
+        room(micros, tokens, width),
+        room(micros, tokens, width),
+        room(micros, 2, tokens, width),
+        room(micros, tokens, width),
+        f32_room(micros, tokens, width),
+        f32_room(micros, tokens, width),
+        room(*token_rows),
+        room(micros, 2, tokens, width),
+        room(*half_room),
+        room(*half_room),
+        room(*half_room),
+        f32_room(piece, max(columns, heads_width)),
+        room(micros, groups, 4, tokens, here),
+        room(micros, groups, 4, tokens, here),
+        room(micros, groups, 3, 4, tokens, here),
+        room(3, micros * 4, tokens, heads_width),
+        room(micros * 4, tokens, heads_width),
+        room(*token_rows),
+        room(3, 2, replicas, piece, heads_width),
+        room(1, groups, 3, 4, tokens, here),
+        *[room(*tables[0].shape)] * 3,
+        *[f32_room(*tables[0].shape)] * 2,
+        pltpu.SemaphoreType.DMA((128,)),
+        pltpu.SemaphoreType.DMA((128,)),
+        pltpu.SemaphoreType.DMA((384,)),
+    ]
+    results = pl.pallas_call(
+        functools.partial(back_kernel, (micros, groups, n_mlp, n_att)),
+        out_shape=outs,
+        in_specs=[any_space] * 7 + [in_vmem] * 4 + [any_space] * (n_mlp + n_att),
+        out_specs=[any_space] * len(outs),
+        scratch_shapes=scratch,
+        compiler_params=pltpu.CompilerParams(
+            collective_id=1, has_side_effects=True, vmem_limit_bytes=63 * 1024 * 1024
+        ),
+    )(partial, mixed, x2, grad_rows, normed_one, attended, sequences, g_rows, x_rows, *tables, *grads, *w_att)
+    own_mlp, results = results[:n_mlp], results[n_mlp:]
+    other_mlp, results = results[:n_mlp], results[n_mlp:]
+    own_att, results = results[:n_att], results[n_att:]
+    other_att, results = results[:n_att], results[n_att:]
+    return list(zip(own_mlp, other_mlp)), list(zip(own_att, other_att)), results[0]
 
 
 def scale_of(values):
@@ -793,23 +1203,14 @@
     mlp_in = jnp.stack(
         [columns_of(scaled(w, gain_two), 4) for w in (gate_weight, up_weight)] + [columns_of(down_weight.T, 4)]
     )
-    inputs_low = reorder(block_input.reshape(micros * tokens, width), to_own).reshape(micros, tokens, width)
-    w_att, w_mlp, held = front(inputs_low, att_in, mlp_in, tables)
-    normed_one_all, sequences, attended, mixed, normed_two_all = held
-    upper = lax.axis_index("blk") // 2
-    sequences = [lax.dynamic_index_in_dim(sequences, upper ^ r, 1, keepdims=False) for r in range(head_groups())]
-    sequences = jnp.concatenate(sequences, 2)
-    attended = jnp.concatenate([attended[:, g] for g in range(head_groups())], -1)
-    attended_all = attended.reshape(micros * 4 * tokens, -1)
-    normed_one_all = normed_one_all.reshape(-1, width)
-    normed_two_all = normed_two_all.reshape(-1, width)
+    block_rows = [array.reshape(micros * tokens, width) for array in (block_input, grad_output)]
+    inputs_low, grad_low = (rows.reshape(micros, tokens, width) for rows in reorder(to_own, *block_rows))
+    grad_turned = turn_features(grad_low.reshape(micros * tokens, width)).reshape(micros, tokens, width)
+    w_att, w_mlp, held = front(inputs_low, grad_low, grad_turned, att_in, mlp_in, tables)
+    normed_one, sequences, attended, mixed, normed_two, grad_rows = held
+    normed_two_all = normed_two.reshape(-1, width)
+    grad_rows_all = grad_rows.reshape(-1, width)
     gate_parts, up_parts, down_parts = w_mlp[0:4:2], w_mlp[1:4:2], w_mlp[4:]
-
-    grad_low = reorder(grad_output.reshape(micros * tokens, width), to_own).reshape(micros, tokens, width)
-    inputs = [inputs_low[m].astype(F32) for m in each]
-    scale_one = [scale_of(inputs[m]) for m in each]
-    scale_two = [scale_of(mixed[m]) for m in each]
-    grad_rows_all = joined([gather_tokens(grad_low[m], head_first[m]) for m in each])
 
     hidden, grad_gate, grad_up = [], [], []
     grad_normed = produced = 0.0
@@ -829,33 +1230,56 @@
         size = rows.shape[0] // micros
         return [rows[m * size : (m + 1) * size] for m in each]
 
-    grad_normed = split(grad_normed)
-    grad_mixed = []
-    for m in each:
-        back = norm_back(scatter_tokens(grad_normed[m], head_first[m]), mixed[m], scale_two[m])
-        grad_mixed.append(grad_low[m].astype(F32) + back)
     produced = split(produced)
     outputs = [(mixed[m] + scatter_tokens(produced[m], head_first[m])).astype(BF16) for m in each]
 
-    gate_grad = scatter_weight_grad(normed_two_all, jnp.concatenate(grad_gate, 1))
-    up_grad = scatter_weight_grad(normed_two_all, jnp.concatenate(grad_up, 1))
-    down_grad = scatter_weight_grad(grad_rows_all, jnp.concatenate(hidden, 1))
-
-    grad_mixed_rows = [gather_tokens(grad_mixed[m].astype(BF16), head_first[m]) for m in each]
-    grad_qkv, input_grads = [], []
-    for m in each:
-        grad_attended = matmul(grad_mixed_rows[m], w_att[3]).astype(BF16)
-        grad_sequences = attention_call(order, sequences[m], tables, to_sequences([grad_attended])[0])
-        returned = from_sequences(grad_sequences)
-        grad_qkv.append(jnp.concatenate([returned[0], returned[1], returned[2]], 1))
-        grad_normed = scatter_tokens(functools.reduce(jnp.add, [matmul_nt(returned[i], w_att[i]) for i in range(3)]), head_first[m])
-        input_grads.append((grad_mixed[m] + norm_back(grad_normed, inputs[m], scale_one[m])).astype(BF16))
-    output_grad = scatter_weight_grad(joined(grad_mixed_rows), attended_all)
-    qkv_grad = scatter_weight_grad(normed_one_all, joined(grad_qkv))
-
-    qkv_grads = [
-        side_by_side(*(side[:, i * heads_width : (i + 1) * heads_width] for side in qkv_grad)) for i in range(3)
-    ]
+    if sequences.shape[-1] % LANES == 0 and micros * 4 * tokens == width // 2:
+        mlp_pairs, att_pairs, input_grads = back(
+            grad_normed.astype(BF16).reshape(normed_two.shape), mixed, normed_two, grad_rows, normed_one, attended,
+            sequences, grad_low, inputs_low, tables,
+            [grad_gate[0], grad_up[0], grad_gate[1], grad_up[1], hidden[0], hidden[1]], w_att,
+        )
+        input_grads = [input_grads[m] for m in each]
+
+        def beside(pairs):
+            return tuple(jnp.concatenate(side, 1) for side in zip(*pairs))
+
+        gate_grad, up_grad, down_grad = beside(mlp_pairs[0:4:2]), beside(mlp_pairs[1:4:2]), beside(mlp_pairs[4:])
+        output_grad = att_pairs[3]
+        qkv_grads = [side_by_side(*pair) for pair in att_pairs[:3]]
+    else:
+        upper = lax.axis_index("blk") // 2
+        w_att = [w.reshape(width, -1) for w in w_att]
+        normed_one_all = normed_one.reshape(-1, width)
+        sequences = [lax.dynamic_index_in_dim(sequences, upper ^ r, 1, keepdims=False) for r in range(head_groups())]
+        sequences = jnp.concatenate(sequences, 2)
+        attended = jnp.concatenate([attended[:, g] for g in range(head_groups())], -1)
+        attended_all = attended.reshape(micros * 4 * tokens, -1)
+        grad_normed = split(grad_normed)
+        grad_mixed = []
+        for m in each:
+            back_rows = norm_back(scatter_tokens(grad_normed[m], head_first[m]), mixed[m], scale_of(mixed[m]))
+            grad_mixed.append(grad_low[m].astype(F32) + back_rows)
+        gate_grad = scatter_weight_grad(normed_two_all, jnp.concatenate(grad_gate, 1))
+        up_grad = scatter_weight_grad(normed_two_all, jnp.concatenate(grad_up, 1))
+        down_grad = scatter_weight_grad(grad_rows_all, jnp.concatenate(hidden, 1))
+        grad_mixed_rows = [gather_tokens(grad_mixed[m].astype(BF16), head_first[m]) for m in each]
+        grad_qkv, input_grads = [], []
+        for m in each:
+            grad_attended = matmul(grad_mixed_rows[m], w_att[3]).astype(BF16)
+            grad_sequences = attention_call(order, sequences[m], tables, to_sequences([grad_attended])[0])
+            returned = from_sequences(grad_sequences)
+            grad_qkv.append(jnp.concatenate([returned[0], returned[1], returned[2]], 1))
+            terms = [matmul_nt(returned[i], w_att[i]) for i in range(3)]
+            grad_normed_one = scatter_tokens(functools.reduce(jnp.add, terms), head_first[m])
+            inputs = inputs_low[m].astype(F32)
+            back_rows = norm_back(grad_normed_one, inputs, scale_of(inputs))
+            input_grads.append((grad_mixed[m] + back_rows).astype(BF16))
+        output_grad = scatter_weight_grad(joined(grad_mixed_rows), attended_all)
+        qkv_grad = scatter_weight_grad(normed_one_all, joined(grad_qkv))
+        qkv_grads = [
+            side_by_side(*(side[:, i * heads_width : (i + 1) * heads_width] for side in qkv_grad)) for i in range(3)
+        ]
     mlp_grads = [side_by_side(*gate_grad), side_by_side(*up_grad)]
 
     def gain_grad(weights, grads):
@@ -865,14 +1289,11 @@
 
     attention_gain_grad = gain_grad((query_weight, key_weight, value_weight), qkv_grads)
     mlp_gain_grad = gain_grad((gate_weight, up_weight), mlp_grads)
-
-    def absolute(parts):
-        rows = reorder(joined(parts), to_absolute)
-        return rows.reshape(micros, 1, tokens, width)
+    block_output, input_grad = reorder(to_absolute, joined(outputs), joined(input_grads))
 
     return (
-        absolute(outputs),
-        absolute(input_grads),
+        block_output.reshape(micros, 1, tokens, width),
+        input_grad.reshape(micros, 1, tokens, width),
         attention_gain_grad,
         qkv_grads[0] * gain_one,
         qkv_grads[1] * gain_one,

time: 1220 us -> 926 us (0.76)
  waiting for transfers between devices: 329 us -> 4.49 us
  Pallas kernels: 453 us -> 770 us
  matrix products: 238 us -> 91.3 us
  starting transfers between devices: 63.5 us -> 6.15 us
  local copies, waits for them, and re-layouts: 57.1 us -> 14.2 us
  other arithmetic: 62.4 us -> 28.7 us
    pallas_call x6 -> x3, Pallas kernels: 80.4 us -> 393 us  [the longest x1 386 us: back(): pl.pallas_call(functools.partial(back_kernel, (micros, groups, n_mlp, n_a...]
    ppermute x57 -> x6, waiting for transfers between devices: 284 us -> 4.49 us  [swap(): return lax.ppermute(value, axis, [(i, i ^ bit) for i in range(count)])]
    dot_general x20 -> x0, matrix products: 121 us -> none  [matmul_tn(): lax.dot_general(left_side, right_side, (((0,), (0,)), ((), ())), preferre...]
    ppermute x57 -> x6, starting transfers between devices: 59.4 us -> 6.15 us  [swap(): return lax.ppermute(value, axis, [(i, i ^ bit) for i in range(count)])]
    ppermute x4 -> x0, waiting for transfers between devices: 45.8 us -> none  [the longest x2 45.8 us: to_sequences(): lax.ppermute(chosen, 'blk', [(i, i ^ 2 * r) for i in range(2 * groups)])]
    unnamed x213 -> x91, local copies, waits for them, and re-layouts: 22.7 us -> 5.12 us
    dot_general x8 -> x6, matrix products: 57.3 us -> 40.3 us  [matmul(): return jnp.dot(left_side, right_side, preferred_element_type=F32)]
    dot_general x12 -> x6, matrix products: 59.8 us -> 51 us  [matmul_nt(): lax.dot_general(left_side, right_side, (((1,), (1,)), ((), ())), preferre...]
  transfers between devices with their start and end apart: 61 -> 6, of which waited for: 27 -> 2; matrix products, arithmetic and copies ran while one was open for 23% -> 6% of each run, Pallas kernels for 37% -> 42%
where the time goes in v3:
time: 926 us; the launch traced here: 917 us
  Pallas kernels  770 us (83%)
  matrix products  91.3 us (10%)
  other arithmetic  28.7 us (3%)
  local copies, waits for them, and re-layouts  14.2 us (2%)
    pallas_call x1, Pallas kernels, back(): pl.pallas_call(functools.partial(back_kernel, (micros, groups, n_mlp, n_a...  386 us
    pallas_call x1, Pallas kernels, front(): pl.pallas_call(functools.partial(front_kernel, (micros, groups, n_att, n_...  378 us
    dot_general x6, matrix products, matmul_nt(): lax.dot_general(left_side, right_side, (((1,), (1,)), ((), ())), preferre...  51 us
    dot_general x6, matrix products, matmul(): return jnp.dot(left_side, right_side, preferred_element_type=F32)  40.3 us
  transfers between devices with their start and end apart: 6, of which 2 were waited for; matrix products, arithmetic and copies ran while one was open for 6% of the time, Pallas kernels for 42%

profile of v3, /device:TPU:0, one launch (start us, length us, event | category | flops | bytes accessed | tf_op | source)
XLA Modules:
  0.0 917.0 jit_solution(7202041781322702392)
XLA Ops:
  3.8 2.1 fusion.11
  8.7 3.5 shard_map.230
  16.3 2.0 pad_maximum_fusion.refs_4_
  19.4 377.6 %shard_map.231 = (bf16[2,8,128,512]{3,2,1,0:T(8,128)(2,1)}, bf16[2,8,128,512]{3,2,1,0:T(8,128)(2,1)}, bf16[2,8,128,512]{3,2,1,0:T(8,128)(2,1)}, bf16[2,8,128,512...) custom-call(bf16[2,128,2048]{2,1,0:T(8,128)(2,1)} %bitcast.123, ...), custom_call_target="tpu_custom_call" | custom-call | tf_op jit(solution)/shard_map/pallas_call | solution.py:754
  397.1 8.2 fusion.26
  405.3 4.5 fusion.25
  409.8 7.4 multiply_convert_fusion.2
  417.2 6.8 fusion.27
  424.0 4.5 fusion.28
  428.5 6.4 fusion.29
  434.9 9.4 %multiply_convert_fusion = (bf16[1024,1024]{1,0:T(8,128)(2,1)}, bf16[1024,1024]{1,0:T(8,128)(2,1)}, bf16[1024,1024]{1,0:T(8,128)(2,1)S(1)}) fusion(f32[1024,1024]{1,0:T(8,128)S(1)} %fusion.28, f32[1024,1024]{1,0:T(8,128)} %fusion.29, bf16[1024,2048]{1,0:T(8,128)(2,1)S(1)} %bitcast.118, bf16[2048,1024]{1,0:T(8,128)(2,1)S(1)} %bitcast.143), kind=kOutput, calls=%fused_computation.3 | convolution fusion | flops 4310695936 | bytes 23068672 | tf_op jit(solution)/shard_map/dot_general | solution.py:36
  444.3 7.8 add_convert_fusion.1
  455.3 9.1 fusion.31
  464.4 6.8 fusion.30
  471.2 7.2 fusion.32
  478.4 13.4 %add_convert_fusion = bf16[1024,2048]{1,0:T(8,128)(2,1)} fusion(f32[1024,2048]{1,0:T(8,128)} %fusion.32, f32[1024,2048]{1,0:T(8,128)} %fusion.30, f32[1024,2048]{1,0:T(8,128)} %fusion.31, bf16[1024,1024]{1,0:T(8,128)(2,1)S(1)} %copy-done.12, bf16[2048,1024]{1,0:T(8,128)(2,1)} %bitcast.135), kind=kOutput, calls=%fused_computation.1 | convolution fusion | flops 4303355904 | bytes 35651584 | tf_op jit(solution)/shard_map/dot_general | solution.py:40
  491.8 385.8 %shard_map.232 = (f32[128,1024]{1,0:T(8,128)}, f32[128,1024]{1,0:T(8,128)}, f32[128,1024]{1,0:T(8,128)}, f32[128,1024]{1,0:T(8,128)}, f32[128,1024]{1,0:T(8,128)...) custom-call(bf16[2,2,2,128,2048]{4,3,2,1,0:T(8,128)(2,1)} %bitcast.1, ...), custom_call_target="tpu_custom_call" | custom-call | tf_op jit(solution)/shard_map/pallas_call | solution.py:1139
  885.1 2.8 fusion.6
  890.8 2.7 add_convert_fusion.3
  894.3 2.5 collective-permute-start.3
  900.2 2.9 copy.45
  905.2 2.9 collective-permute-done.3
  909.7 2.3 fusion.10
  913.1 3.5 shard_map.233
  (141 shorter events, 33.4 us)
Async XLA Ops:
  0.6 7.5 copy-start.42
  8.1 7.4 copy-start.5
  8.1 7.4 copy-start.7
  397.0 8.2 copy-start.2
  397.0 8.2 copy-start.38
  417.2 6.8 copy-start.11
  417.2 38.1 %copy-start.9 = (bf16[1024,1024]{1,0:T(8,128)(2,1)}, bf16[1024,1024]{1,0:T(8,128)(2,1)S(1)}, u32[]{:S(2)}) copy-start(bf16[1024,1024]{1,0:T(8,128)(2,1)S(1)} %get-tuple-element.118.refs_12_) | copy-start | bytes 6291460
  417.2 6.8 copy-start.36
  444.3 7.8 copy-start.14
  453.5 437.3 %collective-permute-start = (bf16[256,2048]{1,0:T(8,128)(2,1)}, bf16[256,2048]{1,0:T(8,128)(2,1)}, u32[]{:S(2)}, u32[]{:S(2)}) collective-permute-start(bf16[256,2048]{1,0:T(8,128)(2,1)} %fusion.8), channel_id=1, source_target_pairs={{0,1},{1,0},{2,3},{3,2},{4,5},{5,4},{6,7},{7,6},{8,9},{9,8},{10,11... | collective-permute-start | bytes 3145736 | tf_op jit(solution)/shard_map/ppermute | solution.py:23
  454.7 436.1 %collective-permute-start.2 = (bf16[256,2048]{1,0:T(8,128)(2,1)}, bf16[256,2048]{1,0:T(8,128)(2,1)}, u32[]{:S(2)}, u32[]{:S(2)}) collective-permute-start(bf16[256,2048]{1,0:T(8,128)(2,1)} %slice.106), channel_id=1, source_target_pairs={{0,4},{4,0},{1,5},{5,1},{2,6},{6,2},{3,7},{7,3},{8,12},{12,8},{9,1... | collective-permute-start | bytes 3145736 | tf_op jit(solution)/shard_map/ppermute | solution.py:23
  455.3 9.1 copy-start.10
  455.3 9.1 copy-start.39
  464.4 6.8 copy-start.13
  464.4 6.8 copy-start.37
  471.2 7.2 copy-start.12
  491.8 389.1 %copy-start.16 = (bf16[128,1024]{1,0:T(8,128)(2,1)S(1)}, bf16[128,1024]{1,0:T(8,128)(2,1)}, u32[]{:S(2)}) copy-start(bf16[128,1024]{1,0:T(8,128)(2,1)} %param.17) | copy-start | bytes 786436
  491.8 389.1 %copy-start.17 = (bf16[128,1024]{1,0:T(8,128)(2,1)S(1)}, bf16[128,1024]{1,0:T(8,128)(2,1)}, u32[]{:S(2)}) copy-start(bf16[128,1024]{1,0:T(8,128)(2,1)} %param.18) | copy-start | bytes 786436
  491.8 389.1 %copy-start.18 = (bf16[128,1024]{1,0:T(8,128)(2,1)S(1)}, bf16[128,1024]{1,0:T(8,128)(2,1)}, u32[]{:S(2)}) copy-start(bf16[128,1024]{1,0:T(8,128)(2,1)} %param.19) | copy-start | bytes 786436
  882.3 21.9 %collective-permute-start.4 = (f32[128]{0:T(128)S(1)}, f32[128]{0:T(128)S(1)}, u32[]{:S(2)}, u32[]{:S(2)}) collective-permute-start(f32[128]{0:T(128)S(1)} %add_add_fusion), channel_id=1, source_target_pairs={{0,4},{4,0},{1,5},{5,1},{2,6},{6,2},{3,7},{7,3},{8,12},{12,8},{9,1... | collective-permute-start | bytes 1544 | tf_op jit(solution)/shard_map/ppermute | solution.py:23
  888.0 16.8 %collective-permute-start.5 = (f32[128]{0:T(128)S(1)}, f32[128]{0:T(128)S(1)}, u32[]{:S(2)}, u32[]{:S(2)}) collective-permute-start(f32[128]{0:T(128)S(1)} %add.108), channel_id=1, source_target_pairs={{0,4},{4,0},{1,5},{5,1},{2,6},{6,2},{3,7},{7,3},{8,12},{12,8},{9,1... | collective-permute-start | bytes 1544 | tf_op jit(solution)/shard_map/ppermute | solution.py:23
  894.3 13.8 %collective-permute-start.3 = (bf16[128,2048]{1,0:T(8,128)(2,1)}, bf16[128,2048]{1,0:T(8,128)(2,1)S(1)}, u32[]{:S(2)}, u32[]{:S(2)}) collective-permute-start(bf16[128,2048]{1,0:T(8,128)(2,1)} %pad_maximum_fusion.8), channel_id=1, source_target_pairs={{0,1},{1,0},{2,3},{3,2},{4,5},{5,4},{6,7},{7,6},{8,9},{9,8},{10,11... | collective-permute-start | bytes 1572872 | tf_op jit(solution)/shard_map/ppermute | solution.py:23
  896.9 12.8 %collective-permute-start.1 = (bf16[128,2048]{1,0:T(8,128)(2,1)}, bf16[128,2048]{1,0:T(8,128)(2,1)}, u32[]{:S(2)}, u32[]{:S(2)}) collective-permute-start(bf16[128,2048]{1,0:T(8,128)(2,1)} %get-tuple-element.123), channel_id=1, source_target_pairs={{0,4},{4,0},{1,5},{5,1},{2,6},{6,2},{3,7},{7,3},{8,12},{12,8},{9,1... | collective-permute-start | bytes 1572872 | tf_op jit(solution)/shard_map/ppermute | solution.py:23
  897.7 12.0 %copy-start.1 = (f32[2,128,2048]{2,1,0:T(8,128)S(1)}, f32[2,128,2048]{2,1,0:T(8,128)}, u32[]{:S(2)}) copy-start(f32[2,128,2048]{2,1,0:T(8,128)} %get-tuple-element.54.refs_1_) | copy-start | bytes 6291460
  (25 other events, 87.9 us)

commit v4 on v3

--- a/solution.py
+++ b/solution.py
@@ -409,14 +409,15 @@
 
 
 class TokenGather:
-    def __init__(self, copies, rows, turned_rows, m):
+    def __init__(self, copies, rows, turned_rows, m, head_first=None):
         self.copies, self.rows, self.turned_rows, self.m = copies, rows, turned_rows, m
-        self.head_first = m % 2 == 1
+        self.head_first = m % 2 == 1 if head_first is None else head_first
         if self.head_first:
             self.copy = copies.remote(rows.at[m, 0, 0], rows.at[m, 1, 0], "head", 1)
         else:
             turned_rows[m, 0] = halves_turned(rows[m, 0, 0])
             self.copy = copies.remote(turned_rows.at[m, 0], rows.at[m, 0, 1], "blk", 1)
+        self.first = self.copy
 
     def second(self):
         m, rows, turned_rows = self.m, self.rows, self.turned_rows
@@ -431,12 +432,16 @@
     def end(self):
         self.copy.wait_recv()
 
+    def release(self):
+        self.copies.wait_sent(self.first)
+        self.copies.wait_sent(self.copy)
+
 
 class TokenScatter:
-    def __init__(self, copies, partial, leaving, came, passing, last, total, m):
+    def __init__(self, copies, partial, leaving, came, passing, last, total, m, head_first=None):
         self.copies, self.partial, self.came, self.passing = copies, partial, came, passing
         self.last, self.total, self.m = last, total, m
-        self.head_first = m % 2 == 0
+        self.head_first = m % 2 == 0 if head_first is None else head_first
         if self.head_first:
             self.copy = copies.remote(partial.at[m, 1], came.at[m], "head", 1)
         else:
@@ -766,64 +771,92 @@
     return w_att, [w.reshape(width, -1) for w in w_mlp], results
 
 
-class GradScatter:
-    def __init__(self, copies, kept, first_copy, landed, room, final, own, other):
-        self.copies, self.kept, self.copy, self.landed = copies, kept, first_copy, landed
-        self.room, self.final, self.own, self.other = room, final, own, other
-        self.stage = 0
-
-    def advance(self):
-        copies, kept, stage = self.copies, self.kept, self.stage
-        stages = replica_stages()[::-1]
-        self.copy.wait_recv()
-        self.stage += 1
-        if stage == len(stages):
-            return
-        count = kept.shape[1] >> stage
-        columns = kept.shape[-1]
-        mine, came = (part.at[:, 0:count, :, 0:columns] for part in self.room)
-        loads = [copies.inside(kept.at[:, 0:count], mine), copies.inside(self.landed[stage], came)]
-        for load in loads:
-            load.wait()
-        if stage == len(stages) - 1:
-            self.final[:, 0:columns] = mine[0, 0].astype(F32) + came[0, 0].astype(F32)
-            mine[1, 0] = (mine[1, 0].astype(F32) + came[1, 0].astype(F32)).astype(BF16)
-            stores = [
-                copies.inside(self.final.at[:, 0:columns], self.own),
-                copies.inside(mine.at[1, 0], kept.at[1, 0]),
-            ]
-            for store in stores:
-                store.wait()
-            self.copy = copies.remote(kept.at[1, 0], self.other, "blk", 1)
-            return
-
-        def one(i, carry):
-            half, row = i // count, i % count
-            mine[half, row] = (mine[half, row].astype(F32) + came[half, row].astype(F32)).astype(BF16)
-            return carry
-
-        lax.fori_loop(0, 2 * count, one, 0)
-        copies.inside(mine, kept.at[:, 0:count]).wait()
-        self.copy = copies.remote(
-            kept.at[:, count // 2 : count], self.landed[stage + 1], *stages[stage + 1]
-        )
-
-
-def attend_back(seq, seq_at, grad, out, m, cosine_ref, sine_ref, held, sums):
-    tokens, width = seq.shape[-2:]
+def absolute_block(place):
+    stages = replica_stages()
+    n_blk = lax.axis_size("blk")
+    bits = [("blk", 1, place >> len(stages) & 1)] + [(a, bit, place >> s & 1) for s, (a, bit) in enumerate(stages)]
+    block = 0
+    for axis, bit, here in bits:
+        digit = (lax.axis_index(axis) // bit) % 2
+        block = block + bit * ((1 - digit) if here else digit) * (1 if axis == "blk" else n_blk)
+    return block
+
+
+def feature_lanes(place, piece):
+    return pl.ds(pl.multiple_of(absolute_block(place) * piece, piece), piece)
+
+
+def to_own_order(read, width, piece):
+    return jnp.concatenate([read(feature_lanes(j, piece)) for j in range(width // piece)], 1)
+
+
+def to_absolute_order(rows, target, at, piece):
+    for j in range(rows.shape[1] // piece):
+        target[at, :, feature_lanes(j, piece)] = rows[:, j * piece : (j + 1) * piece]
+
+
+def part_of(block):
+    n_blk = lax.axis_size("blk")
+    head, blk = block // n_blk, block % n_blk
+    mine = lax.axis_index("blk")
+    near = (blk + mine) % 2
+    return (blk // 2 + mine // 2) % 2, ((head + lax.axis_index("head")) % 2) * 2 + near
+
+
+def load_pair_heads(seq, lane, cosine_ref, sine_ref, held):
+    tokens = seq.shape[-2]
+    lanes = held[0].shape[1]
+    blocks = held[0].shape[0] // tokens
+
+    def one(block, carry):
+        part, group = part_of(block)
+        rows = pl.ds(pl.multiple_of(block * tokens, tokens), tokens)
+        for i in range(3):
+            value = seq[i, part, group, :, pl.ds(lane, lanes)]
+            if i < 2:
+                value = turned(value.astype(F32), cosine_ref[rows, :], sine_ref[rows, :]).astype(BF16)
+            held[i][rows, :] = value
+        return carry
+
+    lax.fori_loop(0, blocks, one, 0)
+
+
+def attend_pair(seq, out, lane, cosine_ref, sine_ref, held):
+    tokens = seq.shape[-2]
+    q_s, k_s, v_s = held
+    length, lanes = q_s.shape
+    rows_at_once = min(256, length)
+    load_pair_heads(seq, lane, cosine_ref, sine_ref, held)
+    for first in range(0, length, rows_at_once):
+        last = first + rows_at_once
+        results = []
+        for start in range(0, lanes, HD):
+            head = slice(start, start + HD)
+            weights, inverse = softmax_rows(q_s[first:last, head], k_s[:last, head], first)
+            results.append(matmul(weights.astype(BF16), v_s[:last, head]) * inverse)
+        result = jnp.concatenate(results, 1).astype(BF16)
+        for offset in range(0, rows_at_once, tokens):
+            part, group = part_of((first + offset) // tokens)
+            out[part, group, :, pl.ds(lane, lanes)] = result[offset : offset + tokens]
+
+
+def attend_pair_back(seq, grad, out, lane, cosine_ref, sine_ref, held, sums):
+    tokens = seq.shape[-2]
     q_s, k_s, v_s = held
     dk_s, dv_s = sums
     length, lanes = q_s.shape
     rows_at_once = min(256, length)
-
-    def rows_of(first, last, lane):
-        places = [place_of((first + offset) // tokens) for offset in range(0, rows_at_once, tokens)]
-        grad_rows = jnp.concatenate([grad[m, u, g, :, pl.ds(lane, lanes)] for u, g in places], 0)
-        rows = pl.ds(first, rows_at_once)
+    load_pair_heads(seq, lane, cosine_ref, sine_ref, held)
+    dk_s[...] = jnp.zeros_like(dk_s)
+    dv_s[...] = jnp.zeros_like(dv_s)
+    for first in range(0, length, rows_at_once):
+        last = first + rows_at_once
+        places = [part_of((first + offset) // tokens) for offset in range(0, rows_at_once, tokens)]
+        grad_rows = jnp.concatenate([grad[p, g, :, pl.ds(lane, lanes)] for p, g in places], 0)
         query_parts, key_parts, value_parts = [], [], []
         for start in range(0, lanes, HD):
             head = slice(start, start + HD)
-            query, keys, grad_part = q_s[rows, head], k_s[:last, head], grad_rows[:, head]
+            query, keys, grad_part = q_s[first:last, head], k_s[:last, head], grad_rows[:, head]
             weights, inverse = softmax_rows(query, keys, first)
             probabilities = weights * inverse
             grad_prob = matmul_nt(grad_part, v_s[:last, head])
@@ -833,67 +866,434 @@
             key_parts.append(matmul_tn(grad_scores, query))
             value_parts.append(matmul_tn(probabilities.astype(BF16), grad_part))
         grad_query = jnp.concatenate(query_parts, 1)
-        grad_query = turned(grad_query, cosine_ref[rows, :], -sine_ref[rows, :]).astype(BF16)
-        for i, (u, g) in enumerate(places):
-            out[m, u, 0, g, :, pl.ds(lane, lanes)] = grad_query[i * tokens : (i + 1) * tokens]
+        grad_query = turned(grad_query, cosine_ref[first:last, :], -sine_ref[first:last, :]).astype(BF16)
+        for i, (p, g) in enumerate(places):
+            out[0, p * 4 + g, :, pl.ds(lane, lanes)] = grad_query[i * tokens : (i + 1) * tokens]
         dk_s[:last, :] += jnp.concatenate(key_parts, 1)
         dv_s[:last, :] += jnp.concatenate(value_parts, 1)
 
-    def heads(lane):
-        load_heads(seq, seq_at, lane, cosine_ref, sine_ref, held)
-        dk_s[...] = jnp.zeros_like(dk_s)
-        dv_s[...] = jnp.zeros_like(dv_s)
-        over_rows(length, rows_at_once, lambda first, last: rows_of(first, last, lane))
-
-        def one(block, carry):
-            u, g = place_of(block)
-            rows = pl.ds(pl.multiple_of(block * tokens, tokens), tokens)
-            grad_key = turned(dk_s[rows, :], cosine_ref[rows, :], -sine_ref[rows, :])
-            out[m, u, 1, g, :, pl.ds(lane, lanes)] = grad_key.astype(BF16)
-            out[m, u, 2, g, :, pl.ds(lane, lanes)] = dv_s[rows, :].astype(BF16)
+    def one(block, carry):
+        p, g = part_of(block)
+        rows = pl.ds(pl.multiple_of(block * tokens, tokens), tokens)
+        grad_key = turned(dk_s[rows, :], cosine_ref[rows, :], -sine_ref[rows, :])
+        out[1, p * 4 + g, :, pl.ds(lane, lanes)] = grad_key.astype(BF16)
+        out[2, p * 4 + g, :, pl.ds(lane, lanes)] = dv_s[rows, :].astype(BF16)
+        return carry
+
+    lax.fori_loop(0, length // tokens, one, 0)
+
+
+def greet_pairs():
+    masks = [("head", 1)] + [(axis, bit) for axis in ("blk", "dp") for bit in bits_of(lax.axis_size(axis))]
+    barrier = pltpu.get_barrier_semaphore()
+    for axis, mask in masks:
+        pl.semaphore_signal(barrier, inc=1, device_id={axis: flipped(axis, mask)}, device_id_type=MESH)
+    pl.semaphore_wait(barrier, len(masks))
+
+
+def up_to(chunk, stage):
+    while chunk.stage < stage:
+        chunk.advance()
+
+
+def store_product(product, target, part, columns):
+    tokens = target.shape[-2]
+    for group in range(4):
+        target[part, group // 2, group % 2, :, columns] = product[group * tokens : (group + 1) * tokens]
+
+
+def pair_front_kernel(sizes, *refs):
+    n_att, n_mlp = sizes
+    x_in, g_in, att_in, mlp_in, cosine_ref, sine_ref = refs[:6]
+    refs = refs[6:]
+    w_att, refs = refs[:n_att], refs[n_att:]
+    (w_gu, w_down, grads_out, hidden_out), refs = refs[:4], refs[4:]
+    xg_out, seq_out, attended_out, mixed_out, x2_out, gg_out, x_out, g_out = refs[:8]
+    (x_raw, g_raw, x_own, g_own, g_turned, xg, x2, turned_rows, turned_more, w_in, w_out, seq, attended, partial,
+     leaving, came, passing, last, mixed, slopes, activated, q_s, k_s, v_s, send, recv, local) = refs[8:]
+    held = (q_s, k_s, v_s)
+    near = lax.axis_index("blk") % 2
+    upper = lax.axis_index("blk") // 2
+    tokens, width = x_own.shape[-2:]
+    heads_width = w_in.shape[-1]
+    count = 4 * tokens
+    piece = w_in.shape[-2]
+    copies = Copies(send, recv, local)
+    stages = len(replica_stages())
+
+    loads = [copies.inside(x_in.at[upper, 0], x_raw.at[0]), copies.inside(g_in.at[upper, 0], g_raw.at[0])]
+    greet_pairs()
+    trade = copies.remote(x_in.at[1 - upper, 0], x_raw.at[1], "blk", 2)
+
+    def att_chunk(i):
+        return lambda: WeightGather(copies, att_in.at[i, near], att_in.at[i, 1 - near], w_att[i])
+
+    def mlp_chunk(i):
+        per_weight = n_mlp // 3
+        w, j = (i % 2, i // 2) if i < 2 * per_weight else (2, i - 2 * per_weight)
+        size = mlp_in.shape[-1]
+        if w < 2:
+            full = w_gu.at[:, :, :, i * size : (i + 1) * size]
+        else:
+            full = w_down.at[:, :, :, j * size : (j + 1) * size]
+        own, other = near * per_weight + j, (1 - near) * per_weight + j
+        return lambda: WeightGather(copies, mlp_in.at[w, own], mlp_in.at[w, other], full)
+
+    makers = [att_chunk(i) for i in range(n_att)] + [mlp_chunk(i) for i in range(n_mlp)]
+    chunks = []
+
+    def reach(k, stage):
+        if 0 <= k < len(makers):
+            while len(chunks) <= k:
+                chunks.append(makers[len(chunks)]())
+            up_to(chunks[k], stage)
+
+    def step(k):
+        reach(k - 2, stages + 1)
+        reach(k - 1, 3)
+        reach(k, 2)
+        reach(k + ahead[0], 1)
+        reach(k + 3, 0)
+
+    ahead = [1]
+
+    reach(n_att - 1, 0)
+    reach(0, 1)
+
+    def own_rows(p):
+        x_own[p] = to_own_order(lambda lanes: x_raw[p, :, lanes], width, piece)
+        store_normed(x_own[p].astype(F32), xg, (p, 0, 0))
+        return TokenGather(copies, xg, turned_rows, p, False)
+
+    loads[0].wait()
+    gathers = [own_rows(0)]
+    step(0)
+    gathers[0].second()
+    step(1)
+    trade.wait_recv()
+    gathers.append(own_rows(1))
+    step(2)
+    w_loads = []
+
+    def load_weight(i):
+        reach(i, stages + 1)
+        w_loads.append(copies.inside(w_att[i], w_in.at[i] if i < 3 else w_out))
+
+    def project(i, p):
+        rows = xg[p].reshape(count, width)
+        for start in range(0, heads_width, 256):
+            columns = w_in[i, :, :, :, start : start + 256].reshape(width, 256)
+            product = matmul(rows, columns).astype(BF16)
+            for group in range(4):
+                seq[i, p, group, :, start : start + 256] = product[group * tokens : (group + 1) * tokens]
+
+    gathers[1].second()
+    step(3)
+    trade = copies.remote(g_in.at[1 - upper, 0], g_raw.at[1], "blk", 2)
+    loads[1].wait()
+    for i in range(3):
+        load_weight(i)
+    gathers[0].end()
+    for i in range(3):
+        w_loads[i].wait()
+        project(i, 0)
+    gathers[1].end()
+    for i in range(3):
+        project(i, 1)
+    store_xg = copies.inside(xg, xg_out)
+    writes = [copies.inside(seq, seq_out), copies.inside(x_own, x_out)]
+    first_gathers = gathers
+    trade.wait_recv()
+    ahead[0] = 2
+    reach(5, 1)
+    grad_rows = []
+    for p in range(2):
+        g_own[p] = to_own_order(lambda lanes, p=p: g_raw[p, :, lanes], width, piece)
+        g_turned[p] = halves_turned(g_own[p])
+        mine = copies.inside(g_own.at[p], gg_out.at[p, 0, 0])
+        grad_rows.append((mine, copies.remote(g_turned.at[p], gg_out.at[p, 0, 1], "blk", 1)))
+    writes.append(copies.inside(g_own, g_out))
+    lanes = q_s.shape[1]
+    for at, lane in enumerate(range(0, heads_width, lanes)):
+        attend_pair(seq, attended, lane, cosine_ref, sine_ref, held)
+        if at == 1:
+            step(4)
+    load_weight(3)
+    w_loads[3].wait()
+    scatters = []
+    for p in range(2):
+        rows = attended[p].reshape(count, heads_width)
+        for start in range(0, width, 256):
+            half, first = start // (width // 2), start // piece % (width // piece // 2)
+            part = w_out[half, first : first + 256 // piece].reshape(256, heads_width)
+            store_product(matmul_nt(rows, part).astype(BF16), partial, p, slice(start, start + 256))
+        mixed[p] = x_own[p].astype(F32)
+        scatters.append(TokenScatter(copies, partial, leaving, came, passing, last, mixed, p))
+    writes.append(copies.inside(attended, attended_out))
+    step(5)
+    for scatter in scatters:
+        scatter.second()
+    far = []
+    for p, (mine, turned_copy) in enumerate(grad_rows):
+        mine.wait()
+        turned_copy.wait_recv()
+        far.append(copies.remote(gg_out.at[p, 0], gg_out.at[p, 1], "head", 1))
+    gathers = []
+    for p in range(2):
+        scatters[p].end()
+        store_normed(mixed[p], x2, (p, 0, 0))
+        gathers.append(TokenGather(copies, x2, turned_more, p))
+    writes.append(copies.inside(mixed, mixed_out))
+    step(6)
+    for gather in gathers:
+        gather.second()
+    step(7)
+    for gather in gathers:
+        gather.end()
+    writes.append(copies.inside(x2, x2_out))
+    store_xg.wait()
+    for gather in first_gathers:
+        gather.release()
+    for scatter in scatters:
+        scatter.release()
+    for copy in far:
+        copy.wait_recv()
+    load_rows = [copies.inside(gg_out, xg)]
+    hidden = partial
+    quarters = range(0, 2 * heads_width, heads_width)
+    size = 2 * heads_width
+
+    def tiles(body):
+        def one(i, carry):
+            body(i // 2, i % 2)
             return carry
 
-        lax.fori_loop(0, length // tokens, one, 0)
-
-    over_lanes(width, lanes, heads)
-
-
-def back_kernel(sizes, *refs):
-    micros, groups, n_mlp, n_att = sizes
+        lax.fori_loop(0, 4, one, 0)
+
+    def forward(j):
+        for lane in quarters:
+            sources = [w_gu.at[:, :, :, (2 * j + w) * size + lane : (2 * j + w) * size + lane + heads_width] for w in (0, 1)]
+            loads = [copies.inside(source, w_in.at[w]) for w, source in enumerate(sources)]
+            for load in loads:
+                load.wait()
+            lanes = slice(j * size + lane, j * size + lane + heads_width)
+
+            def body(p, head, lanes=lanes):
+                rows = x2[p, head].reshape(2 * tokens, width)
+                gate = matmul(rows, w_in[0].reshape(width, heads_width))
+                up = matmul(rows, w_in[1].reshape(width, heads_width))
+                sigmoid = jax.nn.sigmoid(gate)
+                active = gate * sigmoid
+                slope = up * sigmoid * (1.0 + gate * (1.0 - sigmoid))
+                shape = (2, tokens, heads_width)
+                slopes[p, head, :, :, lanes] = slope.astype(BF16).reshape(shape)
+                activated[p, head, :, :, lanes] = active.astype(BF16).reshape(shape)
+                hidden[p, head, :, :, lanes] = (active * up).astype(BF16).reshape(shape)
+
+            tiles(body)
+        here = slice(j * size, (j + 1) * size)
+        writes.append(copies.inside(hidden.at[:, :, :, :, here], hidden_out.at[:, :, :, :, here]))
+
+    def backward(j):
+        for lane in quarters:
+            lanes = slice(j * size + lane, j * size + lane + heads_width)
+            copies.inside(w_down.at[:, :, :, lanes], w_in.at[2]).wait()
+
+            def body(p, head, lanes=lanes):
+                rows = xg[p, head].reshape(2 * tokens, width)
+                grad_hidden = matmul(rows, w_in[2].reshape(width, heads_width)).reshape(2, tokens, heads_width)
+                slopes[p, head, :, :, lanes] = (grad_hidden * slopes[p, head, :, :, lanes].astype(F32)).astype(BF16)
+                activated[p, head, :, :, lanes] = (
+                    grad_hidden * activated[p, head, :, :, lanes].astype(F32)
+                ).astype(BF16)
+
+            tiles(body)
+        here = slice(j * size, (j + 1) * size)
+        for w, made in enumerate((slopes, activated)):
+            there = slice((2 * j + w) * size, (2 * j + w + 1) * size)
+            writes.append(copies.inside(made.at[:, :, :, :, here], grads_out.at[:, :, :, :, there]))
+
+    reach(n_att + 1, stages + 1)
+    forward(0)
+    step(8)
+    reach(n_att + 3, stages + 1)
+    forward(1)
+    for load in load_rows:
+        load.wait()
+    step(9)
+    reach(n_att + 4, stages + 1)
+    backward(0)
+    step(10)
+    step(11)
+    backward(1)
+    for copy in writes:
+        copy.wait()
+    copies.finish()
+
+
+def pair_front(block_input, grad_output, att_in, mlp_in, tables):
+    _, _, tokens, width = block_input.shape
+    n_att, _, piece, heads_width = att_in.shape
+    n_weights, parts, _, columns = mlp_in.shape
+    n_mlp = n_weights * parts // 2
+    replicas = width // piece // 2
+    length, lanes = tables[0].shape
+    any_space = pl.BlockSpec(memory_space=pl.ANY)
+    in_vmem = pl.BlockSpec(memory_space=pltpu.VMEM)
+
+    def bf16(*shape):
+        return jax.ShapeDtypeStruct(shape, BF16)
+
+    def room(*shape):
+        return pltpu.VMEM(shape, BF16)
+
+    token_rows = (2, 2, 2, tokens, width)
+    outs = [bf16(2, replicas, piece, heads_width)] * n_att
+    hidden_width = n_mlp // 3 * columns
+    outs += [bf16(2, replicas, piece, 2 * hidden_width), bf16(2, replicas, piece, hidden_width)]
+    outs += [bf16(2, 2, 2, tokens, 2 * hidden_width), bf16(2, 2, 2, tokens, hidden_width)]
+    outs += [
+        bf16(*token_rows),
+        bf16(3, 2, 4, tokens, heads_width),
+        bf16(2, 4, tokens, heads_width),
+        jax.ShapeDtypeStruct((2, tokens, width), F32),
+        bf16(*token_rows),
+        bf16(*token_rows),
+        bf16(2, tokens, width),
+        bf16(2, tokens, width),
+    ]
+    own, pair = (2, tokens, width), (2, 2, tokens, width)
+    scratch = [room(*shape) for shape in [own] * 5 + [token_rows] * 2 + [pair] * 2]
+    scratch += [
+        room(3, 2, replicas, piece, heads_width),
+        room(2, replicas, piece, heads_width),
+        room(3, 2, 4, tokens, heads_width),
+        room(2, 4, tokens, heads_width),
+        room(*token_rows),
+        room(*pair),
+        room(*pair),
+        room(*own),
+        room(*own),
+        pltpu.VMEM(own, F32),
+        room(2, 2, 2, tokens, hidden_width),
+        room(2, 2, 2, tokens, hidden_width),
+        *[room(length, lanes)] * 3,
+        pltpu.SemaphoreType.DMA((96,)),
+        pltpu.SemaphoreType.DMA((96,)),
+        pltpu.SemaphoreType.DMA((64,)),
+    ]
+    results = pl.pallas_call(
+        functools.partial(pair_front_kernel, (n_att, n_mlp)),
+        out_shape=outs,
+        in_specs=[any_space] * 4 + [in_vmem] * 2,
+        out_specs=[any_space] * len(outs),
+        scratch_shapes=scratch,
+        compiler_params=pltpu.CompilerParams(
+            collective_id=2, has_side_effects=True, vmem_limit_bytes=63 * 1024 * 1024
+        ),
+    )(block_input, grad_output, att_in, mlp_in, *tables)
+    w_att, results = results[:n_att], results[n_att:]
+    return w_att, results[:2], results[2:4], results[4:]
+
+
+class GradHalving:
+    def __init__(self, copies, kept, first_copy, landed, room, final, own, other):
+        self.copies, self.kept, self.copy, self.landed = copies, kept, first_copy, landed
+        self.room, self.final, self.own, self.other = room, final, own, other
+        self.stages = replica_stages()[::-1]
+        self.stage, self.state = 0, "sent"
+
+    def reach(self, stage, state):
+        order = ("sent", "here", "added")
+        while (self.stage, order.index(self.state)) < (stage, order.index(state)):
+            if self.state == "sent":
+                self.copy.wait_recv()
+                self.state = "here"
+            elif self.state == "here":
+                self.add()
+                self.state = "added"
+            else:
+                self.stage += 1
+                self.send()
+                self.state = "sent"
+
+    def send(self):
+        copies, kept, stage = self.copies, self.kept, self.stage
+        if stage == len(self.stages):
+            self.copy = copies.remote(kept.at[1, 0], self.other, "blk", 1)
+            return
+        count = kept.shape[1] >> (stage - 1)
+        self.copy = copies.remote(
+            kept.at[:, count // 2 : count], self.landed[stage], *self.stages[stage]
+        )
+
+    def add(self):
+        copies, kept, stage = self.copies, self.kept, self.stage
+        if stage == len(self.stages):
+            return
+        count = kept.shape[1] >> stage
+        columns = kept.shape[-1]
+        mine, came = (part.at[:, 0:count, :, 0:columns] for part in self.room)
+        loads = [copies.inside(kept.at[:, 0:count], mine), copies.inside(self.landed[stage], came)]
+        for load in loads:
+            load.wait()
+        if stage == len(self.stages) - 1:
+            self.final[:, 0:columns] = mine[0, 0].astype(F32) + came[0, 0].astype(F32)
+            mine[1, 0] = (mine[1, 0].astype(F32) + came[1, 0].astype(F32)).astype(BF16)
+            stores = [
+                copies.inside(self.final.at[:, 0:columns], self.own),
+                copies.inside(mine.at[1, 0], kept.at[1, 0]),
+            ]
+            for store in stores:
+                store.wait()
+            return
+
+        def one(i, carry):
+            half, row = i // count, i % count
+            mine[half, row] = (mine[half, row].astype(F32) + came[half, row].astype(F32)).astype(BF16)
+            return carry
+
+        lax.fori_loop(0, 2 * count, one, 0)
+        copies.inside(mine, kept.at[:, 0:count]).wait()
+
+
+def pair_back_kernel(sizes, *refs):
+    n_mlp, n_att = sizes
     stages = len(replica_stages())
 
-    def take(count):
+    def take(number):
         nonlocal refs
-        taken, refs = refs[:count], refs[count:]
+        taken, refs = refs[:number], refs[number:]
         return taken
 
-    e_in, mixed_in, x2_in, gg_in, xg_in, attended_in, seq_in, g_ref, x_ref, cosine_ref, sine_ref = take(11)
-    grads_in, w_att = take(n_mlp), take(n_att)
+    e_in, produced_in, mixed_in, x2_in, gg_in, xg_in, attended_in, seq_in = take(8)
+    g_ref, x_ref, cosine_ref, sine_ref = take(4)
+    (grads_in, hidden_in), w_att = take(2), take(n_att)
     own_mlp, other_mlp, own_att, other_att = take(n_mlp), take(n_mlp), take(n_att), take(n_att)
-    (input_out,) = take(1)
+    output_out, input_out = take(2)
     kept_mlp, kept_att = take(n_mlp), take(n_att)
     landed_mlp = [take(stages) for _ in range(n_mlp)]
     landed_att = [take(stages) for _ in range(n_att)]
-    (partial, leaving, came, passing, last, came_c, last_c, total, total_c, rows_g,
-     turned_g, leaves, room_a, room_b, final, made_o, arrived_o, made_b, rows_b, rows_o,
-     acts, weights, seq, q_s, k_s, v_s, dk_s, dv_s, send, recv, local) = refs
-    each = range(micros)
+    (partial, leaving, came, passing, last, came_o, last_o, came_c, last_c, total, total_c, rows_g,
+     turned_g, leaves, room_a, room_b, final, grad_heads, rows_b, rows_o,
+     acts, weights, seq, ready, q_s, k_s, v_s, dk_s, dv_s, send, recv, local) = refs
+    parts = range(2)
     upper = lax.axis_index("blk") // 2
     tokens, width = x_ref.shape[-2:]
-    here = made_o.shape[-1]
-    heads_width = here * groups
+    heads_width = rows_o.shape[-1]
     _, kept_pieces, piece, _ = kept_mlp[0].shape
     copies = Copies(send, recv, local)
     count = 4 * tokens
     tile = 256
 
-    greet()
-    loads = [copies.inside(e_in, partial), copies.inside(mixed_in, total_c)]
-    for load in loads:
-        load.wait()
-    for m in each:
-        total[m] = jnp.zeros_like(total[m])
-    scatters = [TokenScatter(copies, partial, leaving, came, passing, last, total, m) for m in each]
+    load_e = copies.inside(e_in, partial)
+    load_mixed = copies.inside(mixed_in, total_c)
+    acts_load = copies.inside(x2_in, acts)
+    greet_pairs()
+    load_e.wait()
+    for p in parts:
+        total[p] = jnp.zeros_like(total[p])
+    scatters = [TokenScatter(copies, partial, leaving, came, passing, last, total, p) for p in parts]
 
     busy = []
 
@@ -912,9 +1312,9 @@
                 low, part = i // per_half, i % per_half
                 start = low * (2 * kept_pieces * piece) + side * (kept_pieces * piece) + part * tile
                 lanes = pl.ds(pl.multiple_of(start, tile), tile)
-                left = acts[:, :, :, :, lanes].reshape(micros * count, tile)
+                left = acts[:, :, :, :, lanes].reshape(2 * count, tile)
                 for j, right in enumerate(grads):
-                    product = matmul_tn(left, right[...].reshape(micros * count, part_columns)).astype(BF16)
+                    product = matmul_tn(left, right[...].reshape(2 * count, part_columns)).astype(BF16)
                     columns_here = slice(j * part_columns, (j + 1) * part_columns)
                     side_room[low, pl.ds(part * pieces, pieces), :, columns_here] = product.reshape(
                         pieces, piece, part_columns
@@ -928,25 +1328,34 @@
                 busy.append(first)
             else:
                 copies.inside(source, kept).wait()
-        return GradScatter(copies, kept, first, landed, (room_a, room_b), final, own, other)
+        chunks.append(GradHalving(copies, kept, first, landed, (room_a, room_b), final, own, other))
 
     chunks = []
 
-    def pump():
-        for chunk in reversed(chunks):
-            if chunk.stage <= stages:
-                chunk.advance()
+    def reach(k, stage, state):
+        if 0 <= k < len(chunks):
+            chunks[k].reach(stage, state)
+
+    done = [0]
+
+    def step():
+        k = done[0]
+        done[0] += 1
+        reach(k + 1, 1, "sent")
+        reach(k, 2, "sent")
+        reach(k - 1, 3, "sent")
+        reach(k - 2, 3, "here")
 
     def load_grads(k):
         loads = []
         for half_of in range(2):
-            lanes = slice(half_of * heads_width, (half_of + 1) * heads_width)
             for row in range(2 * kept_pieces):
-                source = grads_in[k].at[row * piece : (row + 1) * piece, lanes]
+                source = grads_in if k < 2 * n_mlp // 3 else hidden_in
+                first = k % (2 * n_mlp // 3) * 2 * heads_width + half_of * heads_width
+                source = source.at[row // 4, row // 2 % 2, row % 2, :, first : first + heads_width]
                 loads.append(copies.inside(source, weights.at[k % 2, half_of, row]))
         return loads
 
-    acts_load = copies.inside(x2_in, acts)
     slots = [load_grads(0)]
 
     def mlp_chunk(k):
@@ -954,137 +1363,118 @@
             load.wait()
         if k + 1 < n_mlp:
             slots.append(load_grads(k + 1))
-        parts = [weights.at[k % 2, half] for half in range(2)]
-        return weight_grad(acts, parts, kept_mlp[k], landed_mlp[k], own_mlp[k], other_mlp[k])
+        halves = [weights.at[k % 2, half_of] for half_of in range(2)]
+        weight_grad(acts, halves, kept_mlp[k], landed_mlp[k], own_mlp[k], other_mlp[k])
 
     acts_load.wait()
-    chunks.append(mlp_chunk(0))
-    chunks.append(mlp_chunk(1))
+    mlp_chunk(0)
+    mlp_chunk(1)
+    reach(0, 1, "sent")
     for scatter in scatters:
         scatter.second()
-    pump()
-    chunks.append(mlp_chunk(2))
+    load_mixed.wait()
+    mlp_chunk(2)
     gathers = []
-    for m in each:
-        scatters[m].end()
-        mixed = total_c[m]
+    for p in parts:
+        scatters[p].end()
+        scatters[p].release()
+        mixed = total_c[p]
         scale = lax.rsqrt(jnp.mean(mixed * mixed, -1, keepdims=True) + EPSILON)
-        total[m] = g_ref[m].astype(F32) + norm_back(total[m], mixed, scale)
-        rows_g[m, 0, 0] = total[m].astype(BF16)
-        gathers.append(TokenGather(copies, rows_g, turned_g, m))
-    pump()
-    chunks.append(mlp_chunk(3))
+        total[p] = g_ref[p].astype(F32) + norm_back(total[p], mixed, scale)
+        rows_g[p, 0, 0] = total[p].astype(BF16)
+        gathers.append(TokenGather(copies, rows_g, turned_g, p))
+    load_produced = copies.inside(produced_in, partial)
+    step()
+    mlp_chunk(3)
     acts_load = copies.inside(gg_in, acts)
     for gather in gathers:
         gather.second()
     acts_load.wait()
-    chunks.append(mlp_chunk(4))
-    pump()
-    chunks.append(mlp_chunk(5))
+    mlp_chunk(4)
+    step()
+    mlp_chunk(5)
+    w_loads = [copies.inside(w_att[i], weights.at[slot]) for i, slot in ((3, 0), (0, 1), (1, 2))]
+    load_seq = copies.inside(seq_in, seq)
+    load_rows_o = [copies.inside(attended_in.at[p], rows_o.at[4 * p : 4 * p + 4]) for p in parts]
     for gather in gathers:
         gather.end()
-
-    for scatter in scatters:
-        scatter.release()
-    w_loads = [copies.inside(w_att[i], weights.at[slot]) for i, slot in ((3, 0), (0, 1), (1, 2))]
-    seq_load = copies.inside(seq_in.at[0], seq.at[0])
-    att_loads = [
-        copies.inside(attended_in.at[m, place], rows_o.at[4 * m : 4 * m + 4, :, place * here : (place + 1) * here])
-        for m in each
-        for place in range(groups)
-    ]
+    load_produced.wait()
+    scatters = [TokenScatter(copies, partial, leaving, came_o, passing, last_o, total_c, p, True) for p in parts]
     w_loads[0].wait()
-    crossing = []
-    for m in each:
-        rows = rows_g[m].reshape(count, width)
+    for p in parts:
+        rows = rows_g[p].reshape(count, width)
         product = matmul(rows, weights[0].reshape(width, heads_width)).astype(BF16)
-        for place in range(groups):
-            for group in range(4):
-                made_o[m, place, group] = product[
-                    group * tokens : (group + 1) * tokens, place * here : (place + 1) * here
-                ]
-        moves = [copies.inside(made_o.at[m, upper], arrived_o.at[m, upper])]
-        for r in range(1, groups):
-            source = made_o.at[m, flipped("blk", 2 * r) // 2]
-            moves.append(copies.remote(source, arrived_o.at[m, upper], "blk", 2 * r))
-        crossing.append(moves)
+        for group in range(4):
+            grad_heads[p, group] = product[group * tokens : (group + 1) * tokens]
     w_loads.append(copies.inside(w_att[2], weights.at[0]))
-    for load in att_loads:
+    for load in load_rows_o:
         load.wait()
-    chunks.append(weight_grad(rows_g, [rows_o], kept_att[3], landed_att[3], own_att[3], other_att[3]))
-    returning = []
-    own_lanes = pl.ds(pl.multiple_of(upper * here, here), here)
-    for m in each:
-        seq_load.wait()
-        crossing[m][0].wait()
-        for copy in crossing[m][1:]:
-            copy.wait_recv()
-        attend_back(seq, 0, arrived_o, made_b, m, cosine_ref, sine_ref, (q_s, k_s, v_s), (dk_s, dv_s))
-        if m + 1 < micros:
-            seq_load = copies.inside(seq_in.at[m + 1], seq.at[0])
-        moves = ([], [])
-        for i in range(3):
-            target = rows_b.at[i, 4 * m : 4 * m + 4, :, own_lanes]
-            moves[0].append(copies.inside(made_b.at[m, upper, i], target))
-            for r in range(1, groups):
-                source = made_b.at[m, flipped("blk", 2 * r) // 2, i]
-                moves[1].append(copies.remote(source, target, "blk", 2 * r))
-        returning.append(moves)
-        pump()
+    weight_grad(rows_g, [rows_o], kept_att[3], landed_att[3], own_att[3], other_att[3])
+    step()
+    load_seq.wait()
+    lanes = cosine_ref.shape[1]
+    for at, lane in enumerate(range(0, heads_width, lanes)):
+        attend_pair_back(seq, grad_heads, rows_b, lane, cosine_ref, sine_ref, (q_s, k_s, v_s), (dk_s, dv_s))
+        if at == 0:
+            for scatter in scatters:
+                scatter.second()
+        step()
+    trades = []
+    for p in parts:
+        scatters[p].end()
+        scatters[p].release()
+        to_absolute_order(total_c[p].astype(BF16), ready, p, piece)
+    stores = [copies.inside(ready.at[0], output_out.at[upper])]
+    trades.append(copies.remote(ready.at[1], output_out.at[upper], "blk", 2))
+    acts_load = copies.inside(xg_in, acts)
     for load in w_loads[1:]:
         load.wait()
-    started = []
-    for m in each:
-        for copy in returning[m][0]:
-            copy.wait()
-        for copy in returning[m][1]:
-            copy.wait_recv()
+    scatters = []
+    for p in parts:
         pieces = tile // piece
         for start in range(0, width, tile):
             low, first = start // (2 * kept_pieces * piece), start // piece % (2 * kept_pieces)
-            product = functools.reduce(
-                jnp.add,
-                [
-                    matmul_nt(
-                        rows_b[i, 4 * m : 4 * m + 4].reshape(count, heads_width),
-                        weights[(i + 1) % 3, low, first : first + pieces].reshape(tile, heads_width),
-                    )
-                    for i in range(3)
-                ],
-            ).astype(BF16)
-            for group in range(4):
-                partial[m, group // 2, group % 2, :, start : start + tile] = product[
-                    group * tokens : (group + 1) * tokens
-                ]
-        total_c[m] = jnp.zeros_like(total_c[m])
-        started.append(TokenScatter(copies, partial, leaving, came_c, passing, last_c, total_c, m))
-
-    copies.inside(xg_in, acts).wait()
+            terms = []
+            for i in range(3):
+                weight = weights[(i + 1) % 3, low, first : first + pieces].reshape(tile, heads_width)
+                terms.append(matmul_nt(rows_b[i, 4 * p : 4 * p + 4].reshape(count, heads_width), weight))
+            product = functools.reduce(jnp.add, terms).astype(BF16)
+            store_product(product, partial, p, slice(start, start + tile))
+        total_c[p] = jnp.zeros_like(total_c[p])
+        scatters.append(TokenScatter(copies, partial, leaving, came_c, passing, last_c, total_c, p))
+    acts_load.wait()
     for i in range(3):
-        chunks.append(weight_grad(acts, [rows_b.at[i]], kept_att[i], landed_att[i], own_att[i], other_att[i]))
-    pump()
-    for scatter in started:
+        weight_grad(acts, [rows_b.at[i]], kept_att[i], landed_att[i], own_att[i], other_att[i])
+    step()
+    for scatter in scatters:
         scatter.second()
-    pump()
-    for m in each:
-        started[m].end()
-        started[m].release()
-        values = x_ref[m].astype(F32)
+    step()
+    for store in stores:
+        store.wait()
+    copies.wait_sent(trades[0])
+    for p in parts:
+        scatters[p].end()
+        scatters[p].release()
+        values = x_ref[p].astype(F32)
         scale = lax.rsqrt(jnp.mean(values * values, -1, keepdims=True) + EPSILON)
-        passing[m] = (total[m] + norm_back(total_c[m], values, scale)).astype(BF16)
-    copies.inside(passing, input_out).wait()
-    while any(chunk.stage <= stages for chunk in chunks):
-        pump()
+        rows = (total[p] + norm_back(total_c[p], values, scale)).astype(BF16)
+        to_absolute_order(rows, ready, p, piece)
+    store = copies.inside(ready.at[0], input_out.at[upper])
+    trades.append(copies.remote(ready.at[1], input_out.at[upper], "blk", 2))
+    while done[0] < len(chunks) + 2:
+        step()
+    store.wait()
+    for trade in trades:
+        trade.wait_recv()
     copies.finish()
 
 
-def back(partial, mixed, x2, grad_rows, normed_one, attended, sequences, g_rows, x_rows, tables, grads, w_att):
-    micros, tokens, width = x_rows.shape
-    n_mlp, n_att = len(grads), len(w_att)
-    columns = grads[0].shape[1]
+def pair_back(partial, produced, held, tables, grads, w_att):
+    normed_one, sequences, attended, mixed, normed_two, grad_rows, x_rows, g_rows = held
+    _, tokens, width = x_rows.shape
     _, replicas, piece, heads_width = w_att[0].shape
-    groups = head_groups()
-    here = heads_width // groups
+    columns = 2 * heads_width
+    n_mlp, n_att = sum(g.shape[-1] for g in grads) // columns, len(w_att)
     stages = len(replica_stages())
     any_space = pl.BlockSpec(memory_space=pl.ANY)
     in_vmem = pl.BlockSpec(memory_space=pltpu.VMEM)
@@ -1092,65 +1482,70 @@
     def bf16(*shape):
         return jax.ShapeDtypeStruct(shape, BF16)
 
+    def f32(*shape):
+        return jax.ShapeDtypeStruct(shape, F32)
+
     def room(*shape):
         return pltpu.VMEM(shape, BF16)
 
-    def f32_room(*shape):
-        return pltpu.VMEM(shape, F32)
-
     widths = [columns] * n_mlp + [heads_width] * n_att
-    outs = [jax.ShapeDtypeStruct((piece, columns), F32)] * n_mlp + [bf16(piece, columns)] * n_mlp
-    outs += [jax.ShapeDtypeStruct((piece, heads_width), F32)] * n_att + [bf16(piece, heads_width)] * n_att
-    outs += [bf16(micros, tokens, width)]
+    outs = [f32(piece, columns)] * n_mlp + [bf16(piece, columns)] * n_mlp
+    outs += [f32(piece, heads_width)] * n_att + [bf16(piece, heads_width)] * n_att
+    outs += [bf16(2, tokens, width)] * 2
     outs += [bf16(2, replicas // 2, piece, w) for w in widths]
     outs += [bf16(2, replicas >> (s + 1), piece, w) for w in widths for s in range(stages)]
-    token_rows = (micros, 2, 2, tokens, width)
-    half_room = (2, replicas // 2, piece, max(columns, heads_width))
+    token_rows, own, pair = (2, 2, 2, tokens, width), (2, tokens, width), (2, 2, tokens, width)
+    widest = max(columns, heads_width)
+    half_room = (2, replicas // 2, piece, widest)
     scratch = [
         room(*token_rows),
-        room(micros, 2, tokens, width),
-        room(micros, 2, tokens, width),
-        room(micros, tokens, width),
-        room(micros, tokens, width),
-        room(micros, 2, tokens, width),
-        room(micros, tokens, width),
-        f32_room(micros, tokens, width),
-        f32_room(micros, tokens, width),
+        room(*pair),
+        room(*pair),
+        room(*own),
+        room(*own),
+        room(*pair),
+        room(*own),
+        room(*pair),
+        room(*own),
+        pltpu.VMEM(own, F32),
+        pltpu.VMEM(own, F32),
         room(*token_rows),
-        room(micros, 2, tokens, width),
+        room(*pair),
         room(*half_room),
         room(*half_room),
         room(*half_room),
-        f32_room(piece, max(columns, heads_width)),
-        room(micros, groups, 4, tokens, here),
-        room(micros, groups, 4, tokens, here),
-        room(micros, groups, 3, 4, tokens, here),
-        room(3, micros * 4, tokens, heads_width),
-        room(micros * 4, tokens, heads_width),
+        pltpu.VMEM((piece, widest), F32),
+        room(2, 4, tokens, heads_width),
+        room(3, 8, tokens, heads_width),
+        room(8, tokens, heads_width),
         room(*token_rows),
         room(3, 2, replicas, piece, heads_width),
-        room(1, groups, 3, 4, tokens, here),
+        room(3, 2, 4, tokens, heads_width),
+        room(*own),
         *[room(*tables[0].shape)] * 3,
-        *[f32_room(*tables[0].shape)] * 2,
-        pltpu.SemaphoreType.DMA((128,)),
-        pltpu.SemaphoreType.DMA((128,)),
+        *[pltpu.VMEM(tables[0].shape, F32)] * 2,
+        pltpu.SemaphoreType.DMA((96,)),
+        pltpu.SemaphoreType.DMA((96,)),
         pltpu.SemaphoreType.DMA((384,)),
     ]
     results = pl.pallas_call(
-        functools.partial(back_kernel, (micros, groups, n_mlp, n_att)),
+        functools.partial(pair_back_kernel, (n_mlp, n_att)),
         out_shape=outs,
-        in_specs=[any_space] * 7 + [in_vmem] * 4 + [any_space] * (n_mlp + n_att),
+        in_specs=[any_space] * 8 + [in_vmem] * 4 + [any_space] * (2 + n_att),
         out_specs=[any_space] * len(outs),
         scratch_shapes=scratch,
         compiler_params=pltpu.CompilerParams(
-            collective_id=1, has_side_effects=True, vmem_limit_bytes=63 * 1024 * 1024
+            collective_id=3, has_side_effects=True, vmem_limit_bytes=63 * 1024 * 1024
         ),
-    )(partial, mixed, x2, grad_rows, normed_one, attended, sequences, g_rows, x_rows, *tables, *grads, *w_att)
+    )(
+        partial, produced, mixed, normed_two, grad_rows, normed_one, attended, sequences, g_rows, x_rows,
+        *tables, *grads, *w_att,
+    )
     own_mlp, results = results[:n_mlp], results[n_mlp:]
     other_mlp, results = results[:n_mlp], results[n_mlp:]
     own_att, results = results[:n_att], results[n_att:]
     other_att, results = results[:n_att], results[n_att:]
-    return list(zip(own_mlp, other_mlp)), list(zip(own_att, other_att)), results[0]
+    return list(zip(own_mlp, other_mlp)), list(zip(own_att, other_att)), results[0], results[1]
 
 
 def scale_of(values):
@@ -1203,43 +1598,42 @@
     mlp_in = jnp.stack(
         [columns_of(scaled(w, gain_two), 4) for w in (gate_weight, up_weight)] + [columns_of(down_weight.T, 4)]
     )
-    block_rows = [array.reshape(micros * tokens, width) for array in (block_input, grad_output)]
-    inputs_low, grad_low = (rows.reshape(micros, tokens, width) for rows in reorder(to_own, *block_rows))
-    grad_turned = turn_features(grad_low.reshape(micros * tokens, width)).reshape(micros, tokens, width)
-    w_att, w_mlp, held = front(inputs_low, grad_low, grad_turned, att_in, mlp_in, tables)
-    normed_one, sequences, attended, mixed, normed_two, grad_rows = held
-    normed_two_all = normed_two.reshape(-1, width)
-    grad_rows_all = grad_rows.reshape(-1, width)
-    gate_parts, up_parts, down_parts = w_mlp[0:4:2], w_mlp[1:4:2], w_mlp[4:]
-
+    paired = micros == 2 and lax.axis_size("blk") == 4 and heads_width % LANES == 0 and 8 * tokens == width // 2
+    paired = paired and mlp_in.shape[-1] == 2 * heads_width == width // 2 and mlp_in.shape[-2] == tokens
     hidden, grad_gate, grad_up = [], [], []
     grad_normed = produced = 0.0
-    for gate_full, up_full, down_full in zip(gate_parts, up_parts, down_parts):
-        gate = matmul(normed_two_all, gate_full)
-        up = matmul(normed_two_all, up_full)
-        sigmoid = jax.nn.sigmoid(gate)
-        activated = gate * sigmoid
-        hidden.append((activated * up).astype(BF16))
-        grad_hidden = matmul(grad_rows_all, down_full)
-        grad_gate.append((grad_hidden * up * sigmoid * (1.0 + gate * (1.0 - sigmoid))).astype(BF16))
-        grad_up.append((grad_hidden * activated).astype(BF16))
-        grad_normed += matmul_nt(grad_gate[-1], gate_full) + matmul_nt(grad_up[-1], up_full)
-        produced += matmul_nt(hidden[-1], down_full)
+    if paired:
+        w_att, w_mlp, made, held = pair_front(block_input, grad_output, att_in, mlp_in, tables)
+        grad_normed, produced = (
+            matmul_nt(rows.reshape(-1, rows.shape[-1]), weight.reshape(width, -1)) for rows, weight in zip(made, w_mlp)
+        )
+    else:
+        block_rows = [array.reshape(micros * tokens, width) for array in (block_input, grad_output)]
+        inputs_low, grad_low = (rows.reshape(micros, tokens, width) for rows in reorder(to_own, *block_rows))
+        grad_turned = turn_features(grad_low.reshape(micros * tokens, width)).reshape(micros, tokens, width)
+        w_att, w_mlp, held = front(inputs_low, grad_low, grad_turned, att_in, mlp_in, tables)
+        normed_one, sequences, attended, mixed, normed_two, grad_rows = held
+        normed_two_all = normed_two.reshape(-1, width)
+        grad_rows_all = grad_rows.reshape(-1, width)
+        for gate_full, up_full, down_full in zip(w_mlp[0:4:2], w_mlp[1:4:2], w_mlp[4:]):
+            gate = matmul(normed_two_all, gate_full)
+            up = matmul(normed_two_all, up_full)
+            sigmoid = jax.nn.sigmoid(gate)
+            activated = gate * sigmoid
+            hidden.append((activated * up).astype(BF16))
+            grad_hidden = matmul(grad_rows_all, down_full)
+            grad_gate.append((grad_hidden * up * sigmoid * (1.0 + gate * (1.0 - sigmoid))).astype(BF16))
+            grad_up.append((grad_hidden * activated).astype(BF16))
+            grad_normed += matmul_nt(grad_gate[-1], gate_full) + matmul_nt(grad_up[-1], up_full)
+            produced += matmul_nt(hidden[-1], down_full)
 
     def split(rows):
         size = rows.shape[0] // micros
         return [rows[m * size : (m + 1) * size] for m in each]
 
-    produced = split(produced)
-    outputs = [(mixed[m] + scatter_tokens(produced[m], head_first[m])).astype(BF16) for m in each]
-
-    if sequences.shape[-1] % LANES == 0 and micros * 4 * tokens == width // 2:
-        mlp_pairs, att_pairs, input_grads = back(
-            grad_normed.astype(BF16).reshape(normed_two.shape), mixed, normed_two, grad_rows, normed_one, attended,
-            sequences, grad_low, inputs_low, tables,
-            [grad_gate[0], grad_up[0], grad_gate[1], grad_up[1], hidden[0], hidden[1]], w_att,
-        )
-        input_grads = [input_grads[m] for m in each]
+    if paired:
+        partials = [rows.astype(BF16).reshape(held[4].shape) for rows in (grad_normed, produced)]
+        mlp_pairs, att_pairs, block_output, input_grad = pair_back(*partials, held, tables, made, w_att)
 
         def beside(pairs):
             return tuple(jnp.concatenate(side, 1) for side in zip(*pairs))
@@ -1248,6 +1642,8 @@
         output_grad = att_pairs[3]
         qkv_grads = [side_by_side(*pair) for pair in att_pairs[:3]]
     else:
+        produced = split(produced)
+        outputs = [(mixed[m] + scatter_tokens(produced[m], head_first[m])).astype(BF16) for m in each]
         upper = lax.axis_index("blk") // 2
         w_att = [w.reshape(width, -1) for w in w_att]
         normed_one_all = normed_one.reshape(-1, width)
@@ -1280,6 +1676,7 @@
         qkv_grads = [
             side_by_side(*(side[:, i * heads_width : (i + 1) * heads_width] for side in qkv_grad)) for i in range(3)
         ]
+        block_output, input_grad = reorder(to_absolute, joined(outputs), joined(input_grads))
     mlp_grads = [side_by_side(*gate_grad), side_by_side(*up_grad)]
 
     def gain_grad(weights, grads):
@@ -1289,7 +1686,6 @@
 
     attention_gain_grad = gain_grad((query_weight, key_weight, value_weight), qkv_grads)
     mlp_gain_grad = gain_grad((gate_weight, up_weight), mlp_grads)
-    block_output, input_grad = reorder(to_absolute, joined(outputs), joined(input_grads))
 
     return (
         block_output.reshape(micros, 1, tokens, width),

time: 926 us -> 813 us (0.88)
  matrix products: 91.3 us -> 33.1 us
  Pallas kernels: 770 us -> 736 us
  other arithmetic: 28.7 us -> 12.7 us
    dot_general x6 -> x0, matrix products: 40.3 us -> none  [matmul(): return jnp.dot(left_side, right_side, preferred_element_type=F32)]
    pallas_call x4 -> x2, Pallas kernels: 770 us -> 736 us  [the longest x1 388 us: pair_front(): pl.pallas_call(functools.partial(pair_front_kernel, (n_att, n_mlp)), out_...]
    dot_general x6 -> x2, matrix products: 51 us -> 33.1 us  [matmul_nt(): lax.dot_general(left_side, right_side, (((1,), (1,)), ((), ())), preferre...]
  transfers between devices with their start and end apart: 6 -> 2, of which waited for: 2 -> 0; matrix products, arithmetic and copies ran while one was open for 6% -> 1% of each run, Pallas kernels for 42% -> 0%
where the time goes in v4:
time: 813 us; the launch traced here: 804 us
  Pallas kernels  736 us (91%)
  matrix products  33.1 us (4%)
  local copies, waits for them, and re-layouts  15 us (2%)
  other arithmetic  12.7 us (2%)
    pallas_call x1, Pallas kernels, pair_front(): pl.pallas_call(functools.partial(pair_front_kernel, (n_att, n_mlp)), out_...  388 us
    pallas_call x1, Pallas kernels, pair_back(): pl.pallas_call(functools.partial(pair_back_kernel, (n_mlp, n_att)), out_s...  348 us
    dot_general x2, matrix products, matmul_nt(): lax.dot_general(left_side, right_side, (((1,), (1,)), ((), ())), preferre...  33.1 us
  transfers between devices with their start and end apart: 2, of which 0 were waited for; matrix products, arithmetic and copies ran while one was open for 1% of the time, Pallas kernels for 0%

profile of v4, /device:TPU:0, one launch (start us, length us, event | category | flops | bytes accessed | tf_op | source)
XLA Modules:
  0.0 804.2 jit_solution(9575233184289895886)
XLA Ops:
  0.7 0.7 convert_element_type.69
  1.4 2.1 fusion.6
  3.5 0.7 copy.54
  4.2 0.8 copy.36
  5.1 1.5 copy.39
  6.6 1.0 bitcast_bitcast_fusion.2
  8.4 2.0 pad_maximum_fusion.refs_3_
  10.4 1.1 pad_maximum_fusion.3.refs_2_
  11.5 388.1 %shard_map.212 = (bf16[2,8,128,512]{3,2,1,0:T(8,128)(2,1)}, bf16[2,8,128,512]{3,2,1,0:T(8,128)(2,1)}, bf16[2,8,128,512]{3,2,1,0:T(8,128)(2,1)}, bf16[2,8,128,512...) custom-call(bf16[2,1,128,2048]{3,2,1,0:T(8,128)(2,1)} %refs_0_.1, ...), custom_call_target="tpu_custom_call" | custom-call | tf_op jit(solution)/shard_map/pallas_call | solution.py:1185
  399.6 14.1 %convolution_convert_fusion.1 = bf16[1024,2048]{1,0:T(8,128)(2,1)} fusion(bf16[1024,2048]{1,0:T(8,128)(2,1)} %bitcast.70, bf16[2048,2048]{1,0:T(8,128)(2,1)} %bitcast.86), kind=kOutput, calls=%fused_computation.1 | convolution fusion | flops 8592031744 | bytes 16777216 | tf_op jit(solution)/shard_map/dot_general | solution.py:40
  413.7 19.1 %convolution_convert_fusion = bf16[1024,2048]{1,0:T(8,128)(2,1)} fusion(bf16[1024,4096]{1,0:T(8,128)(2,1)S(1)} %bitcast.69, bf16[2048,4096]{1,0:T(8,128)(2,1)S(1)} %bitcast.85), kind=kOutput, calls=%fused_computation | convolution fusion | flops 17181966336 | bytes 29360128 | tf_op jit(solution)/shard_map/dot_general | solution.py:40
  432.7 347.5 %shard_map.213 = (f32[128,1024]{1,0:T(8,128)}, f32[128,1024]{1,0:T(8,128)}, f32[128,1024]{1,0:T(8,128)}, f32[128,1024]{1,0:T(8,128)}, f32[128,1024]{1,0:T(8,128)...) custom-call(bf16[2,2,2,128,2048]{4,3,2,1,0:T(8,128)(2,1)} %bitcast.7, ...), custom_call_target="tpu_custom_call" | custom-call | tf_op jit(solution)/shard_map/pallas_call | solution.py:1531
  780.3 1.2 constant_dynamic-update-slice_fusion.1
  781.5 1.1 constant_dynamic-update-slice_fusion.3
  783.0 0.6 copy-done.22
  784.6 2.8 fusion.4
  787.4 5.6 collective-permute-start.1
  793.3 1.4 fusion.12
  794.7 0.7 collective-permute-start
  796.0 0.8 copy-done.15
  796.9 1.8 copy.43
  798.7 1.0 copy.42
  800.7 2.3 copy.60
  803.1 1.0 copy.61
  (84 shorter events, 3.8 us)
Async XLA Ops:
  0.6 3.6 copy-start.19
  0.7 4.4 copy-start.31
  3.5 4.1 copy-start.1
  3.5 4.1 copy-start.3
  399.6 14.1 %copy-start = (bf16[2,2,2,128,4096]{4,3,2,1,0:T(8,128)(2,1)S(1)}, bf16[2,2,2,128,4096]{4,3,2,1,0:T(8,128)(2,1)}, u32[]{:S(2)}) copy-start(bf16[2,2,2,128,4096]{4,3,2,1,0:T(8,128)(2,1)} %get-tuple-element.49.refs_12_) | copy-start | bytes 25165828
  399.6 14.1 %copy-start.30 = (bf16[2,8,128,4096]{3,2,1,0:T(8,128)(2,1)S(1)}, bf16[2,8,128,4096]{3,2,1,0:T(8,128)(2,1)}, u32[]{:S(2)}) copy-start(bf16[2,8,128,4096]{3,2,1,0:T(8,128)(2,1)} %get-tuple-element.50) | copy-start | bytes 50331652
  780.3 2.3 copy-start.14
  780.3 2.4 copy-start.13
  780.3 2.4 copy-start.24
  780.3 2.4 copy-start.25
  784.6 8.5 %copy-start.18 = (f32[128,512]{1,0:T(8,128)S(1)}, f32[128,512]{1,0:T(8,128)}, u32[]{:S(2)}) copy-start(f32[128,512]{1,0:T(8,128)} %get-tuple-element.69) | copy-start | bytes 786436
  784.6 8.5 %copy-start.29 = (bf16[128,512]{1,0:T(8,128)(2,1)S(1)}, bf16[128,512]{1,0:T(8,128)(2,1)}, u32[]{:S(2)}) copy-start(bf16[128,512]{1,0:T(8,128)(2,1)} %get-tuple-element.70) | copy-start | bytes 393220
  784.6 8.5 %copy-start.17 = (f32[128,512]{1,0:T(8,128)S(1)}, f32[128,512]{1,0:T(8,128)}, u32[]{:S(2)}) copy-start(f32[128,512]{1,0:T(8,128)} %get-tuple-element.67) | copy-start | bytes 786436
  784.6 8.5 %copy-start.28 = (bf16[128,512]{1,0:T(8,128)(2,1)S(1)}, bf16[128,512]{1,0:T(8,128)(2,1)}, u32[]{:S(2)}) copy-start(bf16[128,512]{1,0:T(8,128)(2,1)} %get-tuple-element.68) | copy-start | bytes 393220
  784.6 8.6 %copy-start.16 = (f32[128,512]{1,0:T(8,128)S(1)}, f32[128,512]{1,0:T(8,128)}, u32[]{:S(2)}) copy-start(f32[128,512]{1,0:T(8,128)} %get-tuple-element.71) | copy-start | bytes 786436
  784.6 8.6 %copy-start.27 = (bf16[128,512]{1,0:T(8,128)(2,1)S(1)}, bf16[128,512]{1,0:T(8,128)(2,1)}, u32[]{:S(2)}) copy-start(bf16[128,512]{1,0:T(8,128)(2,1)} %get-tuple-element.72) | copy-start | bytes 393220
  787.4 5.9 copy-start.6
  787.4 5.9 copy-start.7
  787.4 5.9 copy-start.8
  787.4 12.3 %collective-permute-start.1 = (f32[128]{0:T(128)S(1)}, f32[128]{0:T(128)S(1)}, u32[]{:S(2)}, u32[]{:S(2)}) collective-permute-start(f32[128]{0:T(128)S(1)} %add.29), channel_id=1, source_target_pairs={{0,4},{4,0},{1,5},{5,1},{2,6},{6,2},{3,7},{7,3},{8,12},{12,8},{9,1... | collective-permute-start | bytes 1544 | tf_op jit(solution)/shard_map/ppermute | solution.py:23
  793.3 2.2 copy-start.20
  793.3 2.2 copy-start.21
  794.7 5.5 collective-permute-start
  798.7 4.3 copy-start.5
  (10 other events, 15.1 us)

commit v5 on v4

--- a/solution.py
+++ b/solution.py
@@ -467,9 +467,15 @@
         self.copy.wait_recv()
         self.total[self.m] += self.last[self.m].astype(F32)
 
+    def release_first(self):
+        self.copies.wait_sent(self.first)
+
+    def release_last(self):
+        self.copies.wait_sent(self.copy)
+
     def release(self):
-        self.copies.wait_sent(self.first)
-        self.copies.wait_sent(self.copy)
+        self.release_first()
+        self.release_last()
 
 
 def place_of(block):
@@ -928,18 +934,17 @@
     def att_chunk(i):
         return lambda: WeightGather(copies, att_in.at[i, near], att_in.at[i, 1 - near], w_att[i])
 
-    def mlp_chunk(i):
+    def mlp_chunk(w, j, columns):
         per_weight = n_mlp // 3
-        w, j = (i % 2, i // 2) if i < 2 * per_weight else (2, i - 2 * per_weight)
         size = mlp_in.shape[-1]
-        if w < 2:
-            full = w_gu.at[:, :, :, i * size : (i + 1) * size]
-        else:
-            full = w_down.at[:, :, :, j * size : (j + 1) * size]
-        own, other = near * per_weight + j, (1 - near) * per_weight + j
-        return lambda: WeightGather(copies, mlp_in.at[w, own], mlp_in.at[w, other], full)
-
-    makers = [att_chunk(i) for i in range(n_att)] + [mlp_chunk(i) for i in range(n_mlp)]
+        first = (2 * j + w if w < 2 else j) * size + columns.start
+        full = (w_gu if w < 2 else w_down).at[:, :, :, first : first + columns.stop - columns.start]
+        own, other = (mlp_in.at[w, at * per_weight + j, :, columns] for at in (near, 1 - near))
+        return lambda: WeightGather(copies, own, other, full)
+
+    whole, halves = slice(0, 2 * heads_width), [slice(0, heads_width), slice(heads_width, 2 * heads_width)]
+    mlp_order = [(w, j, whole) for j in range(2) for w in range(2)] + [(2, 0, whole)] + [(2, 1, h) for h in halves]
+    makers = [att_chunk(i) for i in range(n_att)] + [mlp_chunk(*chunk) for chunk in mlp_order]
     chunks = []
 
     def reach(k, stage):
@@ -953,7 +958,7 @@
         reach(k - 1, 3)
         reach(k, 2)
         reach(k + ahead[0], 1)
-        reach(k + 3, 0)
+        reach(k + ahead[0] + 1, 0)
 
     ahead = [1]
 
@@ -1004,8 +1009,6 @@
     writes = [copies.inside(seq, seq_out), copies.inside(x_own, x_out)]
     first_gathers = gathers
     trade.wait_recv()
-    ahead[0] = 2
-    reach(5, 1)
     grad_rows = []
     for p in range(2):
         g_own[p] = to_own_order(lambda lanes, p=p: g_raw[p, :, lanes], width, piece)
@@ -1016,8 +1019,6 @@
     lanes = q_s.shape[1]
     for at, lane in enumerate(range(0, heads_width, lanes)):
         attend_pair(seq, attended, lane, cosine_ref, sine_ref, held)
-        if at == 1:
-            step(4)
     load_weight(3)
     w_loads[3].wait()
     scatters = []
@@ -1030,7 +1031,7 @@
         mixed[p] = x_own[p].astype(F32)
         scatters.append(TokenScatter(copies, partial, leaving, came, passing, last, mixed, p))
     writes.append(copies.inside(attended, attended_out))
-    step(5)
+    step(4)
     for scatter in scatters:
         scatter.second()
     far = []
@@ -1038,6 +1039,7 @@
         mine.wait()
         turned_copy.wait_recv()
         far.append(copies.remote(gg_out.at[p, 0], gg_out.at[p, 1], "head", 1))
+    step(5)
     gathers = []
     for p in range(2):
         scatters[p].end()
@@ -1094,24 +1096,23 @@
         here = slice(j * size, (j + 1) * size)
         writes.append(copies.inside(hidden.at[:, :, :, :, here], hidden_out.at[:, :, :, :, here]))
 
-    def backward(j):
-        for lane in quarters:
-            lanes = slice(j * size + lane, j * size + lane + heads_width)
-            copies.inside(w_down.at[:, :, :, lanes], w_in.at[2]).wait()
-
-            def body(p, head, lanes=lanes):
-                rows = xg[p, head].reshape(2 * tokens, width)
-                grad_hidden = matmul(rows, w_in[2].reshape(width, heads_width)).reshape(2, tokens, heads_width)
-                slopes[p, head, :, :, lanes] = (grad_hidden * slopes[p, head, :, :, lanes].astype(F32)).astype(BF16)
-                activated[p, head, :, :, lanes] = (
-                    grad_hidden * activated[p, head, :, :, lanes].astype(F32)
-                ).astype(BF16)
-
-            tiles(body)
-        here = slice(j * size, (j + 1) * size)
+    def backward(j, lane):
+        lanes = slice(j * size + lane, j * size + lane + heads_width)
+        copies.inside(w_down.at[:, :, :, lanes], w_in.at[2]).wait()
+
+        def body(p, head):
+            rows = xg[p, head].reshape(2 * tokens, width)
+            grad_hidden = matmul(rows, w_in[2].reshape(width, heads_width)).reshape(2, tokens, heads_width)
+            slopes[p, head, :, :, lanes] = (grad_hidden * slopes[p, head, :, :, lanes].astype(F32)).astype(BF16)
+            activated[p, head, :, :, lanes] = (
+                grad_hidden * activated[p, head, :, :, lanes].astype(F32)
+            ).astype(BF16)
+
+        tiles(body)
         for w, made in enumerate((slopes, activated)):
-            there = slice((2 * j + w) * size, (2 * j + w + 1) * size)
-            writes.append(copies.inside(made.at[:, :, :, :, here], grads_out.at[:, :, :, :, there]))
+            first = (2 * j + w) * size + lane
+            there = slice(first, first + heads_width)
+            writes.append(copies.inside(made.at[:, :, :, :, lanes], grads_out.at[:, :, :, :, there]))
 
     reach(n_att + 1, stages + 1)
     forward(0)
@@ -1122,10 +1123,14 @@
         load.wait()
     step(9)
     reach(n_att + 4, stages + 1)
-    backward(0)
+    for lane in quarters:
+        backward(0, lane)
     step(10)
+    reach(n_att + 5, stages + 1)
+    backward(1, 0)
     step(11)
-    backward(1)
+    step(12)
+    backward(1, heads_width)
     for copy in writes:
         copy.wait()
     copies.finish()
@@ -1197,55 +1202,51 @@
 
 
 class GradHalving:
-    def __init__(self, copies, kept, first_copy, landed, room, final, own, other):
-        self.copies, self.kept, self.copy, self.landed = copies, kept, first_copy, landed
-        self.room, self.final, self.own, self.other = room, final, own, other
-        self.stages = replica_stages()[::-1]
-        self.stage, self.state = 0, "sent"
-
-    def reach(self, stage, state):
-        order = ("sent", "here", "added")
-        while (self.stage, order.index(self.state)) < (stage, order.index(state)):
-            if self.state == "sent":
-                self.copy.wait_recv()
-                self.state = "here"
-            elif self.state == "here":
-                self.add()
-                self.state = "added"
-            else:
-                self.stage += 1
-                self.send()
-                self.state = "sent"
+    def __init__(self, copies, held, stored, landed, final, own, other):
+        self.copies, self.held, self.stored, self.landed = copies, held, stored, landed
+        self.final, self.own, self.other = final, own, other
+        self.stages = replica_stages()[::-1][1:]
+        self.stage, self.copy = -1, None
 
     def send(self):
-        copies, kept, stage = self.copies, self.kept, self.stage
-        if stage == len(self.stages):
-            self.copy = copies.remote(kept.at[1, 0], self.other, "blk", 1)
+        copies, held = self.copies, self.held
+        for store in self.stored:
+            store.wait()
+        self.stored = []
+        self.stage += 1
+        if self.stage == len(self.stages):
+            self.copy = copies.remote(held.at[1, 0], self.other, "blk", 1)
             return
-        count = kept.shape[1] >> (stage - 1)
+        count = held.shape[1] >> self.stage
         self.copy = copies.remote(
-            kept.at[:, count // 2 : count], self.landed[stage], *self.stages[stage]
+            held.at[:, count // 2 : count], self.landed[self.stage], *self.stages[self.stage]
         )
 
-    def add(self):
-        copies, kept, stage = self.copies, self.kept, self.stage
-        if stage == len(self.stages):
-            return
-        count = kept.shape[1] >> stage
-        columns = kept.shape[-1]
-        mine, came = (part.at[:, 0:count, :, 0:columns] for part in self.room)
-        loads = [copies.inside(kept.at[:, 0:count], mine), copies.inside(self.landed[stage], came)]
-        for load in loads:
+    def arrive(self):
+        self.copy.wait_recv()
+
+    def load(self, rooms):
+        count = self.held.shape[1] >> (self.stage + 1)
+        columns = self.held.shape[-1]
+        self.mine, self.came = (room.at[:, 0:count, :, 0:columns] for room in rooms)
+        self.count = count
+        self.loads = [
+            self.copies.inside(self.held.at[:, 0:count], self.mine),
+            self.copies.inside(self.landed[self.stage], self.came),
+        ]
+
+    def combine(self):
+        copies, mine, came, count = self.copies, self.mine, self.came, self.count
+        columns = self.held.shape[-1]
+        for load in self.loads:
             load.wait()
-        if stage == len(self.stages) - 1:
+        if self.stage == len(self.stages) - 1:
             self.final[:, 0:columns] = mine[0, 0].astype(F32) + came[0, 0].astype(F32)
             mine[1, 0] = (mine[1, 0].astype(F32) + came[1, 0].astype(F32)).astype(BF16)
-            stores = [
+            self.stored = [
                 copies.inside(self.final.at[:, 0:columns], self.own),
-                copies.inside(mine.at[1, 0], kept.at[1, 0]),
+                copies.inside(mine.at[1, 0], self.held.at[1, 0]),
             ]
-            for store in stores:
-                store.wait()
             return
 
         def one(i, carry):
@@ -1254,12 +1255,12 @@
             return carry
 
         lax.fori_loop(0, 2 * count, one, 0)
-        copies.inside(mine, kept.at[:, 0:count]).wait()
+        self.stored = [copies.inside(mine, self.held.at[:, 0:count])]
 
 
 def pair_back_kernel(sizes, *refs):
     n_mlp, n_att = sizes
-    stages = len(replica_stages())
+    stages = len(replica_stages()) - 1
 
     def take(number):
         nonlocal refs
@@ -1271,91 +1272,140 @@
     (grads_in, hidden_in), w_att = take(2), take(n_att)
     own_mlp, other_mlp, own_att, other_att = take(n_mlp), take(n_mlp), take(n_att), take(n_att)
     output_out, input_out = take(2)
-    kept_mlp, kept_att = take(n_mlp), take(n_att)
+    far_x2, far_gg, far_xg, far_rows, far_grads, far_hidden, far_attended, far_b = take(8)
+    held_mlp, held_att = take(n_mlp), take(n_att)
     landed_mlp = [take(stages) for _ in range(n_mlp)]
     landed_att = [take(stages) for _ in range(n_att)]
     (partial, leaving, came, passing, last, came_o, last_o, came_c, last_c, total, total_c, rows_g,
-     turned_g, leaves, room_a, room_b, final, grad_heads, rows_b, rows_o,
+     staged, room_a, room_b, room_c, room_d, final, grad_heads, rows_b, rows_o,
      acts, weights, seq, ready, q_s, k_s, v_s, dk_s, dv_s, send, recv, local) = refs
     parts = range(2)
     upper = lax.axis_index("blk") // 2
     tokens, width = x_ref.shape[-2:]
     heads_width = rows_o.shape[-1]
-    _, kept_pieces, piece, _ = kept_mlp[0].shape
+    size = 2 * heads_width
+    _, held_pieces, piece, _ = held_mlp[0].shape
     copies = Copies(send, recv, local)
     count = 4 * tokens
     tile = 256
+    half, quarter = width // 2, width // 4
+    core = replica_stages()[-1]
+
+    def to_core(source, target):
+        return [
+            copies.remote(
+                source.at[:, :, :, :, low * half + quarter : (low + 1) * half],
+                target.at[:, :, :, :, low * quarter : (low + 1) * quarter],
+                *core,
+            )
+            for low in range(2)
+        ]
 
     load_e = copies.inside(e_in, partial)
     load_mixed = copies.inside(mixed_in, total_c)
-    acts_load = copies.inside(x2_in, acts)
     greet_pairs()
     load_e.wait()
     for p in parts:
         total[p] = jnp.zeros_like(total[p])
     scatters = [TokenScatter(copies, partial, leaving, came, passing, last, total, p) for p in parts]
-
-    busy = []
-
-    def weight_grad(acts, grads, kept, landed, own, other):
-        part_columns = grads[0].shape[-1]
-        columns = part_columns * len(grads)
-        for copy in busy:
-            copies.wait_sent(copy)
-        busy.clear()
-        per_half = kept_pieces * piece // tile
+    x2_moves = to_core(x2_in, far_x2)
+    mlp_moves = []
+    for k in range(n_mlp):
+        first = k % (2 * n_mlp // 3) * size
+        columns = slice(first, first + size)
+        source, target = (grads_in, far_grads) if k < 2 * n_mlp // 3 else (hidden_in, far_hidden)
+        if k == 2 * n_mlp // 3:
+            gg_moves = to_core(gg_in, far_gg)
+        mlp_moves.append(
+            copies.remote(source.at[:, :, :, :, columns], target.at[:, :, :, :, columns], *core)
+        )
+    xg_moves = to_core(xg_in, far_xg)
+    attended_move = copies.remote(attended_in, far_attended, *core)
+
+    def load_acts(source, far, moves):
+        loads = [
+            copies.inside(
+                source.at[:, :, :, :, low * half : low * half + quarter],
+                acts.at[0, :, :, :, :, low * quarter : (low + 1) * quarter],
+            )
+            for low in range(2)
+        ]
+        for move in moves:
+            move.wait_recv()
+        return loads + [copies.inside(far, acts.at[1])]
+
+    chunks = []
+    staging = []
+
+    def weight_grad(lefts, held, landed, own, other):
+        part_columns = lefts[0][2][0].shape[-1]
+        columns = part_columns * len(lefts[0][2])
+        for store in staging:
+            store.wait()
+        staging.clear()
         pieces = tile // piece
-        for side in (1, 0):
-            side_room = leaves if side else room_a
-
-            def one(i, carry, side=side, side_room=side_room):
-                low, part = i // per_half, i % per_half
-                start = low * (2 * kept_pieces * piece) + side * (kept_pieces * piece) + part * tile
-                lanes = pl.ds(pl.multiple_of(start, tile), tile)
-                left = acts[:, :, :, :, lanes].reshape(2 * count, tile)
-                for j, right in enumerate(grads):
-                    product = matmul_tn(left, right[...].reshape(2 * count, part_columns)).astype(BF16)
-                    columns_here = slice(j * part_columns, (j + 1) * part_columns)
-                    side_room[low, pl.ds(part * pieces, pieces), :, columns_here] = product.reshape(
-                        pieces, piece, part_columns
-                    )
-                return carry
-
-            lax.fori_loop(0, 2 * per_half, one, 0)
-            source = side_room.at[:, :, :, 0:columns]
-            if side:
-                first = copies.remote(source, landed[0], *replica_stages()[-1])
-                busy.append(first)
-            else:
-                copies.inside(source, kept).wait()
-        chunks.append(GradHalving(copies, kept, first, landed, (room_a, room_b), final, own, other))
-
-    chunks = []
-
-    def reach(k, stage, state):
-        if 0 <= k < len(chunks):
-            chunks[k].reach(stage, state)
+        per_low = quarter // tile
+
+        def one(i, carry):
+            low, part = i // per_low, i % per_low
+            for j in range(len(lefts[0][2])):
+                product = None
+                for stride, left, rights in lefts:
+                    lanes = pl.ds(pl.multiple_of(low * stride + part * tile, tile), tile)
+                    rows = left[:, :, :, :, lanes].reshape(2 * count, tile)
+                    term = matmul_tn(rows, rights[j][...].reshape(2 * count, part_columns))
+                    product = term if product is None else product + term
+                staged[low, pl.ds(part * pieces, pieces), :, j * part_columns : (j + 1) * part_columns] = (
+                    product.astype(BF16).reshape(pieces, piece, part_columns)
+                )
+            return carry
+
+        lax.fori_loop(0, 2 * per_low, one, 0)
+        store = copies.inside(staged.at[:, :, :, 0:columns], held)
+        staging.append(store)
+        chunks.append(GradHalving(copies, held, [], landed, final, own, other))
+
+    def send(k):
+        if k < len(chunks) and chunks[k].stage < 0:
+            if k == len(chunks) - 1:
+                for store in staging:
+                    store.wait()
+                staging.clear()
+            chunks[k].send()
 
     done = [0]
 
     def step():
         k = done[0]
         done[0] += 1
-        reach(k + 1, 1, "sent")
-        reach(k, 2, "sent")
-        reach(k - 1, 3, "sent")
-        reach(k - 2, 3, "here")
+        here = []
+        for at, rooms in ((k, (room_a, room_b)), (k - 1, (room_c, room_d))):
+            if 0 <= at < len(chunks):
+                chunks[at].arrive()
+                if at == k:
+                    send(k + 1)
+                chunks[at].load(rooms)
+                here.append(chunks[at])
+        for chunk in here:
+            chunk.combine()
+        for chunk in here:
+            chunk.send()
+        if 0 <= k - 2 < len(chunks):
+            chunks[k - 2].arrive()
 
     def load_grads(k):
+        own_source, far_source = (grads_in, far_grads) if k < 2 * n_mlp // 3 else (hidden_in, far_hidden)
+        mlp_moves[k].wait_recv()
         loads = []
-        for half_of in range(2):
-            for row in range(2 * kept_pieces):
-                source = grads_in if k < 2 * n_mlp // 3 else hidden_in
-                first = k % (2 * n_mlp // 3) * 2 * heads_width + half_of * heads_width
-                source = source.at[row // 4, row // 2 % 2, row % 2, :, first : first + heads_width]
-                loads.append(copies.inside(source, weights.at[k % 2, half_of, row]))
+        for device, source in enumerate((own_source, far_source)):
+            for half_of in range(2):
+                first = k % (2 * n_mlp // 3) * size + half_of * heads_width
+                for row in range(8):
+                    part = source.at[row // 4, row // 2 % 2, row % 2, :, first : first + heads_width]
+                    loads.append(copies.inside(part, weights.at[2 * (k % 2) + device, half_of, row]))
         return loads
 
+    acts_loads = load_acts(x2_in, far_x2, x2_moves)
     slots = [load_grads(0)]
 
     def mlp_chunk(k):
@@ -1363,13 +1413,17 @@
             load.wait()
         if k + 1 < n_mlp:
             slots.append(load_grads(k + 1))
-        halves = [weights.at[k % 2, half_of] for half_of in range(2)]
-        weight_grad(acts, halves, kept_mlp[k], landed_mlp[k], own_mlp[k], other_mlp[k])
-
-    acts_load.wait()
+        lefts = [
+            (quarter, acts.at[device], [weights.at[2 * (k % 2) + device, half_of] for half_of in range(2)])
+            for device in range(2)
+        ]
+        weight_grad(lefts, held_mlp[k], landed_mlp[k], own_mlp[k], other_mlp[k])
+
+    for load in acts_loads:
+        load.wait()
     mlp_chunk(0)
+    send(0)
     mlp_chunk(1)
-    reach(0, 1, "sent")
     for scatter in scatters:
         scatter.second()
     load_mixed.wait()
@@ -1382,24 +1436,30 @@
         scale = lax.rsqrt(jnp.mean(mixed * mixed, -1, keepdims=True) + EPSILON)
         total[p] = g_ref[p].astype(F32) + norm_back(total[p], mixed, scale)
         rows_g[p, 0, 0] = total[p].astype(BF16)
-        gathers.append(TokenGather(copies, rows_g, turned_g, p))
+    for p in parts:
+        gathers.append(TokenGather(copies, rows_g, leaving, p))
     load_produced = copies.inside(produced_in, partial)
     step()
     mlp_chunk(3)
-    acts_load = copies.inside(gg_in, acts)
+    acts_loads = load_acts(gg_in, far_gg, gg_moves)
     for gather in gathers:
         gather.second()
-    acts_load.wait()
+    for load in acts_loads:
+        load.wait()
     mlp_chunk(4)
+    mlp_chunk(5)
     step()
-    mlp_chunk(5)
     w_loads = [copies.inside(w_att[i], weights.at[slot]) for i, slot in ((3, 0), (0, 1), (1, 2))]
     load_seq = copies.inside(seq_in, seq)
     load_rows_o = [copies.inside(attended_in.at[p], rows_o.at[4 * p : 4 * p + 4]) for p in parts]
+    attended_move.wait_recv()
+    load_rows_o += [copies.inside(far_attended.at[p], weights.at[3, 0, 4 * p : 4 * p + 4]) for p in parts]
     for gather in gathers:
         gather.end()
+        gather.release()
+    rows_moves = to_core(rows_g, far_rows)
     load_produced.wait()
-    scatters = [TokenScatter(copies, partial, leaving, came_o, passing, last_o, total_c, p, True) for p in parts]
+    scatters = [TokenScatter(copies, partial, leaving, came_o, passing, last_o, total_c, p) for p in parts]
     w_loads[0].wait()
     for p in parts:
         rows = rows_g[p].reshape(count, width)
@@ -1407,63 +1467,80 @@
         for group in range(4):
             grad_heads[p, group] = product[group * tokens : (group + 1) * tokens]
     w_loads.append(copies.inside(w_att[2], weights.at[0]))
-    for load in load_rows_o:
+    step()
+    for move in rows_moves:
+        move.wait_recv()
+    far_load = copies.inside(far_rows, acts.at[1])
+    for load in load_rows_o + [far_load]:
         load.wait()
-    weight_grad(rows_g, [rows_o], kept_att[3], landed_att[3], own_att[3], other_att[3])
-    step()
+    lefts = [(half, rows_g, [rows_o]), (quarter, acts.at[1], [weights.at[3, 0]])]
+    weight_grad(lefts, held_att[3], landed_att[3], own_att[3], other_att[3])
+    acts_loads = load_acts(xg_in, far_xg, xg_moves)
     load_seq.wait()
     lanes = cosine_ref.shape[1]
     for at, lane in enumerate(range(0, heads_width, lanes)):
         attend_pair_back(seq, grad_heads, rows_b, lane, cosine_ref, sine_ref, (q_s, k_s, v_s), (dk_s, dv_s))
-        if at == 0:
+        if at == 2:
             for scatter in scatters:
                 scatter.second()
-        step()
-    trades = []
-    for p in parts:
-        scatters[p].end()
-        scatters[p].release()
-        to_absolute_order(total_c[p].astype(BF16), ready, p, piece)
-    stores = [copies.inside(ready.at[0], output_out.at[upper])]
-    trades.append(copies.remote(ready.at[1], output_out.at[upper], "blk", 2))
-    acts_load = copies.inside(xg_in, acts)
+        if at % 2:
+            step()
+    b_moves = [copies.remote(rows_b.at[i], far_b.at[i], *core) for i in range(3)]
     for load in w_loads[1:]:
         load.wait()
-    scatters = []
+    out_scatters, scatters = scatters, []
     for p in parts:
+        out_scatters[p].release_first()
         pieces = tile // piece
         for start in range(0, width, tile):
-            low, first = start // (2 * kept_pieces * piece), start // piece % (2 * kept_pieces)
+            low, first = start // half, start // piece % (half // piece)
             terms = []
             for i in range(3):
                 weight = weights[(i + 1) % 3, low, first : first + pieces].reshape(tile, heads_width)
                 terms.append(matmul_nt(rows_b[i, 4 * p : 4 * p + 4].reshape(count, heads_width), weight))
             product = functools.reduce(jnp.add, terms).astype(BF16)
             store_product(product, partial, p, slice(start, start + tile))
+        scatters.append(TokenScatter(copies, partial, leaving, came_c, passing, last_c, total_c, p, True))
+    step()
+    b_loads = []
+    for i in range(3):
+        b_moves[i].wait_recv()
+        b_loads.append(copies.inside(far_b.at[i], weights.at[i, 0]))
+    for load in acts_loads:
+        load.wait()
+    for i in range(3):
+        b_loads[i].wait()
+        lefts = [(quarter, acts.at[0], [rows_b.at[i]]), (quarter, acts.at[1], [weights.at[i, 0]])]
+        weight_grad(lefts, held_att[i], landed_att[i], own_att[i], other_att[i])
+    for p in parts:
+        out_scatters[p].end()
+        out_scatters[p].release_last()
+        to_absolute_order(total_c[p].astype(BF16), ready, p, piece)
         total_c[p] = jnp.zeros_like(total_c[p])
-        scatters.append(TokenScatter(copies, partial, leaving, came_c, passing, last_c, total_c, p))
-    acts_load.wait()
-    for i in range(3):
-        weight_grad(acts, [rows_b.at[i]], kept_att[i], landed_att[i], own_att[i], other_att[i])
-    step()
+    stores = [copies.inside(ready.at[0], output_out.at[upper])]
     for scatter in scatters:
         scatter.second()
     step()
-    for store in stores:
-        store.wait()
-    copies.wait_sent(trades[0])
+    send(len(chunks) - 2)
+    trades = [copies.remote(ready.at[1], output_out.at[upper], "blk", 2)]
+    step()
+    send(len(chunks) - 1)
     for p in parts:
         scatters[p].end()
         scatters[p].release()
         values = x_ref[p].astype(F32)
         scale = lax.rsqrt(jnp.mean(values * values, -1, keepdims=True) + EPSILON)
-        rows = (total[p] + norm_back(total_c[p], values, scale)).astype(BF16)
-        to_absolute_order(rows, ready, p, piece)
-    store = copies.inside(ready.at[0], input_out.at[upper])
+        total[p] += norm_back(total_c[p], values, scale)
+    stores[0].wait()
+    copies.wait_sent(trades[0])
+    for p in parts:
+        to_absolute_order(total[p].astype(BF16), ready, p, piece)
+    stores = [copies.inside(ready.at[0], input_out.at[upper])]
     trades.append(copies.remote(ready.at[1], input_out.at[upper], "blk", 2))
     while done[0] < len(chunks) + 2:
         step()
-    store.wait()
+    for store in stores:
+        store.wait()
     for trade in trades:
         trade.wait_recv()
     copies.finish()
@@ -1475,7 +1552,7 @@
     _, replicas, piece, heads_width = w_att[0].shape
     columns = 2 * heads_width
     n_mlp, n_att = sum(g.shape[-1] for g in grads) // columns, len(w_att)
-    stages = len(replica_stages())
+    stages = len(replica_stages()) - 1
     any_space = pl.BlockSpec(memory_space=pl.ANY)
     in_vmem = pl.BlockSpec(memory_space=pltpu.VMEM)
 
@@ -1489,14 +1566,15 @@
         return pltpu.VMEM(shape, BF16)
 
     widths = [columns] * n_mlp + [heads_width] * n_att
+    token_rows, own, pair = (2, 2, 2, tokens, width), (2, tokens, width), (2, 2, tokens, width)
+    half_rows = (2, 2, 2, tokens, width // 2)
     outs = [f32(piece, columns)] * n_mlp + [bf16(piece, columns)] * n_mlp
     outs += [f32(piece, heads_width)] * n_att + [bf16(piece, heads_width)] * n_att
     outs += [bf16(2, tokens, width)] * 2
+    outs += [bf16(*half_rows)] * 4 + [bf16(*g.shape) for g in grads]
+    outs += [bf16(2, 4, tokens, heads_width), bf16(3, 8, tokens, heads_width)]
     outs += [bf16(2, replicas // 2, piece, w) for w in widths]
-    outs += [bf16(2, replicas >> (s + 1), piece, w) for w in widths for s in range(stages)]
-    token_rows, own, pair = (2, 2, 2, tokens, width), (2, tokens, width), (2, 2, tokens, width)
-    widest = max(columns, heads_width)
-    half_room = (2, replicas // 2, piece, widest)
+    outs += [bf16(2, replicas >> (s + 2), piece, w) for w in widths for s in range(stages)]
     scratch = [
         room(*token_rows),
         room(*pair),
@@ -1510,23 +1588,22 @@
         pltpu.VMEM(own, F32),
         pltpu.VMEM(own, F32),
         room(*token_rows),
-        room(*pair),
-        room(*half_room),
-        room(*half_room),
-        room(*half_room),
-        pltpu.VMEM((piece, widest), F32),
+        room(2, replicas // 2, piece, columns),
+        *[room(2, replicas // 4, piece, columns)] * 2,
+        *[room(2, replicas // 8, piece, columns)] * 2,
+        pltpu.VMEM((piece, columns), F32),
         room(2, 4, tokens, heads_width),
         room(3, 8, tokens, heads_width),
         room(8, tokens, heads_width),
-        room(*token_rows),
-        room(3, 2, replicas, piece, heads_width),
+        room(2, *half_rows),
+        room(4, 2, replicas, piece, heads_width),
         room(3, 2, 4, tokens, heads_width),
         room(*own),
         *[room(*tables[0].shape)] * 3,
         *[pltpu.VMEM(tables[0].shape, F32)] * 2,
-        pltpu.SemaphoreType.DMA((96,)),
-        pltpu.SemaphoreType.DMA((96,)),
-        pltpu.SemaphoreType.DMA((384,)),
+        pltpu.SemaphoreType.DMA((128,)),
+        pltpu.SemaphoreType.DMA((128,)),
+        pltpu.SemaphoreType.DMA((448,)),
     ]
     results = pl.pallas_call(
         functools.partial(pair_back_kernel, (n_mlp, n_att)),

time: 813 us -> 765 us (0.941)
  Pallas kernels: 736 us -> 692 us
    pallas_call x1, Pallas kernels: 388 us -> 366 us  [pair_front(): pl.pallas_call(functools.partial(pair_front_kernel, (n_att, n_mlp)), out_...]
    pallas_call x1, Pallas kernels: 348 us -> 326 us  [pair_back(): pl.pallas_call(functools.partial(pair_back_kernel, (n_mlp, n_att)), out_s...]
where the time goes in v5:
time: 765 us; the launch traced here: 757 us
  Pallas kernels  692 us (90%)
  matrix products  33.5 us (4%)
  local copies, waits for them, and re-layouts  15.7 us (2%)
  other arithmetic  12.7 us (2%)
    pallas_call x1, Pallas kernels, pair_front(): pl.pallas_call(functools.partial(pair_front_kernel, (n_att, n_mlp)), out_...  366 us
    pallas_call x1, Pallas kernels, pair_back(): pl.pallas_call(functools.partial(pair_back_kernel, (n_mlp, n_att)), out_s...  326 us
    dot_general x2, matrix products, matmul_nt(): lax.dot_general(left_side, right_side, (((1,), (1,)), ((), ())), preferre...  33.5 us
  transfers between devices with their start and end apart: 2, of which 0 were waited for; matrix products, arithmetic and copies ran while one was open for 1% of the time, Pallas kernels for 0%

profile of v5, /device:TPU:0, one launch (start us, length us, event | category | flops | bytes accessed | tf_op | source)
XLA Modules:
  0.0 756.6 jit_solution(10476913997763048781)
XLA Ops:
  0.7 0.7 convert_element_type.69
  1.4 2.1 fusion.6
  3.5 0.7 copy.54
  4.2 0.8 copy.36
  5.1 1.5 copy.39
  6.6 1.0 bitcast_bitcast_fusion.2
  8.4 2.0 pad_maximum_fusion.refs_3_
  10.4 1.1 pad_maximum_fusion.3.refs_2_
  11.5 365.5 %shard_map.212 = (bf16[2,8,128,512]{3,2,1,0:T(8,128)(2,1)}, bf16[2,8,128,512]{3,2,1,0:T(8,128)(2,1)}, bf16[2,8,128,512]{3,2,1,0:T(8,128)(2,1)}, bf16[2,8,128,512...) custom-call(bf16[2,1,128,2048]{3,2,1,0:T(8,128)(2,1)} %refs_0_.1, ...), custom_call_target="tpu_custom_call" | custom-call | tf_op jit(solution)/shard_map/pallas_call | solution.py:1190
  377.0 14.1 %convolution_convert_fusion.1 = bf16[1024,2048]{1,0:T(8,128)(2,1)} fusion(bf16[1024,2048]{1,0:T(8,128)(2,1)} %bitcast.70, bf16[2048,2048]{1,0:T(8,128)(2,1)} %bitcast.86), kind=kOutput, calls=%fused_computation.1 | convolution fusion | flops 8592031744 | bytes 16777216 | tf_op jit(solution)/shard_map/dot_general | solution.py:40
  391.1 19.5 %convolution_convert_fusion = bf16[1024,2048]{1,0:T(8,128)(2,1)} fusion(bf16[1024,4096]{1,0:T(8,128)(2,1)S(1)} %bitcast.69, bf16[2048,4096]{1,0:T(8,128)(2,1)S(1)} %bitcast.85), kind=kOutput, calls=%fused_computation | convolution fusion | flops 17181966336 | bytes 29360128 | tf_op jit(solution)/shard_map/dot_general | solution.py:40
  410.6 326.4 %shard_map.213 = (f32[128,1024]{1,0:T(8,128)}, f32[128,1024]{1,0:T(8,128)}, f32[128,1024]{1,0:T(8,128)}, f32[128,1024]{1,0:T(8,128)}, f32[128,1024]{1,0:T(8,128)...) custom-call(bf16[2,2,2,128,2048]{4,3,2,1,0:T(8,128)(2,1)} %bitcast.7, ...), custom_call_target="tpu_custom_call" | custom-call | tf_op jit(solution)/shard_map/pallas_call | solution.py:1608
  737.0 1.2 constant_dynamic-update-slice_fusion.1
  738.2 1.1 constant_dynamic-update-slice_fusion.3
  739.7 0.6 copy-done.22
  741.3 2.8 fusion.4
  744.4 0.6 copy-done.6
  745.2 1.4 fusion.12
  746.6 1.3 collective-permute-start
  748.4 0.8 copy-done.15
  749.3 1.8 copy.43
  751.1 1.0 copy.42
  753.2 2.3 copy.60
  755.5 1.0 copy.61
  (84 shorter events, 4.0 us)
Async XLA Ops:
  0.6 3.6 copy-start.19
  0.7 4.4 copy-start.31
  3.5 4.1 copy-start.1
  3.5 4.1 copy-start.3
  8.3 2.0 copy-start.9
  377.0 14.1 %copy-start = (bf16[2,2,2,128,4096]{4,3,2,1,0:T(8,128)(2,1)S(1)}, bf16[2,2,2,128,4096]{4,3,2,1,0:T(8,128)(2,1)}, u32[]{:S(2)}) copy-start(bf16[2,2,2,128,4096]{4,3,2,1,0:T(8,128)(2,1)} %get-tuple-element.49.refs_12_) | copy-start | bytes 25165828
  377.0 14.1 %copy-start.30 = (bf16[2,8,128,4096]{3,2,1,0:T(8,128)(2,1)S(1)}, bf16[2,8,128,4096]{3,2,1,0:T(8,128)(2,1)}, u32[]{:S(2)}) copy-start(bf16[2,8,128,4096]{3,2,1,0:T(8,128)(2,1)} %get-tuple-element.50) | copy-start | bytes 50331652
  737.0 2.3 copy-start.14
  737.0 2.4 copy-start.13
  737.0 2.4 copy-start.24
  737.0 2.4 copy-start.25
  741.3 2.9 copy-start.18
  741.3 2.9 copy-start.29
  741.3 3.0 copy-start.17
  741.3 3.0 copy-start.28
  741.3 3.1 copy-start.16
  741.3 3.1 copy-start.27
  744.1 8.0 %collective-permute-start.1 = (f32[128]{0:T(128)S(1)}, f32[128]{0:T(128)S(1)}, u32[]{:S(2)}, u32[]{:S(2)}) collective-permute-start(f32[128]{0:T(128)S(1)} %add.29), channel_id=1, source_target_pairs={{0,4},{4,0},{1,5},{5,1},{2,6},{6,2},{3,7},{7,3},{8,12},{12,8},{9,1... | collective-permute-start | bytes 1544 | tf_op jit(solution)/shard_map/ppermute | solution.py:23
  744.4 3.4 copy-start.12
  745.2 2.7 copy-start.11
  745.2 2.8 copy-start.20
  745.2 2.8 copy-start.21
  746.6 6.1 collective-permute-start
  751.1 4.3 copy-start.5
  (10 other events, 11.8 us)

commit v6 on v5

--- a/solution.py
+++ b/solution.py
@@ -408,74 +408,100 @@
         self.stage += 1
 
 
+def lane_halves(width):
+    return [slice(0, width // 2), slice(width // 2, width)]
+
+
 class TokenGather:
     def __init__(self, copies, rows, turned_rows, m, head_first=None):
         self.copies, self.rows, self.turned_rows, self.m = copies, rows, turned_rows, m
         self.head_first = m % 2 == 1 if head_first is None else head_first
+        self.halves = lane_halves(rows.shape[-1])
+        self.first, self.last = [], []
+        for here, there in zip(self.halves, self.halves[::-1]):
+            if self.head_first:
+                copy = copies.remote(rows.at[m, 0, 0, :, here], rows.at[m, 1, 0, :, here], "head", 1)
+            else:
+                turned_rows[m, 0, :, there] = rows[m, 0, 0, :, here]
+                copy = copies.remote(turned_rows.at[m, 0, :, there], rows.at[m, 0, 1, :, there], "blk", 1)
+            self.first.append(copy)
+
+    def second_half(self, h):
+        m, rows, turned_rows = self.m, self.rows, self.turned_rows
+        here, there = self.halves[h], self.halves[1 - h]
+        self.first[h].wait_recv()
         if self.head_first:
-            self.copy = copies.remote(rows.at[m, 0, 0], rows.at[m, 1, 0], "head", 1)
+            turned_rows[m, 0, :, there] = rows[m, 0, 0, :, here]
+            turned_rows[m, 1, :, there] = rows[m, 1, 0, :, here]
+            copy = self.copies.remote(turned_rows.at[m, :, :, there], rows.at[m, :, 1, :, there], "blk", 1)
         else:
-            turned_rows[m, 0] = halves_turned(rows[m, 0, 0])
-            self.copy = copies.remote(turned_rows.at[m, 0], rows.at[m, 0, 1], "blk", 1)
-        self.first = self.copy
+            copy = self.copies.remote(rows.at[m, 0, :, :, there], rows.at[m, 1, :, :, there], "head", 1)
+        self.last.append(copy)
 
     def second(self):
-        m, rows, turned_rows = self.m, self.rows, self.turned_rows
-        self.copy.wait_recv()
-        if self.head_first:
-            turned_rows[m, 0] = halves_turned(rows[m, 0, 0])
-            turned_rows[m, 1] = halves_turned(rows[m, 1, 0])
-            self.copy = self.copies.remote(turned_rows.at[m], rows.at[m, :, 1], "blk", 1)
-        else:
-            self.copy = self.copies.remote(rows.at[m, 0], rows.at[m, 1], "head", 1)
+        seconds([self])
 
     def end(self):
-        self.copy.wait_recv()
+        for copy in self.last:
+            copy.wait_recv()
 
     def release(self):
-        self.copies.wait_sent(self.first)
-        self.copies.wait_sent(self.copy)
+        for copy in self.first + self.last:
+            self.copies.wait_sent(copy)
 
 
 class TokenScatter:
     def __init__(self, copies, partial, leaving, came, passing, last, total, m, head_first=None):
         self.copies, self.partial, self.came, self.passing = copies, partial, came, passing
-        self.last, self.total, self.m = last, total, m
+        self.arrived, self.total, self.m = last, total, m
         self.head_first = m % 2 == 0 if head_first is None else head_first
-        if self.head_first:
-            self.copy = copies.remote(partial.at[m, 1], came.at[m], "head", 1)
-        else:
-            leaving[m, 0] = halves_turned(partial[m, 0, 1])
-            leaving[m, 1] = halves_turned(partial[m, 1, 1])
-            self.copy = copies.remote(leaving.at[m], came.at[m], "blk", 1)
-        self.first = self.copy
+        self.halves = lane_halves(partial.shape[-1])
+        self.first, self.last = [], []
+        for here, there in zip(self.halves, self.halves[::-1]):
+            if self.head_first:
+                copy = copies.remote(partial.at[m, 1, :, :, here], came.at[m, :, :, here], "head", 1)
+            else:
+                leaving[m, 0, :, there] = partial[m, 0, 1, :, here]
+                leaving[m, 1, :, there] = partial[m, 1, 1, :, here]
+                copy = copies.remote(leaving.at[m, :, :, there], came.at[m, :, :, there], "blk", 1)
+            self.first.append(copy)
+
+    def second_half(self, h):
+        m, partial, came = self.m, self.partial, self.came
+        self.first[h].wait_recv()
+        here = self.halves[h] if self.head_first else self.halves[1 - h]
+        there = self.halves[1 - h] if self.head_first else here
+        kept = partial[m, 0, 1, :, here] if self.head_first else partial[m, 1, 0, :, here]
+        self.passing[m, :, there] = (kept.astype(F32) + came[m, 1, :, here].astype(F32)).astype(BF16)
+        axis = "blk" if self.head_first else "head"
+        self.last.append(self.copies.remote(self.passing.at[m, :, there], self.arrived.at[m, :, there], axis, 1))
+        self.total[m, :, here] += partial[m, 0, 0, :, here].astype(F32) + came[m, 0, :, here].astype(F32)
 
     def second(self):
-        m, partial = self.m, self.partial
-        self.copy.wait_recv()
-        kept = partial[m, 0, 1] if self.head_first else partial[m, 1, 0]
-        theirs = (kept.astype(F32) + self.came[m, 1].astype(F32)).astype(BF16)
-        if self.head_first:
-            self.passing[m] = halves_turned(theirs)
-            self.copy = self.copies.remote(self.passing.at[m], self.last.at[m], "blk", 1)
-        else:
-            self.passing[m] = theirs
-            self.copy = self.copies.remote(self.passing.at[m], self.last.at[m], "head", 1)
-        self.total[m] += partial[m, 0, 0].astype(F32) + self.came[m, 0].astype(F32)
+        seconds([self])
 
     def end(self):
-        self.copy.wait_recv()
-        self.total[self.m] += self.last[self.m].astype(F32)
+        for copy in self.last:
+            copy.wait_recv()
+        self.total[self.m] += self.arrived[self.m].astype(F32)
 
     def release_first(self):
-        self.copies.wait_sent(self.first)
+        for copy in self.first:
+            self.copies.wait_sent(copy)
 
     def release_last(self):
-        self.copies.wait_sent(self.copy)
+        for copy in self.last:
+            self.copies.wait_sent(copy)
 
     def release(self):
         self.release_first()
         self.release_last()
+
+
+def seconds(ways):
+    for h in range(2):
+        for way in ways:
+            way.second_half(h)
 
 
 def place_of(block):
@@ -910,8 +936,9 @@
 
 def pair_front_kernel(sizes, *refs):
     n_att, n_mlp = sizes
-    x_in, g_in, att_in, mlp_in, cosine_ref, sine_ref = refs[:6]
-    refs = refs[6:]
+    (x_in, g_in), refs = refs[:2], refs[2:]
+    att_in, mlp_in, refs = refs[:n_att], refs[n_att : n_att + 3], refs[n_att + 3 :]
+    (cosine_ref, sine_ref), refs = refs[:2], refs[2:]
     w_att, refs = refs[:n_att], refs[n_att:]
     (w_gu, w_down, grads_out, hidden_out), refs = refs[:4], refs[4:]
     xg_out, seq_out, attended_out, mixed_out, x2_out, gg_out, x_out, g_out = refs[:8]
@@ -932,14 +959,14 @@
     trade = copies.remote(x_in.at[1 - upper, 0], x_raw.at[1], "blk", 2)
 
     def att_chunk(i):
-        return lambda: WeightGather(copies, att_in.at[i, near], att_in.at[i, 1 - near], w_att[i])
+        return lambda: WeightGather(copies, att_in[i].at[near], att_in[i].at[1 - near], w_att[i])
 
     def mlp_chunk(w, j, columns):
         per_weight = n_mlp // 3
-        size = mlp_in.shape[-1]
+        size = mlp_in[w].shape[-1]
         first = (2 * j + w if w < 2 else j) * size + columns.start
         full = (w_gu if w < 2 else w_down).at[:, :, :, first : first + columns.stop - columns.start]
-        own, other = (mlp_in.at[w, at * per_weight + j, :, columns] for at in (near, 1 - near))
+        own, other = (mlp_in[w].at[at * per_weight + j, :, columns] for at in (near, 1 - near))
         return lambda: WeightGather(copies, own, other, full)
 
     whole, halves = slice(0, 2 * heads_width), [slice(0, heads_width), slice(heads_width, 2 * heads_width)]
@@ -1032,8 +1059,7 @@
         scatters.append(TokenScatter(copies, partial, leaving, came, passing, last, mixed, p))
     writes.append(copies.inside(attended, attended_out))
     step(4)
-    for scatter in scatters:
-        scatter.second()
+    seconds(scatters)
     far = []
     for p, (mine, turned_copy) in enumerate(grad_rows):
         mine.wait()
@@ -1047,8 +1073,7 @@
         gathers.append(TokenGather(copies, x2, turned_more, p))
     writes.append(copies.inside(mixed, mixed_out))
     step(6)
-    for gather in gathers:
-        gather.second()
+    seconds(gathers)
     step(7)
     for gather in gathers:
         gather.end()
@@ -1138,9 +1163,9 @@
 
 def pair_front(block_input, grad_output, att_in, mlp_in, tables):
     _, _, tokens, width = block_input.shape
-    n_att, _, piece, heads_width = att_in.shape
-    n_weights, parts, _, columns = mlp_in.shape
-    n_mlp = n_weights * parts // 2
+    n_att, (_, piece, heads_width) = len(att_in), att_in[0].shape
+    parts, _, columns = mlp_in[0].shape
+    n_mlp = len(mlp_in) * parts // 2
     replicas = width // piece // 2
     length, lanes = tables[0].shape
     any_space = pl.BlockSpec(memory_space=pl.ANY)
@@ -1190,13 +1215,13 @@
     results = pl.pallas_call(
         functools.partial(pair_front_kernel, (n_att, n_mlp)),
         out_shape=outs,
-        in_specs=[any_space] * 4 + [in_vmem] * 2,
+        in_specs=[any_space] * (2 + len(att_in) + len(mlp_in)) + [in_vmem] * 2,
         out_specs=[any_space] * len(outs),
         scratch_shapes=scratch,
         compiler_params=pltpu.CompilerParams(
             collective_id=2, has_side_effects=True, vmem_limit_bytes=63 * 1024 * 1024
         ),
-    )(block_input, grad_output, att_in, mlp_in, *tables)
+    )(block_input, grad_output, *att_in, *mlp_in, *tables)
     w_att, results = results[:n_att], results[n_att:]
     return w_att, results[:2], results[2:4], results[4:]
 
@@ -1424,8 +1449,7 @@
     mlp_chunk(0)
     send(0)
     mlp_chunk(1)
-    for scatter in scatters:
-        scatter.second()
+    seconds(scatters)
     load_mixed.wait()
     mlp_chunk(2)
     gathers = []
@@ -1442,8 +1466,7 @@
     step()
     mlp_chunk(3)
     acts_loads = load_acts(gg_in, far_gg, gg_moves)
-    for gather in gathers:
-        gather.second()
+    seconds(gathers)
     for load in acts_loads:
         load.wait()
     mlp_chunk(4)
@@ -1481,8 +1504,7 @@
     for at, lane in enumerate(range(0, heads_width, lanes)):
         attend_pair_back(seq, grad_heads, rows_b, lane, cosine_ref, sine_ref, (q_s, k_s, v_s), (dk_s, dv_s))
         if at == 2:
-            for scatter in scatters:
-                scatter.second()
+            seconds(scatters)
         if at % 2:
             step()
     b_moves = [copies.remote(rows_b.at[i], far_b.at[i], *core) for i in range(3)]
@@ -1518,8 +1540,7 @@
         to_absolute_order(total_c[p].astype(BF16), ready, p, piece)
         total_c[p] = jnp.zeros_like(total_c[p])
     stores = [copies.inside(ready.at[0], output_out.at[upper])]
-    for scatter in scatters:
-        scatter.second()
+    seconds(scatters)
     step()
     send(len(chunks) - 2)
     trades = [copies.remote(ready.at[1], output_out.at[upper], "blk", 2)]
@@ -1668,15 +1689,12 @@
         rows, columns = weight.shape
         return weight.reshape(rows, parts, columns // parts).swapaxes(0, 1)
 
-    att_in = jnp.stack(
-        [columns_of(scaled(w, gain_one), 2) for w in (query_weight, key_weight, value_weight)]
-        + [columns_of(output_weight.T, 2)]
-    )
-    mlp_in = jnp.stack(
-        [columns_of(scaled(w, gain_two), 4) for w in (gate_weight, up_weight)] + [columns_of(down_weight.T, 4)]
-    )
+    att_in = [columns_of(scaled(w, gain_one), 2) for w in (query_weight, key_weight, value_weight)]
+    att_in.append(columns_of(output_weight.T, 2))
+    mlp_in = [columns_of(scaled(w, gain_two), 4) for w in (gate_weight, up_weight)] + [columns_of(down_weight.T, 4)]
+    part_rows, part_columns = mlp_in[0].shape[1:]
     paired = micros == 2 and lax.axis_size("blk") == 4 and heads_width % LANES == 0 and 8 * tokens == width // 2
-    paired = paired and mlp_in.shape[-1] == 2 * heads_width == width // 2 and mlp_in.shape[-2] == tokens
+    paired = paired and part_columns == 2 * heads_width == width // 2 and part_rows == tokens
     hidden, grad_gate, grad_up = [], [], []
     grad_normed = produced = 0.0
     if paired:
@@ -1688,7 +1706,7 @@
         block_rows = [array.reshape(micros * tokens, width) for array in (block_input, grad_output)]
         inputs_low, grad_low = (rows.reshape(micros, tokens, width) for rows in reorder(to_own, *block_rows))
         grad_turned = turn_features(grad_low.reshape(micros * tokens, width)).reshape(micros, tokens, width)
-        w_att, w_mlp, held = front(inputs_low, grad_low, grad_turned, att_in, mlp_in, tables)
+        w_att, w_mlp, held = front(inputs_low, grad_low, grad_turned, jnp.stack(att_in), jnp.stack(mlp_in), tables)
         normed_one, sequences, attended, mixed, normed_two, grad_rows = held
         normed_two_all = normed_two.reshape(-1, width)
         grad_rows_all = grad_rows.reshape(-1, width)

time: 765 us -> 761 us (level)
  Pallas kernels: 692 us -> 684 us
where the time goes in v6:
time: 761 us; the launch traced here: 749 us
  Pallas kernels  684 us (90%)
  matrix products  33.5 us (4%)
  local copies, waits for them, and re-layouts  17.8 us (2%)
  other arithmetic  10.4 us (1%)
    pallas_call x1, Pallas kernels, pair_front(): pl.pallas_call(functools.partial(pair_front_kernel, (n_att, n_mlp)), out_...  362 us
    pallas_call x1, Pallas kernels, pair_back(): pl.pallas_call(functools.partial(pair_back_kernel, (n_mlp, n_att)), out_s...  322 us
    dot_general x2, matrix products, matmul_nt(): lax.dot_general(left_side, right_side, (((1,), (1,)), ((), ())), preferre...  33.5 us
  transfers between devices with their start and end apart: 2, of which 0 were waited for; matrix products, arithmetic and copies ran while one was open for 1% of the time, Pallas kernels for 0%

profile of v6, /device:TPU:0, one launch (start us, length us, event | category | flops | bytes accessed | tf_op | source)
XLA Modules:
  0.0 749.3 jit_solution(11000519771424203767)
XLA Ops:
  0.7 0.7 convert_element_type.69
  1.4 0.7 convert_element_type.76
  2.1 2.2 fusion.10
  4.2 0.7 copy.54
  4.9 1.3 copy.39
  6.2 1.8 copy.36
  8.0 1.8 bitcast_bitcast_fusion.2
  10.4 1.5 bitcast_bitcast_fusion
  11.8 362.2 %shard_map.212 = (bf16[2,8,128,512]{3,2,1,0:T(8,128)(2,1)}, bf16[2,8,128,512]{3,2,1,0:T(8,128)(2,1)}, bf16[2,8,128,512]{3,2,1,0:T(8,128)(2,1)}, bf16[2,8,128,512...) custom-call(bf16[2,1,128,2048]{3,2,1,0:T(8,128)(2,1)} %refs_0_.1, ...), custom_call_target="tpu_custom_call" | custom-call | tf_op jit(solution)/shard_map/pallas_call | solution.py:1215
  374.1 14.1 %convolution_convert_fusion.1 = bf16[1024,2048]{1,0:T(8,128)(2,1)} fusion(bf16[1024,2048]{1,0:T(8,128)(2,1)} %bitcast.56, bf16[2048,2048]{1,0:T(8,128)(2,1)} %bitcast.72), kind=kOutput, calls=%fused_computation.1 | convolution fusion | flops 8592031744 | bytes 16777216 | tf_op jit(solution)/shard_map/dot_general | solution.py:40
  388.2 19.4 %convolution_convert_fusion = bf16[1024,2048]{1,0:T(8,128)(2,1)} fusion(bf16[1024,4096]{1,0:T(8,128)(2,1)S(1)} %bitcast.55, bf16[2048,4096]{1,0:T(8,128)(2,1)S(1)} %bitcast.71), kind=kOutput, calls=%fused_computation | convolution fusion | flops 17181966336 | bytes 29360128 | tf_op jit(solution)/shard_map/dot_general | solution.py:40
  407.6 322.0 %shard_map.213 = (f32[128,1024]{1,0:T(8,128)}, f32[128,1024]{1,0:T(8,128)}, f32[128,1024]{1,0:T(8,128)}, f32[128,1024]{1,0:T(8,128)}, f32[128,1024]{1,0:T(8,128)...) custom-call(bf16[2,2,2,128,2048]{4,3,2,1,0:T(8,128)(2,1)} %bitcast.5, ...), custom_call_target="tpu_custom_call" | custom-call | tf_op jit(solution)/shard_map/pallas_call | solution.py:1629
  729.7 1.2 constant_dynamic-update-slice_fusion.1
  730.9 1.1 constant_dynamic-update-slice_fusion.3
  732.4 0.6 copy-done.20
  734.0 2.8 fusion.4
  736.8 1.0 collective-permute-start.1
  738.0 1.4 fusion.12
  739.4 1.1 collective-permute-start
  741.1 0.8 copy-done.14
  742.0 1.8 copy.43
  743.8 1.0 copy.42
  745.8 2.3 copy.60
  748.1 1.0 copy.61
  (76 shorter events, 3.6 us)
Async XLA Ops:
  0.6 4.3 copy-start.5
  4.2 5.6 copy-start.1
  4.2 5.6 copy-start.3
  374.1 14.1 %copy-start = (bf16[2,2,2,128,4096]{4,3,2,1,0:T(8,128)(2,1)S(1)}, bf16[2,2,2,128,4096]{4,3,2,1,0:T(8,128)(2,1)}, u32[]{:S(2)}) copy-start(bf16[2,2,2,128,4096]{4,3,2,1,0:T(8,128)(2,1)} %get-tuple-element.49.refs_12_) | copy-start | bytes 25165828
  374.1 14.1 %copy-start.28 = (bf16[2,8,128,4096]{3,2,1,0:T(8,128)(2,1)S(1)}, bf16[2,8,128,4096]{3,2,1,0:T(8,128)(2,1)}, u32[]{:S(2)}) copy-start(bf16[2,8,128,4096]{3,2,1,0:T(8,128)(2,1)} %get-tuple-element.50) | copy-start | bytes 50331652
  729.6 2.3 copy-start.13
  729.6 2.4 copy-start.12
  729.6 2.4 copy-start.22
  729.7 2.4 copy-start.23
  732.3 1.3 copy-start.2
  732.4 1.6 copy-start.4
  733.9 3.8 copy-start.17
  733.9 3.8 copy-start.27
  733.9 3.9 copy-start.16
  733.9 3.9 copy-start.26
  733.9 3.9 copy-start.15
  734.0 3.9 copy-start.25
  736.8 8.0 %collective-permute-start.1 = (f32[128]{0:T(128)S(1)}, f32[128]{0:T(128)S(1)}, u32[]{:S(2)}, u32[]{:S(2)}) collective-permute-start(f32[128]{0:T(128)S(1)} %add.29), channel_id=1, source_target_pairs={{0,4},{4,0},{1,5},{5,1},{2,6},{6,2},{3,7},{7,3},{8,12},{12,8},{9,1... | collective-permute-start | bytes 1544 | tf_op jit(solution)/shard_map/ppermute | solution.py:23
  738.0 2.6 copy-start.11
  738.0 2.6 copy-start.10
  738.0 2.6 copy-start.18
  738.0 2.6 copy-start.19
  739.4 5.9 collective-permute-start
  743.8 4.3 copy-start.6
  (7 other events, 7.5 us)
